TPU v7x, 512 devices: a whole 4x4x16 slice. The times are simulated.
512 devices in a mesh: src: 32 (over z, y_hi), tgt: 16 (over x, y_lo, core).
Axes of the slice: x: 4, y: 4 (y_hi: 2, y_lo: 2; y = y_hi * 2 + y_lo), z: 16, core: 2. Of those that a mesh axis runs over, the one named last changes fastest.
Arguments:
- edge_state: bfloat16 [32, 16, 512, 1024], P('src', 'tgt'), may hold values from -8 to 8
- atom_state: bfloat16 [32, 256, 256], P('src', 'tgt'), may hold values from -6 to 6
- edge_source: int32 [32, 16, 512], P('src', 'tgt'), may hold values from 0 to 255, as said below
- trip_source: int32 [32, 16, 4096], P('src', 'tgt'), may hold values from 0 to 16383
- trip_target: int32 [32, 16, 4096], P('src', 'tgt'), may hold values from 0 to 511
- trip_count: int32 [32, 16], P('src', 'tgt'), may hold values from 1024 to 4096, as said below
- trip_basis: bfloat16 [32, 16, 16, 4096], P('src', 'tgt'), may hold values from -6 to 6
- reverse_perm: int32 [32, 16, 512], P('src', 'tgt'), may hold values from 0 to 511, each once within a row
- down_proj: bfloat16 [1024, 64], replicated, may hold values from -0.1875 to 0.1875
- bilinear: bfloat16 [1024, 64], replicated, may hold values from -0.1875 to 0.1875
- up_forward: bfloat16 [64, 1024], replicated, may hold values from -0.75 to 0.75
- up_reverse: bfloat16 [64, 1024], replicated, may hold values from -0.75 to 0.75
- res_first: bfloat16 [1024, 1024], P('tgt'), may hold values from -0.1875 to 0.1875
- res_second: bfloat16 [1024, 1024], P('tgt'), may hold values from -0.1875 to 0.1875
- atom_proj: bfloat16 [1024, 256], replicated, may hold values from -0.1875 to 0.1875
- atom_self: bfloat16 [256, 256], replicated, may hold values from -0.375 to 0.375
- atom_back: bfloat16 [256, 1024], replicated, may hold values from -0.375 to 0.375
Outputs:
- edge_new: bfloat16 [32, 16, 512, 1024], P('src', 'tgt')
- atom_new: bfloat16 [32, 256, 256], P('src', 'tgt')
Inputs may be any that keep to these rules, and one draw needn't show every extreme that they name: `trip_count`: each tile has 1024 to 4096 live triplet slots, the first ones; some tile has all 4096 live in every draw. `edge_source`: edge slot e of a tile has its source atom in share e mod 16 of the block, that is among atoms of that share times 16 to the next multiple of 16.
All inputs are finite; a program needn't handle non-finite values.
Results may differ from a plain program's by a relative error of at most 0.012.
Values may be sent and summed in bfloat16 or wider, within the bound.
No kernel may reach another device: no remote copies, remote signals or barrier semaphores. Data moves between devices by JAX's collectives and lax.ppermute only.
A program may use at most 64 MiB of HBM per device.

v0:
```python
import math

import jax
import jax.numpy as jnp
from jax import lax
from jax.sharding import PartitionSpec as P

INV_THREE = 1.0 / math.sqrt(3.0)
INV_TWO = 1.0 / math.sqrt(2.0)


def contract_tile(column, source_idx, target_idx, live_count, basis_tile, bilinear, edge_count):
    trip_total = source_idx.shape[0]
    block_size = math.gcd(trip_total, 512)
    block_count = trip_total // block_size
    basis_count = basis_tile.shape[0]
    msg_width = column.shape[1]
    valid_mask = jnp.arange(trip_total, dtype=jnp.int32) < live_count
    edge_ids = jnp.arange(edge_count, dtype=jnp.int32)
    blocks = (
        source_idx.reshape(block_count, block_size),
        target_idx.reshape(block_count, block_size),
        valid_mask.reshape(block_count, block_size),
        basis_tile.reshape(basis_count, block_count, block_size).transpose(1, 0, 2),
    )

    def accumulate(running, pieces):
        src_block, tgt_block, mask_block, basis_block = pieces
        picked = jnp.take(column, src_block, axis=0).astype(jnp.float32)
        outer_prod = (
            (basis_block.T.astype(jnp.float32)[:, :, None] * picked[:, None, :])
            .reshape(block_size, basis_count * msg_width)
            .astype(jnp.bfloat16)
        )
        one_hot = ((tgt_block[None, :] == edge_ids[:, None]) & mask_block[None, :]).astype(
            jnp.bfloat16
        )
        return (running + jnp.dot(one_hot, outer_prod, preferred_element_type=jnp.float32), None)

    start_sum = jnp.zeros((edge_count, basis_count * msg_width), jnp.float32)
    summed, unused = lax.scan(accumulate, start_sum, blocks)
    return jnp.dot(
        summed.astype(jnp.bfloat16), bilinear, preferred_element_type=jnp.float32
    ).astype(jnp.bfloat16)


def local(
    edge_state,
    atom_state,
    edge_source,
    trip_source,
    trip_target,
    trip_count,
    trip_basis,
    reverse_perm,
    down_proj,
    bilinear,
    up_forward,
    up_reverse,
    res_first,
    res_second,
    atom_proj,
    atom_self,
    atom_back,
):
    edge_rows = edge_state[0, 0]
    edge_count = edge_rows.shape[0]
    model_width = edge_rows.shape[1]
    tgt_size = lax.axis_size("tgt")
    src_size = lax.axis_size("src")
    piece_rows = edge_count // (src_size * tgt_size)
    down_msg = jax.nn.silu(
        jnp.dot(edge_rows, down_proj, preferred_element_type=jnp.float32)
    ).astype(jnp.bfloat16)
    column = lax.all_gather(down_msg, "src", axis=0, tiled=True)
    trip_msg = contract_tile(
        column,
        trip_source[0, 0],
        trip_target[0, 0],
        trip_count[0, 0],
        trip_basis[0, 0],
        bilinear,
        edge_count,
    )
    forward_out = jax.nn.silu(
        jnp.dot(trip_msg, up_forward, preferred_element_type=jnp.float32)
    ).astype(jnp.bfloat16)
    partner_ids = reverse_perm[0, 0]
    reverse_out = jax.nn.silu(
        jnp.dot(trip_msg, up_reverse, preferred_element_type=jnp.float32)
    ).astype(jnp.bfloat16)
    grid_rows = reverse_out.reshape(src_size, tgt_size, piece_rows, model_width)
    sectioned = lax.all_to_all(grid_rows, "tgt", split_axis=1, concat_axis=1, tiled=True)
    arranged = lax.all_to_all(sectioned, "src", split_axis=0, concat_axis=0, tiled=True)
    mirrored = jnp.take(arranged.reshape(edge_count, model_width), partner_ids, axis=0)
    mixed_state = (
        (
            edge_rows.astype(jnp.float32)
            + forward_out.astype(jnp.float32)
            + mirrored.astype(jnp.float32)
        )
        * INV_THREE
    ).astype(jnp.bfloat16)
    left_cols = mixed_state
    hidden_pre = jnp.dot(
        left_cols,
        lax.all_gather(res_first, "tgt", axis=0, tiled=True),
        preferred_element_type=jnp.float32,
    )
    inner_act = jax.nn.silu(hidden_pre).astype(jnp.bfloat16)
    left_cols = inner_act
    branch_pre = jnp.dot(
        left_cols,
        lax.all_gather(res_second, "tgt", axis=0, tiled=True),
        preferred_element_type=jnp.float32,
    )
    skipped = ((mixed_state.astype(jnp.float32) + jax.nn.silu(branch_pre)) * INV_TWO).astype(
        jnp.bfloat16
    )
    atom_terms = jax.nn.silu(
        jnp.dot(skipped, atom_proj, preferred_element_type=jnp.float32)
    ).astype(jnp.bfloat16)
    own_atoms = atom_state[0]
    atom_count = own_atoms.shape[0]
    block_atoms = atom_count * tgt_size
    sources = edge_source[0, 0]
    one_hot = (sources[None, :] == jnp.arange(block_atoms, dtype=jnp.int32)[:, None]).astype(
        jnp.bfloat16
    )
    block_terms = jnp.dot(one_hot, atom_terms, preferred_element_type=jnp.float32)
    share_sums = lax.psum_scatter(block_terms, "tgt", scatter_dimension=0, tiled=True)
    atom_new = (
        own_atoms.astype(jnp.float32)
        + jax.nn.silu(
            jnp.dot(share_sums.astype(jnp.bfloat16), atom_self, preferred_element_type=jnp.float32)
        )
    ).astype(jnp.bfloat16)
    atom_block = lax.all_gather(atom_new, "tgt", axis=0, tiled=True)
    source_feats = jnp.take(atom_block, sources, axis=0)
    edge_new = (
        skipped.astype(jnp.float32)
        + jax.nn.silu(jnp.dot(source_feats, atom_back, preferred_element_type=jnp.float32))
    ).astype(jnp.bfloat16)
    return (edge_new[None, None], atom_new[None])


def solution(mesh):
    return jax.shard_map(
        local,
        mesh=mesh,
        in_specs=(
            P("src", "tgt", None, None),
            P("src", "tgt", None),
            P("src", "tgt", None),
            P("src", "tgt", None),
            P("src", "tgt", None),
            P("src", "tgt"),
            P("src", "tgt", None, None),
            P("src", "tgt", None),
            P(),
            P(),
            P(),
            P(),
            P("tgt", None),
            P("tgt", None),
            P(),
            P(),
            P(),
        ),
        out_specs=(P("src", "tgt", None, None), P("src", "tgt", None)),
        check_vma=False,
    )
```

profile of v0, /device:TPU:1, one launch (start us, length us, event | category | flops | bytes accessed | tf_op | source)
XLA Modules:
  0.0 417.4 jit_solution(10758556886884743599)
XLA Ops:
  7.2 0.0 all-gather.4.cloned.1.call-start
  7.2 2.4 multiply_convert_fusion.11
  9.6 0.0 all-gather.4.cloned.1.call-update
  9.6 0.0 all-gather.6.cloned.1.call-start
  9.7 0.7 all-gather.6.cloned.1.call-update
  10.4 0.5 broadcast.127
  10.9 1.4 reduce.9
  12.3 1.4 reduce.8
  13.7 0.9 copy.34
  15.4 138.0 %all-gather.4.cloned.1.call-done = bf16[16384,64]{0,1:T(8,128)(2,1)} async-done(((bf16[512,64]{0,1:T(8,128)(2,1)}), bf16[16384,64]{0,1:T(8,128)(2,1)}) %all-gather.4.cloned.1.call-update) | async-done | bytes 2097168 | tf_op jit(solution)/shard_map/all_gather | solution.py:75
  153.4 4.8 %copy.31 = bf16[16384,64]{1,0:T(8,128)(2,1)} copy(bf16[16384,64]{0,1:T(8,128)(2,1)} %all-gather.4.cloned.1.call-done) | data formatting | bytes 4194304
  158.2 62.4 %while.11 = (s32[]{:T(128)}, f32[512,1024]{1,0:T(8,128)}, s32[8,512]{1,0:T(8,128)S(1)}, pred[8,512]{1,0:T(8,128)(4,1)S(1)}, bf16[8,16,512]{2,1,0:T(8,128)(2,1)S(...) while((s32[]{:T(128)}, f32[512,1024]{1,0:T(8,128)}, ...), condition=%wide.region_1.2_spmd.clone, body=%wide.region_0.1_spmd.clone.sunk | while | flops 539571712 | bytes 6988407 | solution.py:41
  158.2 3.8 gather_fusion
  162.0 0.1 copy.36
  162.2 0.2 multiply_convert_fusion.13
  162.4 2.1 select_add_fusion.2
  164.6 3.8 gather_fusion
  168.4 0.1 copy.36
  168.6 0.2 multiply_convert_fusion.13
  168.8 3.7 select_add_fusion.2
  172.6 3.8 gather_fusion
  176.4 0.1 copy.36
  176.5 0.2 multiply_convert_fusion.13
  176.8 3.7 select_add_fusion.2
  180.6 3.8 gather_fusion
  184.4 0.1 copy.36
  184.6 0.2 multiply_convert_fusion.13
  184.8 3.8 select_add_fusion.2
  188.6 3.8 gather_fusion
  192.5 0.1 copy.36
  192.6 0.2 multiply_convert_fusion.13
  192.9 3.7 select_add_fusion.2
  196.7 3.8 gather_fusion
  200.4 0.1 copy.36
  200.6 0.2 multiply_convert_fusion.13
  200.9 3.7 select_add_fusion.2
  204.6 3.8 gather_fusion
  208.4 0.1 copy.36
  208.6 0.2 multiply_convert_fusion.13
  208.8 3.7 select_add_fusion.2
  212.6 3.8 gather_fusion
  216.4 0.1 copy.36
  216.6 0.2 multiply_convert_fusion.13
  216.8 3.7 select_add_fusion.2
  220.6 2.1 convolution_convert_fusion
  222.6 0.7 multiply_convert_fusion.4
  223.4 0.6 copy.32
  224.0 29.3 %all_to_all.10 = bf16[32,16,1,1024]{3,0,2,1:T(8,128)(2,1)S(1)} all-to-all(bf16[32,16,1,1024]{3,0,2,1:T(8,128)(2,1)S(1)} %copy.32), channel_id=1, replica_groups=mesh['src'=32,'tgt'=16] {'tgt'}, dimensions={1} | all-to-all | bytes 2097152 | tf_op jit(solution)/shard_map/all_to_all | solution.py:93
  253.3 1.5 copy.33
  254.8 8.2 %all-to-all-start.1 = ((bf16[32,16,1,1024]{3,1,2,0:T(8,128)(2,1)}), bf16[32,16,1,1024]{3,1,2,0:T(8,128)(2,1)S(1)}, u32[]{:S(2)}, u32[]{:S(2)}) async-start(bf16[32,16,1,1024]{3,1,2,0:T(8,128)(2,1)} %copy.33), calls=%async_computation.1 | async-start | bytes 2097152 | tf_op jit(solution)/shard_map/all_to_all | solution.py:94
  263.0 0.0 all-gather.8.cloned.1.call-start
  263.1 0.7 all-gather.8.cloned.1.call-update
  263.8 0.0 reduce-scatter.2.cloned.1.call-start
  263.9 51.6 %all-to-all-done.1 = bf16[32,16,1,1024]{3,1,2,0:T(8,128)(2,1)S(1)} async-done(((bf16[32,16,1,1024]{3,1,2,0:T(8,128)(2,1)}), bf16[32,16,1,1024]{3,1,2,0:T(8,128)(2,1)S(1)}, u32[]{:S(2)}, u32[]{:S(2)}) %all-to-all-start.1) | async-done | bytes 1048608 | tf_op jit(solution)/shard_map/all_to_all | solution.py:94
  315.5 2.0 gather_fusion.1
  317.5 3.2 multiply_convert_fusion.3
  320.8 5.7 %multiply_convert_fusion.1 = bf16[512,1024]{1,0:T(8,128)(2,1)S(1)} fusion(bf16[512,1024]{1,0:T(8,128)(2,1)} %multiply_convert_fusion.3, bf16[1024,1024]{1,0:T(8,128)(2,1)} %all-gather.8.cloned.1.call-done, bf16[1024,1024]{1,0:T(8,128)(2,1)} %all-gather.6.cloned.1.call-done), kind=kOutput, calls=%fused_computation.20 | convolution fusion | flops 2154299392 | bytes 6291456 | tf_op jit(solution)/shard_map/dot_general | solution.py:112
  326.5 1.4 fusion.12
  328.0 0.0 reduce-scatter.2.cloned.1.call-update
  328.0 58.9 %reduce-scatter.2.cloned.1.call-done = f32[16,256]{1,0:T(8,128)} async-done(((f32[256,256]{1,0:T(8,128)}), f32[16,256]{1,0:T(8,128)}) %reduce-scatter.2.cloned.1.call-update) | async-done | bytes 16400 | tf_op jit(solution)/shard_map/reduce_scatter | solution.py:131
  386.9 0.9 fusion.19
  387.8 19.3 %all_gather.15 = bf16[256,256]{1,0:T(8,128)(2,1)S(1)} all-gather(bf16[16,256]{1,0:T(8,128)(2,1)S(1)} %fusion.19), channel_id=1, replica_groups=mesh['src'=32,'tgt'=16] {'tgt'}, dimensions={0}, use_global_device_ids=true | all-gather | bytes 139264 | tf_op jit(solution)/shard_map/all_gather | solution.py:138
  407.1 1.9 gather_fusion.2
  409.1 1.8 fusion.6
  (89 shorter events, 0.9 us)
Async XLA Ops:
  7.2 401.9 %copy-start = (bf16[256,1024]{1,0:T(8,128)(2,1)S(1)}, bf16[256,1024]{1,0:T(8,128)(2,1)}, u32[]{:S(2)}) copy-start(bf16[256,1024]{1,0:T(8,128)(2,1)} %param.35) | copy-start | bytes 1572868
  7.2 146.2 %all-gather.4.cloned.1.call-start = ((), (), s32[]{:S(2)}) async-start(), calls=%async_computation.3 | async-start | bytes 2162688 | tf_op jit(solution)/shard_map/all_gather | solution.py:75
  9.6 311.1 %all-gather.6.cloned.1.call-start = ((), (), s32[]{:S(2)}) async-start(), calls=%async_computation.4 | async-start | bytes 2228224 | tf_op jit(solution)/shard_map/all_gather | solution.py:107
  158.2 62.4 %copy-start.1 = (bf16[1024,64]{0,1:T(8,128)(2,1)S(1)}, bf16[1024,64]{0,1:T(8,128)(2,1)}, u32[]{:S(2)}) copy-start(bf16[1024,64]{0,1:T(8,128)(2,1)} %param.28) | copy-start | bytes 393220
  220.6 2.1 copy-start.8
  253.2 10.6 %copy-start.5 = (s32[1,1,512]{2,1,0:T(1,128)S(1)}, s32[1,1,512]{2,1,0:T(1,128)}, u32[]{:S(2)}) copy-start(s32[1,1,512]{2,1,0:T(1,128)} %param.26) | copy-start | bytes 6148
  254.8 60.7 %all-to-all-start.1 = ((bf16[32,16,1,1024]{3,1,2,0:T(8,128)(2,1)}), bf16[32,16,1,1024]{3,1,2,0:T(8,128)(2,1)S(1)}, u32[]{:S(2)}, u32[]{:S(2)}) async-start(bf16[32,16,1,1024]{3,1,2,0:T(8,128)(2,1)} %copy.33), calls=%async_computation.1 | async-start | bytes 2097152 | tf_op jit(solution)/shard_map/all_to_all | solution.py:94
  263.0 57.7 %all-gather.8.cloned.1.call-start = ((), (), s32[]{:S(2)}) async-start(), calls=%async_computation.5 | async-start | bytes 2228224 | tf_op jit(solution)/shard_map/all_gather | solution.py:114
  263.8 123.1 %reduce-scatter.2.cloned.1.call-start = ((), (), s32[]{:S(2)}) async-start(), calls=%async_computation.6 | async-start | bytes 278528 | tf_op jit(solution)/shard_map/reduce_scatter | solution.py:131
  315.5 2.1 copy-start.9
  320.7 5.8 %copy-start.6 = (s32[1,1,512]{2,1,0:T(1,128)S(1)}, s32[1,1,512]{2,1,0:T(1,128)}, u32[]{:S(2)}) copy-start(s32[1,1,512]{2,1,0:T(1,128)} %param.21) | copy-start | bytes 6148
  320.7 5.8 %copy-start.7 = (bf16[1024,256]{1,0:T(8,128)(2,1)S(1)}, bf16[1024,256]{1,0:T(8,128)(2,1)}, u32[]{:S(2)}) copy-start(bf16[1024,256]{1,0:T(8,128)(2,1)} %param.33) | copy-start | bytes 1572868
  326.5 60.4 %copy-start.2 = (bf16[256,256]{1,0:T(8,128)(2,1)S(1)}, bf16[256,256]{1,0:T(8,128)(2,1)}, u32[]{:S(2)}) copy-start(bf16[256,256]{1,0:T(8,128)(2,1)} %param.34) | copy-start | bytes 393220
  326.5 60.4 %copy-start.4 = (bf16[1,16,256]{2,1,0:T(8,128)(2,1)S(1)}, bf16[1,16,256]{2,1,0:T(8,128)(2,1)}, u32[]{:S(2)}) copy-start(bf16[1,16,256]{2,1,0:T(8,128)(2,1)} %param.20) | copy-start | bytes 24580
  387.8 23.0 %copy-start.3 = (bf16[16,256]{1,0:T(8,128)(2,1)}, bf16[16,256]{1,0:T(8,128)(2,1)S(1)}, u32[]{:S(2)}) copy-start(bf16[16,256]{1,0:T(8,128)(2,1)S(1)} %fusion.19) | copy-start | bytes 24580
Sparse Core Ops, SparseCore 0:
  11.5 141.8 all-gather.3
  155.5 45.2 all-gather.5
  266.0 42.9 all-gather.7
  328.1 58.7 reduce-scatter.1
where the time goes:
time: 418 us; the launch traced here: 417 us
  waiting for transfers between devices  250 us (60%)
  blocking collectives  48.6 us (12%)
  matrix products  46.5 us (11%)
  local copies, waits for them, and re-layouts  44 us (11%)
  between operations  14.6 us (3%)
  starting transfers between devices  8.39 us (2%)
  other arithmetic  4.9 us (1%)
    all_gather x1, waiting for transfers between devices, local(): column = lax.all_gather(down_msg, 'src', axis=0, tiled=True)  138 us
    reduce_scatter x1, waiting for transfers between devices, local(): lax.psum_scatter(block_terms, 'tgt', scatter_dimension=0, tiled=True)  58.9 us
    all_to_all x1, waiting for transfers between devices, local(): lax.all_to_all(sectioned, 'src', split_axis=0, concat_axis=0, tiled=True)  51.6 us
    gather x16, local copies, waits for them, and re-layouts, accumulate(): picked = jnp.take(column, src_block, axis=0).astype(jnp.float32)  31.2 us
    all_to_all x1, blocking collectives, local(): lax.all_to_all(grid_rows, 'tgt', split_axis=1, concat_axis=1, tiled=True)  29.3 us
    dot_general x8, matrix products, accumulate(): jnp.dot(one_hot, outer_prod, preferred_element_type=jnp.float32)  28.3 us
    all_gather x1, blocking collectives, local(): atom_block = lax.all_gather(atom_new, 'tgt', axis=0, tiled=True)  19.3 us
  transfers between devices with their start and end apart: 5, of which 3 were waited for; matrix products, arithmetic and copies ran while one was open for 19% of the time, Pallas kernels for 0%

commit v1 on v0

v1 whole, which is shorter than its diff:
```python
import math

import jax
import jax.numpy as jnp
from jax import lax
from jax.experimental import pallas as pl
from jax.experimental.pallas import tpu as pltpu
from jax.sharding import PartitionSpec as P

INV_THREE = 1.0 / math.sqrt(3.0)
INV_TWO = 1.0 / math.sqrt(2.0)
F32 = jnp.float32
BF16 = jnp.bfloat16

Z, YH, NT = 16, 2, 16
NS = Z * YH
FAR = 8
BLOCK = 512


def silu(v):
    return v * (0.5 * jnp.tanh(0.5 * v) + 0.5)


def dot(a, b, ca=1, cb=0):
    return lax.dot_general(a, b, (((ca,), (cb,)), ((), ())), preferred_element_type=F32)


def params(mb=48):
    return pltpu.CompilerParams(vmem_limit_bytes=mb * 1024 * 1024)


VM = pl.BlockSpec(memory_space=pltpu.VMEM)
SM = pl.BlockSpec(memory_space=pltpu.SMEM)
HB = pl.BlockSpec(memory_space=pl.ANY)


def down_kernel(x_ref, w_ref, o_ref):
    y = silu(dot(x_ref[...], w_ref[...], 1, 1)).astype(BF16)
    half = y.shape[0] // 2
    packed = jnp.concatenate([y[:half], y[half:]], axis=1)
    for i in range(o_ref.shape[0]):
        o_ref[i] = packed


def contract_kernel(
    pos_ref, cnt_ref, tgt_ref, basis_ref, bil_ref, b0, b1, b2, b3, tm_ref, send_ref, col, picked, acc
):
    trips = tgt_ref.shape[1]
    edges, width = tm_ref.shape
    lanes = 2 * width
    low = lax.broadcasted_iota(jnp.int32, (256, lanes), 1) < width

    def widen(i, c):
        for n, ref in enumerate((b0, b1, b2, b3)):
            v = ref[i].astype(F32)
            w = pltpu.roll(v, width, 1)
            at = (n * FAR + i) * 512
            col[pl.ds(pl.multiple_of(at, 512), 256), :] = jnp.where(low, v, w)
            col[pl.ds(pl.multiple_of(at + 256, 256), 256), :] = jnp.where(low, w, v)
        return c

    lax.fori_loop(0, FAR, widen, 0)

    unroll = 32

    def fetch(i, c):
        base = pl.multiple_of(i * unroll, unroll)
        for j in range(unroll):
            picked[pl.ds(base + j, 1), :] = col[pl.ds(pos_ref[0, base + j], 1), :]
        return c

    lax.fori_loop(0, trips // unroll, fetch, 0)

    count = cnt_ref[0, 0]
    nb = basis_ref.shape[0]
    full = nb * width
    expand = (
        lax.broadcasted_iota(jnp.int32, (nb, full), 1) // width
        == lax.broadcasted_iota(jnp.int32, (nb, full), 0)
    ).astype(BF16)
    edge_ids = lax.broadcasted_iota(jnp.int32, (edges, BLOCK), 0)
    slot_ids = lax.broadcasted_iota(jnp.int32, (1, BLOCK), 1)
    acc[...] = jnp.zeros_like(acc)

    def block(i, c):
        at = pl.multiple_of(i * BLOCK, BLOCK)
        spread = dot(basis_ref[:, pl.ds(at, BLOCK)], expand, 0, 0).astype(BF16)
        rows = picked[pl.ds(at, BLOCK), :].astype(BF16)
        outer = spread * jnp.concatenate([rows] * (nb // 2), axis=1)
        msg = dot(outer, bil_ref[...], 1, 1)
        hi = msg.astype(BF16)
        lo = (msg - hi.astype(F32)).astype(BF16)
        tgt = jnp.where(slot_ids + at < count, tgt_ref[:, pl.ds(at, BLOCK)], -1)
        hot = jnp.where(edge_ids == tgt, 1.0, 0.0).astype(BF16)
        acc[...] += dot(hot, jnp.concatenate([hi, lo], axis=1))
        return c

    lax.fori_loop(0, trips // BLOCK, block, 0)
    total = acc[...]
    msg = (total[:, :width] + total[:, width:]).astype(BF16)
    tm_ref[...] = msg
    acc[:, :width] = msg.astype(F32)
    for t in range(NT):
        first = acc[pl.ds(t, NT, stride=NT), :]
        second = acc[pl.ds(NT * NT + t, NT, stride=NT), :]
        send_ref[t] = jnp.concatenate([first[:, :width], second[:, :width]], axis=1).astype(BF16)


def turn_kernel(x_ref, o_ref, tmp):
    width = x_ref.shape[2] // 2
    tmp[...] = x_ref[...].reshape(tmp.shape).astype(F32)
    for s in range(NT):
        first = tmp[pl.ds(s, 8, stride=NT), :]
        second = tmp[pl.ds(8 * NT + s, 8, stride=NT), :]
        o_ref[s] = jnp.concatenate([first[:, :width], second[:, :width]], axis=1).astype(BF16)
        o_ref[NT + s] = jnp.concatenate([first[:, width:], second[:, width:]], axis=1).astype(BF16)


def edge_kernel(
    x_ref, tm_ref, got_ref, perm_ref, src_ref, upf_ref, upr_ref, w1_ref, w2_ref, proj_ref,
    skip_ref, part_ref, w1, w2, sems,
):
    load1 = pltpu.make_async_copy(w1_ref, w1, sems.at[0])
    load2 = pltpu.make_async_copy(w2_ref, w2, sems.at[1])
    load1.start()
    load2.start()
    edges = x_ref.shape[0]
    width = tm_ref.shape[1]
    got = got_ref[...]
    got = jnp.concatenate([got[:, :width], got[:, width:]], axis=0)
    perm = perm_ref[...]
    row = ((perm >> 3) & 1) * (edges // 2) + (perm >> 4) * 8 + (perm & 7)
    hot = jnp.where(
        lax.broadcasted_iota(jnp.int32, (edges, edges), 0) == row, 1.0, 0.0
    ).astype(BF16)
    mirror_msg = dot(hot, got, 0, 0).astype(BF16)
    forward_out = silu(dot(tm_ref[...], upf_ref[...])).astype(BF16)
    mirrored = silu(dot(mirror_msg, upr_ref[...])).astype(BF16)
    mixed = (
        (x_ref[...].astype(F32) + forward_out.astype(F32) + mirrored.astype(F32)) * INV_THREE
    ).astype(BF16)
    load1.wait()
    inner = silu(dot(mixed, w1[...])).astype(BF16)
    load2.wait()
    skipped = ((mixed.astype(F32) + silu(dot(inner, w2[...]))) * INV_TWO).astype(BF16)
    skip_ref[...] = skipped
    terms = silu(dot(skipped, proj_ref[...])).astype(BF16)
    atoms = part_ref.shape[0]
    own = jnp.where(
        lax.broadcasted_iota(jnp.int32, (atoms, edges), 0) == src_ref[...], 1.0, 0.0
    ).astype(BF16)
    part_ref[...] = dot(own, terms).astype(BF16)


def atom_kernel(parts_ref, state_ref, w_ref, new_ref, send_ref):
    total = parts_ref[0].astype(F32)
    for i in range(1, NT):
        total = total + parts_ref[i].astype(F32)
    new = (state_ref[...].astype(F32) + silu(dot(total.astype(BF16), w_ref[...]))).astype(BF16)
    new_ref[...] = new
    for i in range(NT):
        send_ref[i] = new


def final_kernel(skip_ref, block_ref, src_ref, back_ref, o_ref):
    atoms = block_ref.shape[0]
    edges = skip_ref.shape[0]
    own = jnp.where(
        lax.broadcasted_iota(jnp.int32, (atoms, edges), 0) == src_ref[...], 1.0, 0.0
    ).astype(BF16)
    feats = dot(own, block_ref[...], 0, 0).astype(BF16)
    o_ref[...] = (skip_ref[...].astype(F32) + silu(dot(feats, back_ref[...]))).astype(BF16)


def shift(d):
    return [(z * YH + h, ((z + d) % Z) * YH + h) for z in range(Z) for h in range(YH)]


def shift_two():
    return [
        (z * YH + h, ((z + (2 if z % 2 == 0 else -2)) % Z) * YH + h)
        for z in range(Z)
        for h in range(YH)
    ]


def struct(shape, dtype=BF16):
    return jax.ShapeDtypeStruct(shape, dtype)


def local(
    edge_state,
    atom_state,
    edge_source,
    trip_source,
    trip_target,
    trip_count,
    trip_basis,
    reverse_perm,
    down_proj,
    bilinear,
    up_forward,
    up_reverse,
    res_first,
    res_second,
    atom_proj,
    atom_self,
    atom_back,
):
    rows = edge_state[0, 0]
    edges, wide = rows.shape
    width = down_proj.shape[1]
    trips = trip_source.shape[2]

    far = pl.pallas_call(
        down_kernel,
        out_shape=struct((FAR, edges // 2, 2 * width)),
        in_specs=[VM] * 2,
        out_specs=VM,
        compiler_params=params(),
    )(rows, down_proj.T)

    groups = [
        [((z0 + 4 * i) % Z) * YH + h for i in range(4) for h in range(YH)] for z0 in range(4)
    ]
    near = lax.all_to_all(
        far, "src", split_axis=0, concat_axis=0, tiled=True, axis_index_groups=groups
    )
    from_next = lax.ppermute(near, "src", shift(-1))
    from_prev = lax.ppermute(near, "src", shift(1))
    from_two = lax.ppermute(near, "src", shift_two())

    first_all = lax.all_gather(res_first, "tgt", axis=0, tiled=True)
    second_all = lax.all_gather(res_second, "tgt", axis=0, tiled=True)

    my_z = lax.axis_index("src") // YH
    ids = trip_source[0]
    q = ids >> 9
    zq = q >> 1
    pos = (((zq - my_z) & 3) * FAR + (zq >> 2) * 2 + (q & 1)) * edges + (ids & (edges - 1))

    tm, send = pl.pallas_call(
        contract_kernel,
        out_shape=(struct((edges, width)), struct((NT, NT, 2 * width))),
        in_specs=[SM, SM] + [VM] * 7,
        out_specs=(VM, VM),
        scratch_shapes=[
            pltpu.VMEM((NS * edges, 2 * width), F32),
            pltpu.VMEM((trips, 2 * width), F32),
            pltpu.VMEM((edges, 2 * width), F32),
        ],
        compiler_params=params(),
    )(
        pos,
        trip_count,
        trip_target[0],
        trip_basis[0, 0],
        bilinear.T,
        near,
        from_next,
        from_two,
        from_prev,
    )

    got = lax.all_to_all(send, "tgt", split_axis=0, concat_axis=0, tiled=True)
    turned = pl.pallas_call(
        turn_kernel,
        out_shape=struct((NS, 8, 2 * width)),
        in_specs=[VM],
        out_specs=VM,
        scratch_shapes=[pltpu.VMEM((NT * NT, 2 * width), F32)],
        compiler_params=params(),
    )(got)
    arrived = lax.all_to_all(turned, "src", split_axis=0, concat_axis=0, tiled=True)

    atoms = atom_state.shape[1] * NT
    da = atom_state.shape[2]
    skipped, part = pl.pallas_call(
        edge_kernel,
        out_shape=(struct((edges, wide)), struct((atoms, da))),
        in_specs=[VM] * 7 + [HB] * 2 + [VM],
        out_specs=(VM, VM),
        scratch_shapes=[
            pltpu.VMEM((wide, wide), BF16),
            pltpu.VMEM((wide, wide), BF16),
            pltpu.SemaphoreType.DMA((2,)),
        ],
        compiler_params=params(),
    )(
        rows,
        tm,
        arrived.reshape(edges // 2, 2 * width),
        reverse_perm[0],
        edge_source[0],
        up_forward,
        up_reverse,
        first_all,
        second_all,
        atom_proj,
    )

    parts = lax.all_to_all(
        part.reshape(NT, atoms // NT, da), "tgt", split_axis=0, concat_axis=0, tiled=True
    )
    atom_new, spread = pl.pallas_call(
        atom_kernel,
        out_shape=(struct((atoms // NT, da)), struct((NT, atoms // NT, da))),
        in_specs=[VM] * 3,
        out_specs=(VM, VM),
        compiler_params=params(),
    )(parts, atom_state[0], atom_self)
    block = lax.all_to_all(spread, "tgt", split_axis=0, concat_axis=0, tiled=True)
    edge_new = pl.pallas_call(
        final_kernel,
        out_shape=struct((edges, wide)),
        in_specs=[VM] * 4,
        out_specs=VM,
        compiler_params=params(),
    )(skipped, block.reshape(atoms, da), edge_source[0], atom_back)
    return (edge_new[None, None], atom_new[None])


def solution(mesh):
    return jax.shard_map(
        local,
        mesh=mesh,
        in_specs=(
            P("src", "tgt", None, None),
            P("src", "tgt", None),
            P("src", "tgt", None),
            P("src", "tgt", None),
            P("src", "tgt", None),
            P("src", "tgt"),
            P("src", "tgt", None, None),
            P("src", "tgt", None),
            P(),
            P(),
            P(),
            P(),
            P("tgt", None),
            P("tgt", None),
            P(),
            P(),
            P(),
        ),
        out_specs=(P("src", "tgt", None, None), P("src", "tgt", None)),
        check_vma=False,
    )
```

time: 418 us -> 179 us (0.43)
  waiting for transfers between devices: 250 us -> 54 us
  matrix products: 46.5 us -> 0 us
  local copies, waits for them, and re-layouts: 44 us -> 3.76 us
  Pallas kernels: 0 us -> 25.4 us
  starting transfers between devices: 8.39 us -> 29.3 us
  other arithmetic: 4.9 us -> 0.06 us
    all_gather x3 -> x2, waiting for transfers between devices: 138 us -> 0.01 us  [the longest x1 0.01 us: local(): first_all = lax.all_gather(res_first, 'tgt', axis=0, tiled=True)]
    reduce_scatter x1 -> x0, waiting for transfers between devices: 58.9 us -> none  [local(): lax.psum_scatter(block_terms, 'tgt', scatter_dimension=0, tiled=True)]
    dot_general x16 -> x0, matrix products: 46.5 us -> none  [the longest x8 28.3 us: accumulate(): jnp.dot(one_hot, outer_prod, preferred_element_type=jnp.float32)]
    gather x18 -> x0, local copies, waits for them, and re-layouts: 35.2 us -> none  [the longest x16 31.2 us: accumulate(): picked = jnp.take(column, src_block, axis=0).astype(jnp.float32)]
    pallas_call x0 -> x6, Pallas kernels: none -> 25.4 us  [the longest x1 16.1 us: local(): pl.pallas_call(contract_kernel, out_shape=(struct((edges, width)), struct...]
    ppermute x0 -> x3, waiting for transfers between devices: none -> 24 us  [the longest x1 15.7 us: local(): from_next = lax.ppermute(near, 'src', shift(-1))]
    all_to_all x1, waiting for transfers between devices: 51.6 us -> 28.6 us  [local(): lax.all_to_all(far, 'src', split_axis=0, concat_axis=0, tiled=True, axis_...]
    all_to_all x1 -> x4, blocking collectives: 29.3 us -> 50.9 us  [the longest x1 20.4 us: local(): lax.all_to_all(turned, 'src', split_axis=0, concat_axis=0, tiled=True)]
  transfers between devices with their start and end apart: 5 -> 6, of which waited for: 3 -> 3; matrix products, arithmetic and copies ran while one was open for 19% -> 0% of each run, Pallas kernels for 0% -> 10%
where the time goes in v1:
time: 179 us; the launch traced here: 178 us
  waiting for transfers between devices  54 us (30%)
  blocking collectives  50.9 us (28%)
  starting transfers between devices  29.3 us (16%)
  Pallas kernels  25.4 us (14%)
  between operations  14.9 us (8%)
  local copies, waits for them, and re-layouts  3.76 us (2%)
    all_to_all x1, waiting for transfers between devices, local(): lax.all_to_all(far, 'src', split_axis=0, concat_axis=0, tiled=True, axis_...  28.6 us
    all_to_all x1, blocking collectives, local(): lax.all_to_all(turned, 'src', split_axis=0, concat_axis=0, tiled=True)  20.4 us
    all_to_all x1, starting transfers between devices, local(): lax.all_to_all(far, 'src', split_axis=0, concat_axis=0, tiled=True, axis_...  18.4 us
    pallas_call x1, Pallas kernels, local(): pl.pallas_call(contract_kernel, out_shape=(struct((edges, width)), struct...  16.1 us
    ppermute x1, waiting for transfers between devices, local(): from_next = lax.ppermute(near, 'src', shift(-1))  15.7 us
    all_to_all x1, blocking collectives, local(): got = lax.all_to_all(send, 'tgt', split_axis=0, concat_axis=0, tiled=True)  10.8 us
    all_to_all x1, blocking collectives, local(): lax.all_to_all(part.reshape(NT, atoms // NT, da), 'tgt', split_axis=0, co...  10.7 us
    all_to_all x1, blocking collectives, local(): lax.all_to_all(spread, 'tgt', split_axis=0, concat_axis=0, tiled=True)  9.06 us
  transfers between devices with their start and end apart: 6, of which 3 were waited for; matrix products, arithmetic and copies ran while one was open for 0% of the time, Pallas kernels for 10%

profile of v1, /device:TPU:1, one launch (start us, length us, event | category | flops | bytes accessed | tf_op | source)
XLA Modules:
  0.0 178.3 jit_solution(11611347536624206550)
XLA Ops:
  7.2 0.0 copy-start.9
  7.2 0.0 copy-start.10
  7.2 0.0 all-gather.3.cloned.1.call-start
  7.2 0.7 all-gather.3.cloned.1.call-update
  7.9 0.0 all-gather.5.cloned.1.call-start
  8.0 0.7 all-gather.5.cloned.1.call-update
  8.7 0.0 copy-start
  8.7 1.2 copy-done
  9.9 0.0 copy-start.8
  9.9 0.9 copy-done.8
  10.8 0.0 copy-start.15
  10.8 0.0 copy-start.11
  10.8 1.3 shard_map.176
  12.1 0.0 copy-start.1
  12.1 0.0 copy-start.4
  12.1 0.0 copy-start.5
  12.1 0.0 copy-start.6
  12.1 0.0 copy-start.12
  12.1 0.0 copy-start.14
  12.1 18.4 %all-to-all-start = ((bf16[8,256,128]{2,1,0:T(8,128)(2,1)}), bf16[8,256,128]{2,1,0:T(8,128)(2,1)S(1)}, u32[]{:S(2)}, u32[]{:S(2)}) async-start(bf16[8,256,128]{2,1,0:T(8,128)(2,1)} %shard_map.176), calls=%async_computation | async-start | bytes 1048576 | tf_op jit(solution)/shard_map/all_to_all | solution.py:227
  31.2 28.6 %all-to-all-done.b0 = bf16[8,256,128]{2,1,0:T(8,128)(2,1)S(1)} async-done(((bf16[8,256,128]{2,1,0:T(8,128)(2,1)}), bf16[8,256,128]{2,1,0:T(8,128)(2,1)S(1)}, u32[]{:S(2)}, u32[]{:S(2)}) %all-to-all-start) | async-done | bytes 524320 | tf_op jit(solution)/shard_map/all_to_all | solution.py:227
  59.8 5.8 %collective-permute-start = (bf16[8,256,128]{2,1,0:T(8,128)(2,1)S(1)}, bf16[8,256,128]{2,1,0:T(8,128)(2,1)S(1)}, u32[]{:S(2)}, u32[]{:S(2)}) collective-permute-start(bf16[8,256,128]{2,1,0:T(8,128)(2,1)S(1)} %all-to-all-done.b0), channel_id=1, source_target_pairs={{0,480},{16,496},{32,0},{48,16},{64,32},{80,48},{96,64},{112,80},{... | collective-permute-start | bytes 1572872 | tf_op jit(solution)/shard_map/ppermute | solution.py:230
  65.7 1.9 %collective-permute-start.1 = (bf16[8,256,128]{2,1,0:T(8,128)(2,1)S(1)}, bf16[8,256,128]{2,1,0:T(8,128)(2,1)S(1)}, u32[]{:S(2)}, u32[]{:S(2)}) collective-permute-start(bf16[8,256,128]{2,1,0:T(8,128)(2,1)S(1)} %all-to-all-done.b0), channel_id=1, source_target_pairs={{0,64},{16,80},{32,480},{48,496},{64,128},{80,144},{96,32},{112,48... | collective-permute-start | bytes 1572872 | tf_op jit(solution)/shard_map/ppermute | solution.py:232
  67.6 3.1 %collective-permute-start.2 = (bf16[8,256,128]{2,1,0:T(8,128)(2,1)S(1)}, bf16[8,256,128]{2,1,0:T(8,128)(2,1)S(1)}, u32[]{:S(2)}, u32[]{:S(2)}) collective-permute-start(bf16[8,256,128]{2,1,0:T(8,128)(2,1)S(1)} %all-to-all-done.b0), channel_id=1, source_target_pairs={{0,32},{16,48},{32,64},{48,80},{64,96},{80,112},{96,128},{112,144}... | collective-permute-start | bytes 1572872 | tf_op jit(solution)/shard_map/ppermute | solution.py:231
  70.7 0.0 copy-done.15
  70.7 0.1 add_bitcast_fusion.pos_ref
  70.8 15.7 %collective-permute-done.b1 = bf16[8,256,128]{2,1,0:T(8,128)(2,1)S(1)} collective-permute-done((bf16[8,256,128]{2,1,0:T(8,128)(2,1)S(1)}, bf16[8,256,128]{2,1,0:T(8,128)(2,1)S(1)}, u32[]{:S(2)}, u32[]{:S(2)}) %collective-permute-start) | collective-permute-done | bytes 524320 | tf_op jit(solution)/shard_map/ppermute | solution.py:230
  86.5 0.0 collective-permute-done.1.b2
  86.5 8.2 %collective-permute-done.2.b3 = bf16[8,256,128]{2,1,0:T(8,128)(2,1)S(1)} collective-permute-done((bf16[8,256,128]{2,1,0:T(8,128)(2,1)S(1)}, bf16[8,256,128]{2,1,0:T(8,128)(2,1)S(1)}, u32[]{:S(2)}, u32[]{:S(2)}) %collective-permute-start.2) | collective-permute-done | bytes 524320 | tf_op jit(solution)/shard_map/ppermute | solution.py:231
  94.7 0.0 copy-done.9
  94.8 0.0 copy-done.10
  94.8 0.0 copy-done.11
  94.8 16.1 %shard_map.177 = (bf16[512,64]{1,0:T(8,128)(2,1)S(1)}, bf16[16,16,128]{2,1,0:T(8,128)(2,1)S(1)}) custom-call(s32[1,4096]{1,0:T(1,128)S(1)} %add_bitcast_fusion.pos_ref, s32[1,1]{1,0:T(1,128)S(6)} %copy.19.cnt_ref, s32[1,4096]{1,0:T(1,128)S(1)} %bitcast.23, bf16[16,4096]{1,0:T(8,128)(2,1)S(1)} %bitcast.21, bf16[64,1024]{1,0:T(8,128)(2,1)S(1)} %bitcast.22, ...), custom_call_target="tpu_custom_call" | custom-call | tf_op jit(solution)/shard_map/pallas_call | solution.py:243
  110.8 10.8 %all_to_all.25.x_ref = bf16[16,16,128]{2,1,0:T(8,128)(2,1)S(1)} all-to-all(bf16[16,16,128]{2,1,0:T(8,128)(2,1)S(1)} %get-tuple-element.9), channel_id=1, replica_groups=mesh['src'=32,'tgt'=16] {'tgt'}, dimensions={0} | all-to-all | bytes 131072 | tf_op jit(solution)/shard_map/all_to_all | solution.py:266
  121.6 0.1 shard_map.178
  121.7 20.4 %all_to_all.26 = bf16[32,8,128]{2,1,0:T(8,128)(2,1)S(1)} all-to-all(bf16[32,8,128]{2,1,0:T(8,128)(2,1)S(1)} %shard_map.178), channel_id=1, replica_groups=mesh['src'=32,'tgt'=16] {'src'}, dimensions={0} | all-to-all | bytes 131072 | tf_op jit(solution)/shard_map/all_to_all | solution.py:275
  142.1 0.0 all-gather.3.cloned.1.call-done.w1_ref
  142.1 0.0 all-gather.5.cloned.1.call-done.w2_ref
  142.1 0.0 copy-done.1
  142.1 0.0 copy-done.4
  142.1 0.0 copy-done.5
  142.1 0.0 copy-done.6
  142.1 0.0 copy-done.12
  142.1 0.0 copy-done.14
  142.1 0.0 copy-start.2
  142.1 1.6 copy-done.2
  143.7 0.0 copy-start.7
  143.7 0.0 copy-start.13
  143.7 0.0 copy-start.3
  143.7 5.3 %shard_map.179 = (bf16[512,1024]{1,0:T(8,128)(2,1)S(1)}, bf16[256,256]{1,0:T(8,128)(2,1)S(1)}) custom-call(bf16[512,1024]{1,0:T(8,128)(2,1)S(1)} %bitcast.16, bf16[512,64]{1,0:T(8,128)(2,1)S(1)} %get-tuple-element.8.tm_ref, bf16[256,128]{1,0:T(8,128)(2,1)S(1)} %bitcast.18, s32[1,512]{1,0:T(1,128)S(1)} %bitcast.27, s32[1,512]{1,0:T(1,128)S(1)} %bitcast.24, ...), custom_call_target="tpu_custom_call" | custom-call | tf_op jit(solution)/shard_map/pallas_call | solution.py:279
  149.0 10.7 %all_to_all.27.parts_ref = bf16[16,16,256]{2,1,0:T(8,128)(2,1)S(1)} all-to-all(bf16[16,16,256]{2,1,0:T(8,128)(2,1)S(1)} %bitcast.19), channel_id=1, replica_groups=mesh['src'=32,'tgt'=16] {'tgt'}, dimensions={0} | all-to-all | bytes 262144 | tf_op jit(solution)/shard_map/all_to_all | solution.py:303
  159.7 0.0 copy-done.7
  159.7 0.0 copy-done.13
  159.7 0.8 shard_map.180
  160.5 9.1 %all_to_all.28 = bf16[16,16,256]{2,1,0:T(8,128)(2,1)S(1)} all-to-all(bf16[16,16,256]{2,1,0:T(8,128)(2,1)S(1)} %get-tuple-element.12), channel_id=1, replica_groups=mesh['src'=32,'tgt'=16] {'tgt'}, dimensions={0} | all-to-all | bytes 262144 | tf_op jit(solution)/shard_map/all_to_all | solution.py:313
  169.5 0.0 copy-done.3
  169.5 1.9 %shard_map.181 = bf16[512,1024]{1,0:T(8,128)(2,1)} custom-call(bf16[512,1024]{1,0:T(8,128)(2,1)S(1)} %get-tuple-element.10.skip_ref, bf16[256,256]{1,0:T(8,128)(2,1)S(1)} %bitcast.17, s32[1,512]{1,0:T(1,128)S(1)} %bitcast.25, bf16[256,1024]{1,0:T(8,128)(2,1)S(1)} %copy-done.3), custom_call_target="tpu_custom_call" | custom-call | tf_op jit(solution)/shard_map/pallas_call | solution.py:314
Async XLA Ops:
  7.2 87.6 %copy-start.9 = (bf16[1,1,16,4096]{3,2,1,0:T(8,128)(2,1)S(1)}, bf16[1,1,16,4096]{3,2,1,0:T(8,128)(2,1)}, u32[]{:S(2)}) copy-start(bf16[1,1,16,4096]{3,2,1,0:T(8,128)(2,1)} %param.23) | copy-start | bytes 393220
  7.2 87.6 %copy-start.10 = (bf16[1024,64]{0,1:T(8,128)(2,1)S(1)}, bf16[1024,64]{0,1:T(8,128)(2,1)}, u32[]{:S(2)}) copy-start(bf16[1024,64]{0,1:T(8,128)(2,1)} %param.26) | copy-start | bytes 393220
  7.2 134.9 %all-gather.3.cloned.1.call-start = ((), (), s32[]{:S(2)}) async-start(), calls=%async_computation.5 | async-start | bytes 2228224 | tf_op jit(solution)/shard_map/all_gather | solution.py:234
  7.9 134.2 %all-gather.5.cloned.1.call-start = ((), (), s32[]{:S(2)}) async-start(), calls=%async_computation.6 | async-start | bytes 2228224 | tf_op jit(solution)/shard_map/all_gather | solution.py:235
  8.7 1.2 copy-start
  9.9 0.9 copy-start.8
  10.8 59.9 %copy-start.15 = (s32[1,1,4096]{2,1,0:T(1,128)S(1)}, s32[1,1,4096]{2,1,0:T(1,128)}, u32[]{:S(2)}) copy-start(s32[1,1,4096]{2,1,0:T(1,128)} %param.20) | copy-start | bytes 49156
  10.8 84.0 %copy-start.11 = (s32[1,1,4096]{2,1,0:T(1,128)S(1)}, s32[1,1,4096]{2,1,0:T(1,128)}, u32[]{:S(2)}) copy-start(s32[1,1,4096]{2,1,0:T(1,128)} %param.21) | copy-start | bytes 49156
  12.1 130.0 %copy-start.1 = (bf16[1,1,512,1024]{3,2,1,0:T(8,128)(2,1)S(1)}, bf16[1,1,512,1024]{3,2,1,0:T(8,128)(2,1)}, u32[]{:S(2)}) copy-start(bf16[1,1,512,1024]{3,2,1,0:T(8,128)(2,1)} %param.17) | copy-start | bytes 3145732
  12.1 130.0 %copy-start.4 = (bf16[1024,256]{1,0:T(8,128)(2,1)S(1)}, bf16[1024,256]{1,0:T(8,128)(2,1)}, u32[]{:S(2)}) copy-start(bf16[1024,256]{1,0:T(8,128)(2,1)} %proj_ref.1) | copy-start | bytes 1572868
  12.1 130.0 %copy-start.5 = (bf16[64,1024]{1,0:T(8,128)(2,1)S(1)}, bf16[64,1024]{1,0:T(8,128)(2,1)}, u32[]{:S(2)}) copy-start(bf16[64,1024]{1,0:T(8,128)(2,1)} %upf_ref.1) | copy-start | bytes 393220
  12.1 130.0 %copy-start.6 = (bf16[64,1024]{1,0:T(8,128)(2,1)S(1)}, bf16[64,1024]{1,0:T(8,128)(2,1)}, u32[]{:S(2)}) copy-start(bf16[64,1024]{1,0:T(8,128)(2,1)} %upr_ref.1) | copy-start | bytes 393220
  12.1 130.0 %copy-start.12 = (s32[1,1,512]{2,1,0:T(1,128)S(1)}, s32[1,1,512]{2,1,0:T(1,128)}, u32[]{:S(2)}) copy-start(s32[1,1,512]{2,1,0:T(1,128)} %param.19) | copy-start | bytes 6148
  12.1 130.0 %copy-start.14 = (s32[1,1,512]{2,1,0:T(1,128)S(1)}, s32[1,1,512]{2,1,0:T(1,128)}, u32[]{:S(2)}) copy-start(s32[1,1,512]{2,1,0:T(1,128)} %param.24) | copy-start | bytes 6148
  12.1 47.7 %all-to-all-start = ((bf16[8,256,128]{2,1,0:T(8,128)(2,1)}), bf16[8,256,128]{2,1,0:T(8,128)(2,1)S(1)}, u32[]{:S(2)}, u32[]{:S(2)}) async-start(bf16[8,256,128]{2,1,0:T(8,128)(2,1)} %shard_map.176), calls=%async_computation | async-start | bytes 1048576 | tf_op jit(solution)/shard_map/all_to_all | solution.py:227
  59.8 26.7 %collective-permute-start = (bf16[8,256,128]{2,1,0:T(8,128)(2,1)S(1)}, bf16[8,256,128]{2,1,0:T(8,128)(2,1)S(1)}, u32[]{:S(2)}, u32[]{:S(2)}) collective-permute-start(bf16[8,256,128]{2,1,0:T(8,128)(2,1)S(1)} %all-to-all-done.b0), channel_id=1, source_target_pairs={{0,480},{16,496},{32,0},{48,16},{64,32},{80,48},{96,64},{112,80},{... | collective-permute-start | bytes 1572872 | tf_op jit(solution)/shard_map/ppermute | solution.py:230
  65.7 20.8 %collective-permute-start.1 = (bf16[8,256,128]{2,1,0:T(8,128)(2,1)S(1)}, bf16[8,256,128]{2,1,0:T(8,128)(2,1)S(1)}, u32[]{:S(2)}, u32[]{:S(2)}) collective-permute-start(bf16[8,256,128]{2,1,0:T(8,128)(2,1)S(1)} %all-to-all-done.b0), channel_id=1, source_target_pairs={{0,64},{16,80},{32,480},{48,496},{64,128},{80,144},{96,32},{112,48... | collective-permute-start | bytes 1572872 | tf_op jit(solution)/shard_map/ppermute | solution.py:232
  67.6 27.2 %collective-permute-start.2 = (bf16[8,256,128]{2,1,0:T(8,128)(2,1)S(1)}, bf16[8,256,128]{2,1,0:T(8,128)(2,1)S(1)}, u32[]{:S(2)}, u32[]{:S(2)}) collective-permute-start(bf16[8,256,128]{2,1,0:T(8,128)(2,1)S(1)} %all-to-all-done.b0), channel_id=1, source_target_pairs={{0,32},{16,48},{32,64},{48,80},{64,96},{80,112},{96,128},{112,144}... | collective-permute-start | bytes 1572872 | tf_op jit(solution)/shard_map/ppermute | solution.py:231
  142.1 1.6 copy-start.2
  143.7 16.0 %copy-start.7 = (bf16[256,256]{1,0:T(8,128)(2,1)S(1)}, bf16[256,256]{1,0:T(8,128)(2,1)}, u32[]{:S(2)}) copy-start(bf16[256,256]{1,0:T(8,128)(2,1)} %w_ref.1) | copy-start | bytes 393220
  143.7 16.0 %copy-start.13 = (bf16[1,16,256]{2,1,0:T(8,128)(2,1)S(1)}, bf16[1,16,256]{2,1,0:T(8,128)(2,1)}, u32[]{:S(2)}) copy-start(bf16[1,16,256]{2,1,0:T(8,128)(2,1)} %param.18) | copy-start | bytes 24580
  143.7 25.8 %copy-start.3 = (bf16[256,1024]{1,0:T(8,128)(2,1)S(1)}, bf16[256,1024]{1,0:T(8,128)(2,1)}, u32[]{:S(2)}) copy-start(bf16[256,1024]{1,0:T(8,128)(2,1)} %back_ref.1) | copy-start | bytes 1572868
Sparse Core Ops, SparseCore 0:
  10.2 49.1 all-gather.2
  61.5 41.0 all-gather.4

commit v2 on v1

--- a/solution.py
+++ b/solution.py
@@ -15,7 +15,9 @@
 Z, YH, NT = 16, 2, 16
 NS = Z * YH
 FAR = 8
-BLOCK = 512
+XS = 4
+PEER = (0, 2, 1, 3)
+BLOCK = 1024
 
 
 def silu(v):
@@ -35,7 +37,9 @@
 HB = pl.BlockSpec(memory_space=pl.ANY)
 
 
-def down_kernel(x_ref, w_ref, o_ref):
+def down_kernel(x_ref, w_ref, a_ref, b_ref, o_ref, ab_ref):
+    ab_ref[0] = a_ref[...]
+    ab_ref[1] = b_ref[...]
     y = silu(dot(x_ref[...], w_ref[...], 1, 1)).astype(BF16)
     half = y.shape[0] // 2
     packed = jnp.concatenate([y[:half], y[half:]], axis=1)
@@ -44,61 +48,56 @@
 
 
 def contract_kernel(
-    pos_ref, cnt_ref, tgt_ref, basis_ref, bil_ref, b0, b1, b2, b3, tm_ref, send_ref, col, picked, acc
+    pos_ref, cnt_ref, ids_ref, tgt_ref, basis_ref, bil_ref, b0, b1, b2, b3,
+    tm_ref, send_ref, col, rows_a, rows_b, acc, total,
 ):
     trips = tgt_ref.shape[1]
     edges, width = tm_ref.shape
     lanes = 2 * width
-    low = lax.broadcasted_iota(jnp.int32, (256, lanes), 1) < width
+    step = rows_a.shape[0]
 
     def widen(i, c):
         for n, ref in enumerate((b0, b1, b2, b3)):
-            v = ref[i].astype(F32)
-            w = pltpu.roll(v, width, 1)
-            at = (n * FAR + i) * 512
-            col[pl.ds(pl.multiple_of(at, 512), 256), :] = jnp.where(low, v, w)
-            col[pl.ds(pl.multiple_of(at + 256, 256), 256), :] = jnp.where(low, w, v)
+            at = pl.multiple_of((n * FAR + i) * 256, 256)
+            col[pl.ds(at, 256), :] = ref[i].astype(F32)
         return c
 
     lax.fori_loop(0, FAR, widen, 0)
-
-    unroll = 32
-
-    def fetch(i, c):
-        base = pl.multiple_of(i * unroll, unroll)
-        for j in range(unroll):
-            picked[pl.ds(base + j, 1), :] = col[pl.ds(pos_ref[0, base + j], 1), :]
-        return c
-
-    lax.fori_loop(0, trips // unroll, fetch, 0)
 
     count = cnt_ref[0, 0]
     nb = basis_ref.shape[0]
-    full = nb * width
-    expand = (
-        lax.broadcasted_iota(jnp.int32, (nb, full), 1) // width
-        == lax.broadcasted_iota(jnp.int32, (nb, full), 0)
-    ).astype(BF16)
-    edge_ids = lax.broadcasted_iota(jnp.int32, (edges, BLOCK), 0)
-    slot_ids = lax.broadcasted_iota(jnp.int32, (1, BLOCK), 1)
-    acc[...] = jnp.zeros_like(acc)
-
-    def block(i, c):
-        at = pl.multiple_of(i * BLOCK, BLOCK)
-        spread = dot(basis_ref[:, pl.ds(at, BLOCK)], expand, 0, 0).astype(BF16)
-        rows = picked[pl.ds(at, BLOCK), :].astype(BF16)
-        outer = spread * jnp.concatenate([rows] * (nb // 2), axis=1)
-        msg = dot(outer, bil_ref[...], 1, 1)
-        hi = msg.astype(BF16)
-        lo = (msg - hi.astype(F32)).astype(BF16)
-        tgt = jnp.where(slot_ids + at < count, tgt_ref[:, pl.ds(at, BLOCK)], -1)
+    eye = (
+        lax.broadcasted_iota(jnp.int32, (lanes, lanes), 0)
+        == lax.broadcasted_iota(jnp.int32, (lanes, lanes), 1)
+    ).astype(BF16)
+    edge_ids = lax.broadcasted_iota(jnp.int32, (edges, step), 0)
+    slot_ids = lax.broadcasted_iota(jnp.int32, (1, step), 1)
+    total[...] = jnp.zeros_like(total)
+
+    def fetch(dst, at):
+        for j in range(step):
+            dst[j : j + 1, :] = col[pl.ds(pos_ref[0, at + j], 1), :]
+
+    def block(at, rows):
+        both = dot(eye, rows[...].astype(BF16), 1, 1)
+        upper = ((ids_ref[:, at : at + step] >> 8) & 1) == 1
+        msg = jnp.where(upper, both[width:], both[:width]).astype(BF16)
+        basis = basis_ref[:, at : at + step]
+        outer = jnp.concatenate([basis[c : c + 1, :] * msg for c in range(nb)], axis=0)
+        out = dot(bil_ref[...], outer)
+        hi = out.astype(BF16)
+        lo = (out - hi.astype(F32)).astype(BF16)
+        tgt = jnp.where(slot_ids + at < count, tgt_ref[:, at : at + step], -1)
         hot = jnp.where(edge_ids == tgt, 1.0, 0.0).astype(BF16)
-        acc[...] += dot(hot, jnp.concatenate([hi, lo], axis=1))
-        return c
-
-    lax.fori_loop(0, trips // BLOCK, block, 0)
-    total = acc[...]
-    msg = (total[:, :width] + total[:, width:]).astype(BF16)
+        total[...] += dot(jnp.concatenate([hi, lo], axis=0), hot, 1, 1)
+
+    held = (rows_a, rows_b)
+    fetch(held[0], 0)
+    for i in range(trips // step):
+        if (i + 1) * step < trips:
+            fetch(held[(i + 1) % 2], (i + 1) * step)
+        block(i * step, held[i % 2])
+    msg = jnp.transpose(total[:width, :] + total[width:, :]).astype(BF16)
     tm_ref[...] = msg
     acc[:, :width] = msg.astype(F32)
     for t in range(NT):
@@ -118,13 +117,23 @@
 
 
 def edge_kernel(
-    x_ref, tm_ref, got_ref, perm_ref, src_ref, upf_ref, upr_ref, w1_ref, w2_ref, proj_ref,
-    skip_ref, part_ref, w1, w2, sems,
+    me_ref, x_ref, tm_ref, got_ref, perm_ref, src_ref, upf_ref, upr_ref, proj_ref,
+    wa_ref, wb_ref, wc_ref, wd_ref, skip_ref, part_ref, w1, w2, sems,
 ):
-    load1 = pltpu.make_async_copy(w1_ref, w1, sems.at[0])
-    load2 = pltpu.make_async_copy(w2_ref, w2, sems.at[1])
-    load1.start()
-    load2.start()
+    me = me_ref[0, 0]
+    loads = ([], [])
+    for k, w in enumerate((w1, w2)):
+        for i, ref in enumerate((wa_ref, wb_ref, wc_ref, wd_ref)):
+            for j in range(XS):
+                at = (((((me >> 2) + j) & 3) * 4 + ((me & 3) ^ PEER[i]))) * ref.shape[2]
+                at = pl.multiple_of(at, 64)
+                loads[k].append(
+                    pltpu.make_async_copy(
+                        ref.at[j, k], w.at[pl.ds(at, ref.shape[2]), :], sems.at[k, i * XS + j]
+                    )
+                )
+    for load in loads[0] + loads[1]:
+        load.start()
     edges = x_ref.shape[0]
     width = tm_ref.shape[1]
     got = got_ref[...]
@@ -140,9 +149,11 @@
     mixed = (
         (x_ref[...].astype(F32) + forward_out.astype(F32) + mirrored.astype(F32)) * INV_THREE
     ).astype(BF16)
-    load1.wait()
+    for load in loads[0]:
+        load.wait()
     inner = silu(dot(mixed, w1[...])).astype(BF16)
-    load2.wait()
+    for load in loads[1]:
+        load.wait()
     skipped = ((mixed.astype(F32) + silu(dot(inner, w2[...]))) * INV_TWO).astype(BF16)
     skip_ref[...] = skipped
     terms = silu(dot(skipped, proj_ref[...])).astype(BF16)
@@ -183,6 +194,14 @@
         for z in range(Z)
         for h in range(YH)
     ]
+
+
+def along_x(d):
+    return [(t, ((t // 4 + d) % XS) * 4 + t % 4) for t in range(NT)]
+
+
+def across(bit):
+    return [(t, t ^ bit) for t in range(NT)]
 
 
 def struct(shape, dtype=BF16):
@@ -213,13 +232,13 @@
     width = down_proj.shape[1]
     trips = trip_source.shape[2]
 
-    far = pl.pallas_call(
+    far, own_w = pl.pallas_call(
         down_kernel,
-        out_shape=struct((FAR, edges // 2, 2 * width)),
-        in_specs=[VM] * 2,
-        out_specs=VM,
-        compiler_params=params(),
-    )(rows, down_proj.T)
+        out_shape=(struct((FAR, edges // 2, 2 * width)), struct((2,) + res_first.shape)),
+        in_specs=[VM] * 4,
+        out_specs=(VM, VM),
+        compiler_params=params(),
+    )(rows, down_proj.T, res_first, res_second)
 
     groups = [
         [((z0 + 4 * i) % Z) * YH + h for i in range(4) for h in range(YH)] for z0 in range(4)
@@ -227,33 +246,38 @@
     near = lax.all_to_all(
         far, "src", split_axis=0, concat_axis=0, tiled=True, axis_index_groups=groups
     )
+    x_w = [own_w] + [lax.ppermute(own_w, "tgt", along_x(d)) for d in (-1, 2, 1)]
     from_next = lax.ppermute(near, "src", shift(-1))
     from_prev = lax.ppermute(near, "src", shift(1))
     from_two = lax.ppermute(near, "src", shift_two())
 
-    first_all = lax.all_gather(res_first, "tgt", axis=0, tiled=True)
-    second_all = lax.all_gather(res_second, "tgt", axis=0, tiled=True)
+    x_w = jnp.stack(x_w)
+    y_w = lax.ppermute(x_w, "tgt", across(2))
+    cx_w = lax.ppermute(x_w, "tgt", across(1))
 
     my_z = lax.axis_index("src") // YH
     ids = trip_source[0]
     q = ids >> 9
     zq = q >> 1
-    pos = (((zq - my_z) & 3) * FAR + (zq >> 2) * 2 + (q & 1)) * edges + (ids & (edges - 1))
+    pos = (((zq - my_z) & 3) * FAR + (zq >> 2) * 2 + (q & 1)) * (edges // 2) + (ids & 255)
 
     tm, send = pl.pallas_call(
         contract_kernel,
         out_shape=(struct((edges, width)), struct((NT, NT, 2 * width))),
-        in_specs=[SM, SM] + [VM] * 7,
+        in_specs=[SM, SM] + [VM] * 8,
         out_specs=(VM, VM),
         scratch_shapes=[
-            pltpu.VMEM((NS * edges, 2 * width), F32),
-            pltpu.VMEM((trips, 2 * width), F32),
+            pltpu.VMEM((NS * edges // 2, 2 * width), F32),
+            pltpu.VMEM((BLOCK, 2 * width), F32),
+            pltpu.VMEM((BLOCK, 2 * width), F32),
             pltpu.VMEM((edges, 2 * width), F32),
+            pltpu.VMEM((2 * width, edges), F32),
         ],
         compiler_params=params(),
     )(
         pos,
         trip_count,
+        ids,
         trip_target[0],
         trip_basis[0, 0],
         bilinear.T,
@@ -264,6 +288,8 @@
     )
 
     got = lax.all_to_all(send, "tgt", split_axis=0, concat_axis=0, tiled=True)
+    got, y_w = lax.optimization_barrier((got, y_w))
+    cy_w = lax.ppermute(y_w, "tgt", across(1))
     turned = pl.pallas_call(
         turn_kernel,
         out_shape=struct((NS, 8, 2 * width)),
@@ -279,15 +305,16 @@
     skipped, part = pl.pallas_call(
         edge_kernel,
         out_shape=(struct((edges, wide)), struct((atoms, da))),
-        in_specs=[VM] * 7 + [HB] * 2 + [VM],
+        in_specs=[SM] + [VM] * 8 + [HB] * 4,
         out_specs=(VM, VM),
         scratch_shapes=[
             pltpu.VMEM((wide, wide), BF16),
             pltpu.VMEM((wide, wide), BF16),
-            pltpu.SemaphoreType.DMA((2,)),
+            pltpu.SemaphoreType.DMA((2, NT)),
         ],
         compiler_params=params(),
     )(
+        lax.axis_index("tgt").astype(jnp.int32).reshape(1, 1),
         rows,
         tm,
         arrived.reshape(edges // 2, 2 * width),
@@ -295,9 +322,11 @@
         edge_source[0],
         up_forward,
         up_reverse,
-        first_all,
-        second_all,
         atom_proj,
+        x_w,
+        y_w,
+        cx_w,
+        cy_w,
     )
 
     parts = lax.all_to_all(

time: 179 us -> 160 us (0.89)
  blocking collectives: 50.9 us -> 20 us
  starting transfers between devices: 29.3 us -> 59.5 us
  between operations: 14.9 us -> 1.55 us
  Pallas kernels: 25.4 us -> 18 us
    all_to_all x2 -> x0, blocking collectives: 31.1 us -> none  [the longest x1 20.4 us: local(): lax.all_to_all(turned, 'src', split_axis=0, concat_axis=0, tiled=True)]
    all_to_all x1, waiting for transfers between devices: 28.6 us -> 8.34 us  [local(): lax.all_to_all(far, 'src', split_axis=0, concat_axis=0, tiled=True, axis_...]
    all_to_all x0 -> x2, waiting for transfers between devices: none -> 17.7 us  [the longest x1 14.1 us: local(): lax.all_to_all(turned, 'src', split_axis=0, concat_axis=0, tiled=True)]
    ppermute x0 -> x6, starting transfers between devices: none -> 17.3 us  [the longest x3 10.5 us: local(): x_w = [own_w] + [lax.ppermute(own_w, 'tgt', along_x(d)) for d in (-1, 2, 1)]]
    ppermute x1, waiting for transfers between devices: 0.01 us -> 13.6 us  [local(): from_two = lax.ppermute(near, 'src', shift_two())]
    all_to_all x0 -> x2, starting transfers between devices: none -> 13.5 us  [the longest x1 7.48 us: local(): lax.all_to_all(turned, 'src', split_axis=0, concat_axis=0, tiled=True)]
    ppermute x1, waiting for transfers between devices: 15.7 us -> 2.63 us  [local(): from_next = lax.ppermute(near, 'src', shift(-1))]
    pallas_call x1, Pallas kernels: 16.1 us -> 6.49 us  [local(): pl.pallas_call(contract_kernel, out_shape=(struct((edges, width)), struct...]
  transfers between devices with their start and end apart: 6 -> 12, of which waited for: 3 -> 8; matrix products, arithmetic and copies ran while one was open for 0% -> 0% of each run, Pallas kernels for 10% -> 5%
where the time goes in v2:
time: 160 us; the launch traced here: 159 us
  starting transfers between devices  59.5 us (37%)
  waiting for transfers between devices  54.6 us (34%)
  blocking collectives  20 us (12%)
  Pallas kernels  18 us (11%)
  local copies, waits for them, and re-layouts  5.27 us (3%)
    all_to_all x1, starting transfers between devices, local(): lax.all_to_all(far, 'src', split_axis=0, concat_axis=0, tiled=True, axis_...  18.3 us
    all_to_all x1, waiting for transfers between devices, local(): lax.all_to_all(turned, 'src', split_axis=0, concat_axis=0, tiled=True)  14.1 us
    ppermute x1, waiting for transfers between devices, local(): from_two = lax.ppermute(near, 'src', shift_two())  13.6 us
    all_to_all x1, blocking collectives, local(): lax.all_to_all(part.reshape(NT, atoms // NT, da), 'tgt', split_axis=0, co...  10.9 us
    ppermute x3, starting transfers between devices, local(): x_w = [own_w] + [lax.ppermute(own_w, 'tgt', along_x(d)) for d in (-1, 2, 1)]  10.5 us
    all_to_all x1, blocking collectives, local(): lax.all_to_all(spread, 'tgt', split_axis=0, concat_axis=0, tiled=True)  9.06 us
    all_to_all x1, waiting for transfers between devices, local(): lax.all_to_all(far, 'src', split_axis=0, concat_axis=0, tiled=True, axis_...  8.34 us
    all_to_all x1, starting transfers between devices, local(): lax.all_to_all(turned, 'src', split_axis=0, concat_axis=0, tiled=True)  7.48 us
  transfers between devices with their start and end apart: 12, of which 8 were waited for; matrix products, arithmetic and copies ran while one was open for 0% of the time, Pallas kernels for 5%

profile of v2, /device:TPU:1, one launch (start us, length us, event | category | flops | bytes accessed | tf_op | source)
XLA Modules:
  0.0 159.0 jit_solution(6755998281101983505)
XLA Ops:
  0.6 0.0 copy-start
  0.6 1.2 copy-done
  1.9 0.0 copy-start.7
  1.9 0.9 copy-done.7
  2.8 0.0 copy-start.8
  2.8 0.9 copy-done.8
  3.7 0.0 copy-start.9
  3.7 0.9 copy-done.9
  4.6 1.3 shard_map.176
  5.9 18.3 %all-to-all-start = ((bf16[8,256,128]{2,1,0:T(8,128)(2,1)}), bf16[8,256,128]{2,1,0:T(8,128)(2,1)S(1)}, u32[]{:S(2)}, u32[]{:S(2)}) async-start(bf16[8,256,128]{2,1,0:T(8,128)(2,1)} %get-tuple-element.12), calls=%async_computation | async-start | bytes 1048576 | tf_op jit(solution)/shard_map/all_to_all | solution.py:246
  24.2 3.1 %collective-permute-start.5 = (bf16[2,64,1024]{2,1,0:T(8,128)(2,1)S(1)}, bf16[2,64,1024]{2,1,0:T(8,128)(2,1)S(1)}, u32[]{:S(2)}, u32[]{:S(2)}) collective-permute-start(bf16[2,64,1024]{2,1,0:T(8,128)(2,1)S(1)} %get-tuple-element.15), channel_id=1, source_target_pairs={{0,4},{1,5},{2,6},{3,7},{4,8},{5,9},{6,10},{7,11},{8,12},{9,13},{1... | collective-permute-start | bytes 786440 | tf_op jit(solution)/shard_map/ppermute | solution.py:249
  27.3 4.4 %collective-permute-start.4 = (bf16[2,64,1024]{2,1,0:T(8,128)(2,1)S(1)}, bf16[2,64,1024]{2,1,0:T(8,128)(2,1)S(1)}, u32[]{:S(2)}, u32[]{:S(2)}) collective-permute-start(bf16[2,64,1024]{2,1,0:T(8,128)(2,1)S(1)} %get-tuple-element.15), channel_id=1, source_target_pairs={{0,8},{1,9},{2,10},{3,11},{4,12},{5,13},{6,14},{7,15},{8,0},{9,1},... | collective-permute-start | bytes 786440 | tf_op jit(solution)/shard_map/ppermute | solution.py:249
  31.6 3.1 %collective-permute-start.3 = (bf16[2,64,1024]{2,1,0:T(8,128)(2,1)S(1)}, bf16[2,64,1024]{2,1,0:T(8,128)(2,1)S(1)}, u32[]{:S(2)}, u32[]{:S(2)}) collective-permute-start(bf16[2,64,1024]{2,1,0:T(8,128)(2,1)S(1)} %get-tuple-element.15), channel_id=1, source_target_pairs={{0,12},{1,13},{2,14},{3,15},{4,0},{5,1},{6,2},{7,3},{8,4},{9,5},{1... | collective-permute-start | bytes 786440 | tf_op jit(solution)/shard_map/ppermute | solution.py:249
  34.7 0.0 collective-permute-done.5
  34.7 6.0 %collective-permute-done.4 = bf16[2,64,1024]{2,1,0:T(8,128)(2,1)S(1)} collective-permute-done((bf16[2,64,1024]{2,1,0:T(8,128)(2,1)S(1)}, bf16[2,64,1024]{2,1,0:T(8,128)(2,1)S(1)}, u32[]{:S(2)}, u32[]{:S(2)}) %collective-permute-start.4) | collective-permute-done | bytes 262176 | tf_op jit(solution)/shard_map/ppermute | solution.py:249
  40.7 1.2 collective-permute-done.3
  41.9 0.0 copy-start.10
  41.9 0.0 copy-start.11
  41.9 0.1 pad_maximum_fusion.wa_ref
  42.1 2.3 %collective-permute-start.6 = (bf16[4,2,64,1024]{3,2,1,0:T(8,128)(2,1)S(1)}, bf16[4,2,64,1024]{3,2,1,0:T(8,128)(2,1)}, u32[]{:S(2)}, u32[]{:S(2)}) collective-permute-start(bf16[4,2,64,1024]{3,2,1,0:T(8,128)(2,1)S(1)} %pad_maximum_fusion.wa_ref), channel_id=1, source_target_pairs={{0,2},{1,3},{2,0},{3,1},{4,6},{5,7},{6,4},{7,5},{8,10},{9,11},{10,... | collective-permute-start | bytes 3145736 | tf_op jit(solution)/shard_map/ppermute | solution.py:255
  44.4 0.0 copy-start.12
  45.1 8.3 %all-to-all-done.b0 = bf16[8,256,128]{2,1,0:T(8,128)(2,1)S(1)} async-done(((bf16[8,256,128]{2,1,0:T(8,128)(2,1)}), bf16[8,256,128]{2,1,0:T(8,128)(2,1)S(1)}, u32[]{:S(2)}, u32[]{:S(2)}) %all-to-all-start) | async-done | bytes 524320 | tf_op jit(solution)/shard_map/all_to_all | solution.py:246
  53.4 0.0 copy-start.14
  53.4 3.1 %collective-permute-start.2 = (bf16[8,256,128]{2,1,0:T(8,128)(2,1)S(1)}, bf16[8,256,128]{2,1,0:T(8,128)(2,1)S(1)}, u32[]{:S(2)}, u32[]{:S(2)}) collective-permute-start(bf16[8,256,128]{2,1,0:T(8,128)(2,1)S(1)} %all-to-all-done.b0), channel_id=1, source_target_pairs={{0,32},{16,48},{32,64},{48,80},{64,96},{80,112},{96,128},{112,144}... | collective-permute-start | bytes 1572872 | tf_op jit(solution)/shard_map/ppermute | solution.py:251
  56.5 2.9 %collective-permute-start.1 = (bf16[8,256,128]{2,1,0:T(8,128)(2,1)S(1)}, bf16[8,256,128]{2,1,0:T(8,128)(2,1)S(1)}, u32[]{:S(2)}, u32[]{:S(2)}) collective-permute-start(bf16[8,256,128]{2,1,0:T(8,128)(2,1)S(1)} %all-to-all-done.b0), channel_id=1, source_target_pairs={{0,64},{16,80},{32,480},{48,496},{64,128},{80,144},{96,32},{112,48... | collective-permute-start | bytes 1572872 | tf_op jit(solution)/shard_map/ppermute | solution.py:252
  59.4 4.5 %collective-permute-start = (bf16[8,256,128]{2,1,0:T(8,128)(2,1)S(1)}, bf16[8,256,128]{2,1,0:T(8,128)(2,1)S(1)}, u32[]{:S(2)}, u32[]{:S(2)}) collective-permute-start(bf16[8,256,128]{2,1,0:T(8,128)(2,1)S(1)} %all-to-all-done.b0), channel_id=1, source_target_pairs={{0,480},{16,496},{32,0},{48,16},{64,32},{80,48},{96,64},{112,80},{... | collective-permute-start | bytes 1572872 | tf_op jit(solution)/shard_map/ppermute | solution.py:250
  63.9 0.0 copy-done.12
  63.9 0.1 and_add_fusion.pos_ref
  64.0 5.1 %collective-permute-done.2.b3 = bf16[8,256,128]{2,1,0:T(8,128)(2,1)S(1)} collective-permute-done((bf16[8,256,128]{2,1,0:T(8,128)(2,1)S(1)}, bf16[8,256,128]{2,1,0:T(8,128)(2,1)S(1)}, u32[]{:S(2)}, u32[]{:S(2)}) %collective-permute-start.2) | collective-permute-done | bytes 524320 | tf_op jit(solution)/shard_map/ppermute | solution.py:251
  69.0 13.6 %collective-permute-done.1.b2 = bf16[8,256,128]{2,1,0:T(8,128)(2,1)S(1)} collective-permute-done((bf16[8,256,128]{2,1,0:T(8,128)(2,1)S(1)}, bf16[8,256,128]{2,1,0:T(8,128)(2,1)S(1)}, u32[]{:S(2)}, u32[]{:S(2)}) %collective-permute-start.1) | collective-permute-done | bytes 524320 | tf_op jit(solution)/shard_map/ppermute | solution.py:252
  82.6 2.6 %collective-permute-done.b1 = bf16[8,256,128]{2,1,0:T(8,128)(2,1)S(1)} collective-permute-done((bf16[8,256,128]{2,1,0:T(8,128)(2,1)S(1)}, bf16[8,256,128]{2,1,0:T(8,128)(2,1)S(1)}, u32[]{:S(2)}, u32[]{:S(2)}) %collective-permute-start) | collective-permute-done | bytes 524320 | tf_op jit(solution)/shard_map/ppermute | solution.py:250
  85.3 0.0 copy-done.10
  85.3 0.0 copy-done.11
  85.3 0.0 copy-done.14
  85.3 0.0 copy-start.3
  85.3 6.5 %shard_map.177 = (bf16[512,64]{1,0:T(8,128)(2,1)S(1)}, bf16[16,16,128]{2,1,0:T(8,128)(2,1)S(1)}) custom-call(s32[1,4096]{1,0:T(1,128)S(1)} %and_add_fusion.pos_ref, s32[1,1]{1,0:T(1,128)S(6)} %copy.19.cnt_ref, s32[1,4096]{1,0:T(1,128)S(1)} %bitcast.29, s32[1,4096]{1,0:T(1,128)S(1)} %bitcast.30, bf16[16,4096]{1,0:T(8,128)(2,1)S(1)} %bitcast.27, ...), custom_call_target="tpu_custom_call" | custom-call | tf_op jit(solution)/shard_map/pallas_call | solution.py:264
  91.8 0.0 copy-start.13
  91.8 0.6 copy-done.13
  92.4 6.0 %all-to-all-start.1 = ((bf16[16,16,128]{2,1,0:T(8,128)(2,1)}), bf16[16,16,128]{2,1,0:T(8,128)(2,1)S(1)}, u32[]{:S(2)}, u32[]{:S(2)}) async-start(bf16[16,16,128]{2,1,0:T(8,128)(2,1)} %copy-done.13), calls=%async_computation.1 | async-start | bytes 131072 | tf_op jit(solution)/shard_map/all_to_all | solution.py:290
  98.4 0.0 copy-start.5
  98.4 2.1 %collective-permute-start.7 = (bf16[4,2,64,1024]{3,2,1,0:T(8,128)(2,1)S(1)}, bf16[4,2,64,1024]{3,2,1,0:T(8,128)(2,1)}, u32[]{:S(2)}, u32[]{:S(2)}) collective-permute-start(bf16[4,2,64,1024]{3,2,1,0:T(8,128)(2,1)S(1)} %pad_maximum_fusion.wa_ref), channel_id=1, source_target_pairs={{0,1},{1,0},{2,3},{3,2},{4,5},{5,4},{6,7},{7,6},{8,9},{9,8},{10,11... | collective-permute-start | bytes 3145736 | tf_op jit(solution)/shard_map/ppermute | solution.py:256
  100.6 0.0 collective-permute-done.6.wb_ref
  100.6 3.7 %all-to-all-done.1.x_ref = bf16[16,16,128]{2,1,0:T(8,128)(2,1)S(1)} async-done(((bf16[16,16,128]{2,1,0:T(8,128)(2,1)}), bf16[16,16,128]{2,1,0:T(8,128)(2,1)S(1)}, u32[]{:S(2)}, u32[]{:S(2)}) %all-to-all-start.1) | async-done | bytes 65568 | tf_op jit(solution)/shard_map/all_to_all | solution.py:290
  104.3 2.3 %collective-permute-start.8 = (bf16[4,2,64,1024]{3,2,1,0:T(8,128)(2,1)}, bf16[4,2,64,1024]{3,2,1,0:T(8,128)(2,1)}, u32[]{:S(2)}, u32[]{:S(2)}) collective-permute-start(bf16[4,2,64,1024]{3,2,1,0:T(8,128)(2,1)} %collective-permute-done.6.wb_ref), channel_id=1, source_target_pairs={{0,1},{1,0},{2,3},{3,2},{4,5},{5,4},{6,7},{7,6},{8,9},{9,8},{10,11... | collective-permute-start | bytes 3145736 | tf_op jit(solution)/shard_map/ppermute | solution.py:292
  106.6 0.8 shard_map.178
  107.3 7.5 %all-to-all-start.2 = ((bf16[32,8,128]{2,1,0:T(8,128)(2,1)}), bf16[32,8,128]{2,1,0:T(8,128)(2,1)S(1)}, u32[]{:S(2)}, u32[]{:S(2)}) async-start(bf16[32,8,128]{2,1,0:T(8,128)(2,1)} %shard_map.178), calls=%async_computation.2 | async-start | bytes 131072 | tf_op jit(solution)/shard_map/all_to_all | solution.py:301
  114.8 0.0 collective-permute-done.7.wc_ref
  114.8 14.1 %all-to-all-done.2 = bf16[32,8,128]{2,1,0:T(8,128)(2,1)S(1)} async-done(((bf16[32,8,128]{2,1,0:T(8,128)(2,1)}), bf16[32,8,128]{2,1,0:T(8,128)(2,1)S(1)}, u32[]{:S(2)}, u32[]{:S(2)}) %all-to-all-start.2) | async-done | bytes 65568 | tf_op jit(solution)/shard_map/all_to_all | solution.py:301
  128.9 0.0 collective-permute-done.8.wd_ref
  128.9 0.0 copy-done.1
  128.9 0.0 copy-done.3
  128.9 0.0 copy-done.4
  128.9 0.0 copy-done.5
  128.9 0.6 copy-done.17
  129.6 0.0 copy-done.15
  129.6 6.8 %shard_map.179 = (bf16[512,1024]{1,0:T(8,128)(2,1)S(1)}, bf16[256,256]{1,0:T(8,128)(2,1)S(1)}) custom-call(s32[1,1]{1,0:T(1,128)} %bitcast.me_ref, bf16[512,1024]{1,0:T(8,128)(2,1)S(1)} %bitcast.21, bf16[512,64]{1,0:T(8,128)(2,1)S(1)} %get-tuple-element.13.tm_ref, bf16[256,128]{1,0:T(8,128)(2,1)S(1)} %bitcast.23, s32[1,512]{1,0:T(1,128)S(1)} %bitcast.34, ...), custom_call_target="tpu_custom_call" | custom-call | tf_op jit(solution)/shard_map/pallas_call | solution.py:305
  136.4 0.0 copy-start.2
  136.4 10.9 %all_to_all.25.parts_ref = bf16[16,16,256]{2,1,0:T(8,128)(2,1)S(1)} all-to-all(bf16[16,16,256]{2,1,0:T(8,128)(2,1)S(1)} %bitcast.25), channel_id=1, replica_groups=mesh['src'=32,'tgt'=16] {'tgt'}, dimensions={0} | all-to-all | bytes 262144 | tf_op jit(solution)/shard_map/all_to_all | solution.py:332
  147.3 0.0 copy-done.6
  147.3 0.0 copy-done.16
  147.3 0.8 shard_map.180
  148.1 9.1 %all_to_all.26 = bf16[16,16,256]{2,1,0:T(8,128)(2,1)S(1)} all-to-all(bf16[16,16,256]{2,1,0:T(8,128)(2,1)S(1)} %get-tuple-element.20), channel_id=1, replica_groups=mesh['src'=32,'tgt'=16] {'tgt'}, dimensions={0} | all-to-all | bytes 262144 | tf_op jit(solution)/shard_map/all_to_all | solution.py:342
  157.2 0.0 copy-done.2
  157.2 1.9 %shard_map.181 = bf16[512,1024]{1,0:T(8,128)(2,1)} custom-call(bf16[512,1024]{1,0:T(8,128)(2,1)S(1)} %get-tuple-element.18.skip_ref, bf16[256,256]{1,0:T(8,128)(2,1)S(1)} %bitcast.22, s32[1,512]{1,0:T(1,128)S(1)} %bitcast.32, bf16[256,1024]{1,0:T(8,128)(2,1)S(1)} %copy-done.2), custom_call_target="tpu_custom_call" | custom-call | tf_op jit(solution)/shard_map/pallas_call | solution.py:343
  (6 shorter events, 0.0 us)
Async XLA Ops:
  0.6 1.2 copy-start
  1.9 0.9 copy-start.7
  2.8 0.9 copy-start.8
  3.7 0.9 copy-start.9
  5.9 47.5 %all-to-all-start = ((bf16[8,256,128]{2,1,0:T(8,128)(2,1)}), bf16[8,256,128]{2,1,0:T(8,128)(2,1)S(1)}, u32[]{:S(2)}, u32[]{:S(2)}) async-start(bf16[8,256,128]{2,1,0:T(8,128)(2,1)} %get-tuple-element.12), calls=%async_computation | async-start | bytes 1048576 | tf_op jit(solution)/shard_map/all_to_all | solution.py:246
  24.2 10.6 %collective-permute-start.5 = (bf16[2,64,1024]{2,1,0:T(8,128)(2,1)S(1)}, bf16[2,64,1024]{2,1,0:T(8,128)(2,1)S(1)}, u32[]{:S(2)}, u32[]{:S(2)}) collective-permute-start(bf16[2,64,1024]{2,1,0:T(8,128)(2,1)S(1)} %get-tuple-element.15), channel_id=1, source_target_pairs={{0,4},{1,5},{2,6},{3,7},{4,8},{5,9},{6,10},{7,11},{8,12},{9,13},{1... | collective-permute-start | bytes 786440 | tf_op jit(solution)/shard_map/ppermute | solution.py:249
  27.3 13.4 %collective-permute-start.4 = (bf16[2,64,1024]{2,1,0:T(8,128)(2,1)S(1)}, bf16[2,64,1024]{2,1,0:T(8,128)(2,1)S(1)}, u32[]{:S(2)}, u32[]{:S(2)}) collective-permute-start(bf16[2,64,1024]{2,1,0:T(8,128)(2,1)S(1)} %get-tuple-element.15), channel_id=1, source_target_pairs={{0,8},{1,9},{2,10},{3,11},{4,12},{5,13},{6,14},{7,15},{8,0},{9,1},... | collective-permute-start | bytes 786440 | tf_op jit(solution)/shard_map/ppermute | solution.py:249
  31.6 10.3 %collective-permute-start.3 = (bf16[2,64,1024]{2,1,0:T(8,128)(2,1)S(1)}, bf16[2,64,1024]{2,1,0:T(8,128)(2,1)S(1)}, u32[]{:S(2)}, u32[]{:S(2)}) collective-permute-start(bf16[2,64,1024]{2,1,0:T(8,128)(2,1)S(1)} %get-tuple-element.15), channel_id=1, source_target_pairs={{0,12},{1,13},{2,14},{3,15},{4,0},{5,1},{6,2},{7,3},{8,4},{9,5},{1... | collective-permute-start | bytes 786440 | tf_op jit(solution)/shard_map/ppermute | solution.py:249
  41.9 43.3 %copy-start.10 = (bf16[1,1,16,4096]{3,2,1,0:T(8,128)(2,1)S(1)}, bf16[1,1,16,4096]{3,2,1,0:T(8,128)(2,1)}, u32[]{:S(2)}) copy-start(bf16[1,1,16,4096]{3,2,1,0:T(8,128)(2,1)} %param.23) | copy-start | bytes 393220
  41.9 43.3 %copy-start.11 = (bf16[1024,64]{0,1:T(8,128)(2,1)S(1)}, bf16[1024,64]{0,1:T(8,128)(2,1)}, u32[]{:S(2)}) copy-start(bf16[1024,64]{0,1:T(8,128)(2,1)} %param.26) | copy-start | bytes 393220
  42.1 58.5 %collective-permute-start.6 = (bf16[4,2,64,1024]{3,2,1,0:T(8,128)(2,1)S(1)}, bf16[4,2,64,1024]{3,2,1,0:T(8,128)(2,1)}, u32[]{:S(2)}, u32[]{:S(2)}) collective-permute-start(bf16[4,2,64,1024]{3,2,1,0:T(8,128)(2,1)S(1)} %pad_maximum_fusion.wa_ref), channel_id=1, source_target_pairs={{0,2},{1,3},{2,0},{3,1},{4,6},{5,7},{6,4},{7,5},{8,10},{9,11},{10,... | collective-permute-start | bytes 3145736 | tf_op jit(solution)/shard_map/ppermute | solution.py:255
  44.4 19.5 %copy-start.12 = (s32[1,1,4096]{2,1,0:T(1,128)S(1)}, s32[1,1,4096]{2,1,0:T(1,128)}, u32[]{:S(2)}) copy-start(s32[1,1,4096]{2,1,0:T(1,128)} %param.20) | copy-start | bytes 49156
  53.4 31.9 %copy-start.14 = (s32[1,1,4096]{2,1,0:T(1,128)S(1)}, s32[1,1,4096]{2,1,0:T(1,128)}, u32[]{:S(2)}) copy-start(s32[1,1,4096]{2,1,0:T(1,128)} %param.21) | copy-start | bytes 49156
  53.4 15.6 %collective-permute-start.2 = (bf16[8,256,128]{2,1,0:T(8,128)(2,1)S(1)}, bf16[8,256,128]{2,1,0:T(8,128)(2,1)S(1)}, u32[]{:S(2)}, u32[]{:S(2)}) collective-permute-start(bf16[8,256,128]{2,1,0:T(8,128)(2,1)S(1)} %all-to-all-done.b0), channel_id=1, source_target_pairs={{0,32},{16,48},{32,64},{48,80},{64,96},{80,112},{96,128},{112,144}... | collective-permute-start | bytes 1572872 | tf_op jit(solution)/shard_map/ppermute | solution.py:251
  56.5 26.1 %collective-permute-start.1 = (bf16[8,256,128]{2,1,0:T(8,128)(2,1)S(1)}, bf16[8,256,128]{2,1,0:T(8,128)(2,1)S(1)}, u32[]{:S(2)}, u32[]{:S(2)}) collective-permute-start(bf16[8,256,128]{2,1,0:T(8,128)(2,1)S(1)} %all-to-all-done.b0), channel_id=1, source_target_pairs={{0,64},{16,80},{32,480},{48,496},{64,128},{80,144},{96,32},{112,48... | collective-permute-start | bytes 1572872 | tf_op jit(solution)/shard_map/ppermute | solution.py:252
  59.4 25.9 %collective-permute-start = (bf16[8,256,128]{2,1,0:T(8,128)(2,1)S(1)}, bf16[8,256,128]{2,1,0:T(8,128)(2,1)S(1)}, u32[]{:S(2)}, u32[]{:S(2)}) collective-permute-start(bf16[8,256,128]{2,1,0:T(8,128)(2,1)S(1)} %all-to-all-done.b0), channel_id=1, source_target_pairs={{0,480},{16,496},{32,0},{48,16},{64,32},{80,48},{96,64},{112,80},{... | collective-permute-start | bytes 1572872 | tf_op jit(solution)/shard_map/ppermute | solution.py:250
  85.3 43.6 %copy-start.1 = (bf16[1,1,512,1024]{3,2,1,0:T(8,128)(2,1)S(1)}, bf16[1,1,512,1024]{3,2,1,0:T(8,128)(2,1)}, u32[]{:S(2)}) copy-start(bf16[1,1,512,1024]{3,2,1,0:T(8,128)(2,1)} %param.17) | copy-start | bytes 3145732
  85.3 43.6 %copy-start.3 = (bf16[1024,256]{1,0:T(8,128)(2,1)S(1)}, bf16[1024,256]{1,0:T(8,128)(2,1)}, u32[]{:S(2)}) copy-start(bf16[1024,256]{1,0:T(8,128)(2,1)} %proj_ref.1) | copy-start | bytes 1572868
  91.8 0.6 copy-start.13
  92.4 11.9 %all-to-all-start.1 = ((bf16[16,16,128]{2,1,0:T(8,128)(2,1)}), bf16[16,16,128]{2,1,0:T(8,128)(2,1)S(1)}, u32[]{:S(2)}, u32[]{:S(2)}) async-start(bf16[16,16,128]{2,1,0:T(8,128)(2,1)} %copy-done.13), calls=%async_computation.1 | async-start | bytes 131072 | tf_op jit(solution)/shard_map/all_to_all | solution.py:290
  98.4 30.5 %copy-start.4 = (bf16[64,1024]{1,0:T(8,128)(2,1)S(1)}, bf16[64,1024]{1,0:T(8,128)(2,1)}, u32[]{:S(2)}) copy-start(bf16[64,1024]{1,0:T(8,128)(2,1)} %upf_ref.1) | copy-start | bytes 393220
  98.4 30.5 %copy-start.5 = (bf16[64,1024]{1,0:T(8,128)(2,1)S(1)}, bf16[64,1024]{1,0:T(8,128)(2,1)}, u32[]{:S(2)}) copy-start(bf16[64,1024]{1,0:T(8,128)(2,1)} %upr_ref.1) | copy-start | bytes 393220
  98.4 16.4 %collective-permute-start.7 = (bf16[4,2,64,1024]{3,2,1,0:T(8,128)(2,1)S(1)}, bf16[4,2,64,1024]{3,2,1,0:T(8,128)(2,1)}, u32[]{:S(2)}, u32[]{:S(2)}) collective-permute-start(bf16[4,2,64,1024]{3,2,1,0:T(8,128)(2,1)S(1)} %pad_maximum_fusion.wa_ref), channel_id=1, source_target_pairs={{0,1},{1,0},{2,3},{3,2},{4,5},{5,4},{6,7},{7,6},{8,9},{9,8},{10,11... | collective-permute-start | bytes 3145736 | tf_op jit(solution)/shard_map/ppermute | solution.py:256
  104.3 24.6 %collective-permute-start.8 = (bf16[4,2,64,1024]{3,2,1,0:T(8,128)(2,1)}, bf16[4,2,64,1024]{3,2,1,0:T(8,128)(2,1)}, u32[]{:S(2)}, u32[]{:S(2)}) collective-permute-start(bf16[4,2,64,1024]{3,2,1,0:T(8,128)(2,1)} %collective-permute-done.6.wb_ref), channel_id=1, source_target_pairs={{0,1},{1,0},{2,3},{3,2},{4,5},{5,4},{6,7},{7,6},{8,9},{9,8},{10,11... | collective-permute-start | bytes 3145736 | tf_op jit(solution)/shard_map/ppermute | solution.py:292
  107.3 21.6 %all-to-all-start.2 = ((bf16[32,8,128]{2,1,0:T(8,128)(2,1)}), bf16[32,8,128]{2,1,0:T(8,128)(2,1)S(1)}, u32[]{:S(2)}, u32[]{:S(2)}) async-start(bf16[32,8,128]{2,1,0:T(8,128)(2,1)} %shard_map.178), calls=%async_computation.2 | async-start | bytes 131072 | tf_op jit(solution)/shard_map/all_to_all | solution.py:301
  128.9 0.7 copy-start.17
  128.9 0.7 copy-start.15
  129.6 17.7 %copy-start.6 = (bf16[256,256]{1,0:T(8,128)(2,1)S(1)}, bf16[256,256]{1,0:T(8,128)(2,1)}, u32[]{:S(2)}) copy-start(bf16[256,256]{1,0:T(8,128)(2,1)} %w_ref.1) | copy-start | bytes 393220
  129.6 17.7 %copy-start.16 = (bf16[1,16,256]{2,1,0:T(8,128)(2,1)S(1)}, bf16[1,16,256]{2,1,0:T(8,128)(2,1)}, u32[]{:S(2)}) copy-start(bf16[1,16,256]{2,1,0:T(8,128)(2,1)} %param.18) | copy-start | bytes 24580
  136.4 20.8 %copy-start.2 = (bf16[256,1024]{1,0:T(8,128)(2,1)S(1)}, bf16[256,1024]{1,0:T(8,128)(2,1)}, u32[]{:S(2)}) copy-start(bf16[256,1024]{1,0:T(8,128)(2,1)} %back_ref.1) | copy-start | bytes 1572868

commit v3 on v2

--- a/solution.py
+++ b/solution.py
@@ -15,6 +15,7 @@
 Z, YH, NT = 16, 2, 16
 NS = Z * YH
 FAR = 8
+NEAR = YH * NT
 XS = 4
 PEER = (0, 2, 1, 3)
 BLOCK = 1024
@@ -37,14 +38,23 @@
 HB = pl.BlockSpec(memory_space=pl.ANY)
 
 
-def down_kernel(x_ref, w_ref, a_ref, b_ref, o_ref, ab_ref):
-    ab_ref[0] = a_ref[...]
-    ab_ref[1] = b_ref[...]
-    y = silu(dot(x_ref[...], w_ref[...], 1, 1)).astype(BF16)
+def down_kernel(x_ref, w_ref, o_ref, x, w, sems):
+    load_w = pltpu.make_async_copy(w_ref, w, sems.at[0])
+    load_x = pltpu.make_async_copy(x_ref, x, sems.at[1])
+    load_w.start()
+    load_x.start()
+    load_w.wait()
+    load_x.wait()
+    y = silu(dot(x[...], w[...], 1, 1)).astype(BF16)
     half = y.shape[0] // 2
     packed = jnp.concatenate([y[:half], y[half:]], axis=1)
     for i in range(o_ref.shape[0]):
         o_ref[i] = packed
+
+
+def pack_kernel(after_ref, a_ref, b_ref, ab_ref):
+    ab_ref[0] = a_ref[...]
+    ab_ref[1] = b_ref[...]
 
 
 def contract_kernel(
@@ -100,20 +110,21 @@
     msg = jnp.transpose(total[:width, :] + total[width:, :]).astype(BF16)
     tm_ref[...] = msg
     acc[:, :width] = msg.astype(F32)
-    for t in range(NT):
-        first = acc[pl.ds(t, NT, stride=NT), :]
-        second = acc[pl.ds(NT * NT + t, NT, stride=NT), :]
-        send_ref[t] = jnp.concatenate([first[:, :width], second[:, :width]], axis=1).astype(BF16)
+    for m in range(NEAR):
+        first = acc[pl.ds(m, Z // 2, stride=NEAR), :]
+        second = acc[pl.ds(NEAR * Z // 2 + m, Z // 2, stride=NEAR), :]
+        send_ref[m] = jnp.concatenate([first[:, :width], second[:, :width]], axis=1).astype(BF16)
 
 
 def turn_kernel(x_ref, o_ref, tmp):
     width = x_ref.shape[2] // 2
+    half = Z // 2
     tmp[...] = x_ref[...].reshape(tmp.shape).astype(F32)
-    for s in range(NT):
-        first = tmp[pl.ds(s, 8, stride=NT), :]
-        second = tmp[pl.ds(8 * NT + s, 8, stride=NT), :]
-        o_ref[s] = jnp.concatenate([first[:, :width], second[:, :width]], axis=1).astype(BF16)
-        o_ref[NT + s] = jnp.concatenate([first[:, width:], second[:, width:]], axis=1).astype(BF16)
+    for j in range(half):
+        first = tmp[pl.ds(j, NEAR // 2, stride=half), :]
+        second = tmp[pl.ds(NEAR // 2 * half + j, NEAR // 2, stride=half), :]
+        o_ref[j] = jnp.concatenate([first[:, :width], second[:, :width]], axis=1).astype(BF16)
+        o_ref[half + j] = jnp.concatenate([first[:, width:], second[:, width:]], axis=1).astype(BF16)
 
 
 def edge_kernel(
@@ -139,7 +150,7 @@
     got = got_ref[...]
     got = jnp.concatenate([got[:, :width], got[:, width:]], axis=0)
     perm = perm_ref[...]
-    row = ((perm >> 3) & 1) * (edges // 2) + (perm >> 4) * 8 + (perm & 7)
+    row = ((perm >> 4) & 1) * (edges // 2) + (perm >> 5) * 16 + (perm & 15)
     hot = jnp.where(
         lax.broadcasted_iota(jnp.int32, (edges, edges), 0) == row, 1.0, 0.0
     ).astype(BF16)
@@ -232,13 +243,18 @@
     width = down_proj.shape[1]
     trips = trip_source.shape[2]
 
-    far, own_w = pl.pallas_call(
+    far = pl.pallas_call(
         down_kernel,
-        out_shape=(struct((FAR, edges // 2, 2 * width)), struct((2,) + res_first.shape)),
-        in_specs=[VM] * 4,
-        out_specs=(VM, VM),
-        compiler_params=params(),
-    )(rows, down_proj.T, res_first, res_second)
+        out_shape=struct((FAR, edges // 2, 2 * width)),
+        in_specs=[HB] * 2,
+        out_specs=VM,
+        scratch_shapes=[
+            pltpu.VMEM((edges, wide), BF16),
+            pltpu.VMEM((width, wide), BF16),
+            pltpu.SemaphoreType.DMA((2,)),
+        ],
+        compiler_params=params(),
+    )(rows, down_proj.T)
 
     groups = [
         [((z0 + 4 * i) % Z) * YH + h for i in range(4) for h in range(YH)] for z0 in range(4)
@@ -246,6 +262,13 @@
     near = lax.all_to_all(
         far, "src", split_axis=0, concat_axis=0, tiled=True, axis_index_groups=groups
     )
+    own_w = pl.pallas_call(
+        pack_kernel,
+        out_shape=struct((2,) + res_first.shape),
+        in_specs=[HB, VM, VM],
+        out_specs=VM,
+        compiler_params=params(),
+    )(far, res_first, res_second)
     x_w = [own_w] + [lax.ppermute(own_w, "tgt", along_x(d)) for d in (-1, 2, 1)]
     from_next = lax.ppermute(near, "src", shift(-1))
     from_prev = lax.ppermute(near, "src", shift(1))
@@ -263,7 +286,7 @@
 
     tm, send = pl.pallas_call(
         contract_kernel,
-        out_shape=(struct((edges, width)), struct((NT, NT, 2 * width))),
+        out_shape=(struct((edges, width)), struct((NEAR, Z // 2, 2 * width))),
         in_specs=[SM, SM] + [VM] * 8,
         out_specs=(VM, VM),
         scratch_shapes=[
@@ -274,6 +297,7 @@
             pltpu.VMEM((2 * width, edges), F32),
         ],
         compiler_params=params(),
+        cost_estimate=pl.CostEstimate(flops=10**11, bytes_accessed=10**7, transcendentals=0),
     )(
         pos,
         trip_count,
@@ -287,18 +311,24 @@
         from_prev,
     )
 
-    got = lax.all_to_all(send, "tgt", split_axis=0, concat_axis=0, tiled=True)
+    plane = [[(z * YH + h) * NT + t for h in range(YH) for t in range(NT)] for z in range(Z)]
+    lines = [[z * YH + h for z in range(Z)] for h in range(YH)]
+    got = lax.all_to_all(
+        send, ("src", "tgt"), split_axis=0, concat_axis=0, tiled=True, axis_index_groups=plane
+    )
     got, y_w = lax.optimization_barrier((got, y_w))
     cy_w = lax.ppermute(y_w, "tgt", across(1))
     turned = pl.pallas_call(
         turn_kernel,
-        out_shape=struct((NS, 8, 2 * width)),
+        out_shape=struct((Z, NEAR // 2, 2 * width)),
         in_specs=[VM],
         out_specs=VM,
-        scratch_shapes=[pltpu.VMEM((NT * NT, 2 * width), F32)],
+        scratch_shapes=[pltpu.VMEM((NEAR * Z // 2, 2 * width), F32)],
         compiler_params=params(),
     )(got)
-    arrived = lax.all_to_all(turned, "src", split_axis=0, concat_axis=0, tiled=True)
+    arrived = lax.all_to_all(
+        turned, "src", split_axis=0, concat_axis=0, tiled=True, axis_index_groups=lines
+    )
 
     atoms = atom_state.shape[1] * NT
     da = atom_state.shape[2]

time: 160 us -> 162 us (1.012)
  Pallas kernels: 18 us -> 20.2 us
    all_to_all x1, waiting for transfers between devices: 8.34 us -> 18.6 us  [local(): lax.all_to_all(far, 'src', split_axis=0, concat_axis=0, tiled=True, axis_...]
    ppermute x3, waiting for transfers between devices: 7.2 us -> 0.01 us  [local(): x_w = [own_w] + [lax.ppermute(own_w, 'tgt', along_x(d)) for d in (-1, 2, 1)]]
    ppermute x1, waiting for transfers between devices: 5.08 us -> 1.66 us  [local(): from_prev = lax.ppermute(near, 'src', shift(1))]
    ppermute x1, waiting for transfers between devices: 2.63 us -> 4.36 us  [local(): from_next = lax.ppermute(near, 'src', shift(-1))]
    unnamed x36 -> x42, local copies, waits for them, and re-layouts: 5.27 us -> 6.5 us
  transfers between devices with their start and end apart: 12 -> 12, of which waited for: 8 -> 6; matrix products, arithmetic and copies ran while one was open for 0% -> 0% of each run, Pallas kernels for 5% -> 5%
where the time goes in v3:
time: 162 us; the launch traced here: 161 us
  starting transfers between devices  59.1 us (36%)
  waiting for transfers between devices  53.3 us (33%)
  Pallas kernels  20.2 us (12%)
  blocking collectives  19.9 us (12%)
  local copies, waits for them, and re-layouts  6.5 us (4%)
    all_to_all x1, waiting for transfers between devices, local(): lax.all_to_all(far, 'src', split_axis=0, concat_axis=0, tiled=True, axis_...  18.6 us
    all_to_all x1, starting transfers between devices, local(): lax.all_to_all(far, 'src', split_axis=0, concat_axis=0, tiled=True, axis_...  18.4 us
    ppermute x1, waiting for transfers between devices, local(): from_two = lax.ppermute(near, 'src', shift_two())  12.1 us
    all_to_all x1, waiting for transfers between devices, local(): lax.all_to_all(turned, 'src', split_axis=0, concat_axis=0, tiled=True, ax...  11.6 us
    all_to_all x1, blocking collectives, local(): lax.all_to_all(part.reshape(NT, atoms // NT, da), 'tgt', split_axis=0, co...  10.8 us
    ppermute x3, starting transfers between devices, local(): x_w = [own_w] + [lax.ppermute(own_w, 'tgt', along_x(d)) for d in (-1, 2, 1)]  10.5 us
    all_to_all x1, blocking collectives, local(): lax.all_to_all(spread, 'tgt', split_axis=0, concat_axis=0, tiled=True)  9.06 us
    pallas_call x1, Pallas kernels, local(): pl.pallas_call(edge_kernel, out_shape=(struct((edges, wide)), struct((ato...  8.16 us
  transfers between devices with their start and end apart: 12, of which 6 were waited for; matrix products, arithmetic and copies ran while one was open for 0% of the time, Pallas kernels for 5%

profile of v3, /device:TPU:1, one launch (start us, length us, event | category | flops | bytes accessed | tf_op | source)
XLA Modules:
  0.0 160.8 jit_solution(8641972194817542318)
XLA Ops:
  0.6 0.0 copy-start
  0.6 1.2 copy-done
  1.9 0.9 copy-done.11
  2.8 1.5 shard_map.176.after_ref
  4.3 0.0 copy-start.12
  4.3 0.0 copy-start.13
  4.3 18.4 %all-to-all-start = ((bf16[8,256,128]{2,1,0:T(8,128)(2,1)}), bf16[8,256,128]{2,1,0:T(8,128)(2,1)S(1)}, u32[]{:S(2)}, u32[]{:S(2)}) async-start(bf16[8,256,128]{2,1,0:T(8,128)(2,1)} %shard_map.176.after_ref), calls=%async_computation | async-start | bytes 1048576 | tf_op jit(solution)/shard_map/all_to_all | solution.py:262
  22.7 0.0 copy-done.12
  22.7 0.0 copy-done.13
  22.8 3.1 %collective-permute-start.5 = (bf16[2,64,1024]{2,1,0:T(8,128)(2,1)S(1)}, bf16[2,64,1024]{2,1,0:T(8,128)(2,1)S(1)}, u32[]{:S(2)}, u32[]{:S(2)}) collective-permute-start(bf16[2,64,1024]{2,1,0:T(8,128)(2,1)S(1)} %shard_map.178), channel_id=1, source_target_pairs={{0,4},{1,5},{2,6},{3,7},{4,8},{5,9},{6,10},{7,11},{8,12},{9,13},{1... | collective-permute-start | bytes 786440 | tf_op jit(solution)/shard_map/ppermute | solution.py:272
  25.9 4.4 %collective-permute-start.4 = (bf16[2,64,1024]{2,1,0:T(8,128)(2,1)S(1)}, bf16[2,64,1024]{2,1,0:T(8,128)(2,1)S(1)}, u32[]{:S(2)}, u32[]{:S(2)}) collective-permute-start(bf16[2,64,1024]{2,1,0:T(8,128)(2,1)S(1)} %shard_map.178), channel_id=1, source_target_pairs={{0,8},{1,9},{2,10},{3,11},{4,12},{5,13},{6,14},{7,15},{8,0},{9,1},... | collective-permute-start | bytes 786440 | tf_op jit(solution)/shard_map/ppermute | solution.py:272
  30.3 3.1 %collective-permute-start.3 = (bf16[2,64,1024]{2,1,0:T(8,128)(2,1)S(1)}, bf16[2,64,1024]{2,1,0:T(8,128)(2,1)S(1)}, u32[]{:S(2)}, u32[]{:S(2)}) collective-permute-start(bf16[2,64,1024]{2,1,0:T(8,128)(2,1)S(1)} %shard_map.178), channel_id=1, source_target_pairs={{0,12},{1,13},{2,14},{3,15},{4,0},{5,1},{6,2},{7,3},{8,4},{9,5},{1... | collective-permute-start | bytes 786440 | tf_op jit(solution)/shard_map/ppermute | solution.py:272
  33.3 0.0 copy-start.14
  33.4 18.6 %all-to-all-done.b0 = bf16[8,256,128]{2,1,0:T(8,128)(2,1)S(1)} async-done(((bf16[8,256,128]{2,1,0:T(8,128)(2,1)}), bf16[8,256,128]{2,1,0:T(8,128)(2,1)S(1)}, u32[]{:S(2)}, u32[]{:S(2)}) %all-to-all-start) | async-done | bytes 524320 | tf_op jit(solution)/shard_map/all_to_all | solution.py:262
  52.0 2.9 %collective-permute-start.2 = (bf16[8,256,128]{2,1,0:T(8,128)(2,1)S(1)}, bf16[8,256,128]{2,1,0:T(8,128)(2,1)S(1)}, u32[]{:S(2)}, u32[]{:S(2)}) collective-permute-start(bf16[8,256,128]{2,1,0:T(8,128)(2,1)S(1)} %all-to-all-done.b0), channel_id=1, source_target_pairs={{0,32},{16,48},{32,64},{48,80},{64,96},{80,112},{96,128},{112,144}... | collective-permute-start | bytes 1572872 | tf_op jit(solution)/shard_map/ppermute | solution.py:274
  54.9 2.9 %collective-permute-start.1 = (bf16[8,256,128]{2,1,0:T(8,128)(2,1)S(1)}, bf16[8,256,128]{2,1,0:T(8,128)(2,1)S(1)}, u32[]{:S(2)}, u32[]{:S(2)}) collective-permute-start(bf16[8,256,128]{2,1,0:T(8,128)(2,1)S(1)} %all-to-all-done.b0), channel_id=1, source_target_pairs={{0,64},{16,80},{32,480},{48,496},{64,128},{80,144},{96,32},{112,48... | collective-permute-start | bytes 1572872 | tf_op jit(solution)/shard_map/ppermute | solution.py:275
  57.9 0.0 collective-permute-done.5
  57.9 4.5 %collective-permute-start = (bf16[8,256,128]{2,1,0:T(8,128)(2,1)S(1)}, bf16[8,256,128]{2,1,0:T(8,128)(2,1)S(1)}, u32[]{:S(2)}, u32[]{:S(2)}) collective-permute-start(bf16[8,256,128]{2,1,0:T(8,128)(2,1)S(1)} %all-to-all-done.b0), channel_id=1, source_target_pairs={{0,480},{16,496},{32,0},{48,16},{64,32},{80,48},{96,64},{112,80},{... | collective-permute-start | bytes 1572872 | tf_op jit(solution)/shard_map/ppermute | solution.py:273
  62.3 0.0 copy-done.14
  62.4 0.1 and_add_fusion.pos_ref
  63.1 0.0 collective-permute-done.4
  63.1 0.0 collective-permute-done.3
  63.1 0.0 copy-start.18
  63.1 0.0 copy-start.19
  63.1 0.0 copy-start.20
  63.1 0.1 pad_maximum_fusion.wa_ref
  63.3 0.0 copy-done.2
  63.3 2.3 %collective-permute-start.6 = (bf16[4,2,64,1024]{3,2,1,0:T(8,128)(2,1)S(1)}, bf16[4,2,64,1024]{3,2,1,0:T(8,128)(2,1)S(1)}, u32[]{:S(2)}, u32[]{:S(2)}) collective-permute-start(bf16[4,2,64,1024]{3,2,1,0:T(8,128)(2,1)S(1)} %pad_maximum_fusion.wa_ref), channel_id=1, source_target_pairs={{0,2},{1,3},{2,0},{3,1},{4,6},{5,7},{6,4},{7,5},{8,10},{9,11},{10,... | collective-permute-start | bytes 3145736 | tf_op jit(solution)/shard_map/ppermute | solution.py:278
  65.6 1.7 %collective-permute-done.2.b3 = bf16[8,256,128]{2,1,0:T(8,128)(2,1)S(1)} collective-permute-done((bf16[8,256,128]{2,1,0:T(8,128)(2,1)S(1)}, bf16[8,256,128]{2,1,0:T(8,128)(2,1)S(1)}, u32[]{:S(2)}, u32[]{:S(2)}) %collective-permute-start.2) | collective-permute-done | bytes 524320 | tf_op jit(solution)/shard_map/ppermute | solution.py:274
  67.3 12.1 %collective-permute-done.1.b2 = bf16[8,256,128]{2,1,0:T(8,128)(2,1)S(1)} collective-permute-done((bf16[8,256,128]{2,1,0:T(8,128)(2,1)S(1)}, bf16[8,256,128]{2,1,0:T(8,128)(2,1)S(1)}, u32[]{:S(2)}, u32[]{:S(2)}) %collective-permute-start.1) | collective-permute-done | bytes 524320 | tf_op jit(solution)/shard_map/ppermute | solution.py:275
  79.4 4.4 %collective-permute-done.b1 = bf16[8,256,128]{2,1,0:T(8,128)(2,1)S(1)} collective-permute-done((bf16[8,256,128]{2,1,0:T(8,128)(2,1)S(1)}, bf16[8,256,128]{2,1,0:T(8,128)(2,1)S(1)}, u32[]{:S(2)}, u32[]{:S(2)}) %collective-permute-start) | collective-permute-done | bytes 524320 | tf_op jit(solution)/shard_map/ppermute | solution.py:273
  83.7 0.0 copy-done.18
  83.7 0.0 copy-done.19
  83.7 0.0 copy-done.20
  83.8 1.0 copy-done.3
  84.8 7.1 %shard_map.177 = (bf16[512,64]{1,0:T(8,128)(2,1)S(1)}, bf16[32,8,128]{2,1,0:T(8,128)(2,1)}) custom-call(s32[1,4096]{1,0:T(1,128)S(1)} %and_add_fusion.pos_ref, s32[1,1]{1,0:T(1,128)S(6)} %copy.19.cnt_ref, s32[1,4096]{1,0:T(1,128)S(1)} %bitcast.27, s32[1,4096]{1,0:T(1,128)S(1)} %bitcast.34, bf16[16,4096]{1,0:T(8,128)(2,1)S(1)} %bitcast.32, ...), custom_call_target="tpu_custom_call" | custom-call | flops 99999997952 | bytes 10000000 | tf_op jit(solution)/shard_map/pallas_call | solution.py:287
  91.9 0.7 copy-done.8
  92.6 6.3 %all-to-all-start.1 = ((bf16[32,8,128]{2,1,0:T(8,128)(2,1)}), bf16[32,8,128]{2,1,0:T(8,128)(2,1)S(1)}, u32[]{:S(2)}, u32[]{:S(2)}) async-start(bf16[32,8,128]{2,1,0:T(8,128)(2,1)} %get-tuple-element.11), calls=%async_computation.1 | async-start | bytes 131072 | tf_op jit(solution)/shard_map/all_to_all | solution.py:316
  98.9 0.0 copy-start.6
  98.9 0.0 copy-start.7
  99.0 2.3 %collective-permute-start.7 = (bf16[4,2,64,1024]{3,2,1,0:T(8,128)(2,1)S(1)}, bf16[4,2,64,1024]{3,2,1,0:T(8,128)(2,1)}, u32[]{:S(2)}, u32[]{:S(2)}) collective-permute-start(bf16[4,2,64,1024]{3,2,1,0:T(8,128)(2,1)S(1)} %pad_maximum_fusion.wa_ref), channel_id=1, source_target_pairs={{0,1},{1,0},{2,3},{3,2},{4,5},{5,4},{6,7},{7,6},{8,9},{9,8},{10,11... | collective-permute-start | bytes 3145736 | tf_op jit(solution)/shard_map/ppermute | solution.py:279
  101.2 0.0 collective-permute-done.6.wb_ref
  101.3 4.8 %all-to-all-done.1.x_ref = bf16[32,8,128]{2,1,0:T(8,128)(2,1)S(1)} async-done(((bf16[32,8,128]{2,1,0:T(8,128)(2,1)}), bf16[32,8,128]{2,1,0:T(8,128)(2,1)S(1)}, u32[]{:S(2)}, u32[]{:S(2)}) %all-to-all-start.1) | async-done | bytes 65568 | tf_op jit(solution)/shard_map/all_to_all | solution.py:316
  106.1 2.7 %collective-permute-start.8 = (bf16[4,2,64,1024]{3,2,1,0:T(8,128)(2,1)S(1)}, bf16[4,2,64,1024]{3,2,1,0:T(8,128)(2,1)}, u32[]{:S(2)}, u32[]{:S(2)}) collective-permute-start(bf16[4,2,64,1024]{3,2,1,0:T(8,128)(2,1)S(1)} %collective-permute-done.6.wb_ref), channel_id=1, source_target_pairs={{0,1},{1,0},{2,3},{3,2},{4,5},{5,4},{6,7},{7,6},{8,9},{9,8},{10,11... | collective-permute-start | bytes 3145736 | tf_op jit(solution)/shard_map/ppermute | solution.py:320
  108.8 0.7 shard_map.179
  109.5 6.2 %all-to-all-start.2 = ((bf16[16,16,128]{2,1,0:T(8,128)(2,1)}), bf16[16,16,128]{2,1,0:T(8,128)(2,1)S(1)}, u32[]{:S(2)}, u32[]{:S(2)}) async-start(bf16[16,16,128]{2,1,0:T(8,128)(2,1)} %shard_map.179), calls=%async_computation.2 | async-start | bytes 131072 | tf_op jit(solution)/shard_map/all_to_all | solution.py:329
  115.8 0.0 collective-permute-done.7.wc_ref
  115.8 11.6 %all-to-all-done.2 = bf16[16,16,128]{2,1,0:T(8,128)(2,1)S(1)} async-done(((bf16[16,16,128]{2,1,0:T(8,128)(2,1)}), bf16[16,16,128]{2,1,0:T(8,128)(2,1)S(1)}, u32[]{:S(2)}, u32[]{:S(2)}) %all-to-all-start.2) | async-done | bytes 65568 | tf_op jit(solution)/shard_map/all_to_all | solution.py:329
  127.4 0.0 collective-permute-done.8.wd_ref
  127.4 0.0 copy-done.1
  127.4 0.0 copy-done.6
  127.4 0.0 copy-done.7
  127.4 0.7 copy-done.17
  128.1 0.0 copy-done.15
  128.1 1.0 copy-done.5
  129.1 0.9 copy-done.9
  130.1 8.2 %shard_map.180 = (bf16[512,1024]{1,0:T(8,128)(2,1)S(1)}, bf16[256,256]{1,0:T(8,128)(2,1)S(1)}) custom-call(s32[1,1]{1,0:T(1,128)} %bitcast.me_ref, bf16[512,1024]{1,0:T(8,128)(2,1)S(1)} %bitcast.21, bf16[512,64]{1,0:T(8,128)(2,1)S(1)} %copy-done.9, bf16[256,128]{1,0:T(8,128)(2,1)S(1)} %bitcast.24, s32[1,512]{1,0:T(1,128)S(1)} %bitcast.31, ...), custom_call_target="tpu_custom_call" | custom-call | tf_op jit(solution)/shard_map/pallas_call | solution.py:335
  138.2 0.0 copy-start.4
  138.2 10.8 %all_to_all.25.parts_ref = bf16[16,16,256]{2,1,0:T(8,128)(2,1)S(1)} all-to-all(bf16[16,16,256]{2,1,0:T(8,128)(2,1)S(1)} %bitcast.25), channel_id=1, replica_groups=mesh['src'=32,'tgt'=16] {'tgt'}, dimensions={0} | all-to-all | bytes 262144 | tf_op jit(solution)/shard_map/all_to_all | solution.py:362
  149.0 0.0 copy-done.10
  149.0 0.8 shard_map.181
  149.8 9.1 %all_to_all.26 = bf16[16,16,256]{2,1,0:T(8,128)(2,1)S(1)} all-to-all(bf16[16,16,256]{2,1,0:T(8,128)(2,1)S(1)} %get-tuple-element.16), channel_id=1, replica_groups=mesh['src'=32,'tgt'=16] {'tgt'}, dimensions={0} | all-to-all | bytes 262144 | tf_op jit(solution)/shard_map/all_to_all | solution.py:372
  158.9 0.0 copy-done.4
  158.9 1.9 %shard_map.182 = bf16[512,1024]{1,0:T(8,128)(2,1)} custom-call(bf16[512,1024]{1,0:T(8,128)(2,1)S(1)} %get-tuple-element.14.skip_ref, bf16[256,256]{1,0:T(8,128)(2,1)S(1)} %bitcast.23, s32[1,512]{1,0:T(1,128)S(1)} %bitcast.29, bf16[256,1024]{1,0:T(8,128)(2,1)S(1)} %copy-done.4), custom_call_target="tpu_custom_call" | custom-call | tf_op jit(solution)/shard_map/pallas_call | solution.py:373
  (13 shorter events, 0.0 us)
Async XLA Ops:
  0.6 1.2 copy-start
  1.9 0.9 copy-start.11
  4.3 18.4 %copy-start.12 = (bf16[64,1024]{1,0:T(8,128)(2,1)S(1)}, bf16[64,1024]{1,0:T(8,128)(2,1)}, u32[]{:S(2)}) copy-start(bf16[64,1024]{1,0:T(8,128)(2,1)} %a_ref.1) | copy-start | bytes 393220
  4.3 18.4 %copy-start.13 = (bf16[64,1024]{1,0:T(8,128)(2,1)S(1)}, bf16[64,1024]{1,0:T(8,128)(2,1)}, u32[]{:S(2)}) copy-start(bf16[64,1024]{1,0:T(8,128)(2,1)} %b_ref.1) | copy-start | bytes 393220
  4.3 47.7 %all-to-all-start = ((bf16[8,256,128]{2,1,0:T(8,128)(2,1)}), bf16[8,256,128]{2,1,0:T(8,128)(2,1)S(1)}, u32[]{:S(2)}, u32[]{:S(2)}) async-start(bf16[8,256,128]{2,1,0:T(8,128)(2,1)} %shard_map.176.after_ref), calls=%async_computation | async-start | bytes 1048576 | tf_op jit(solution)/shard_map/all_to_all | solution.py:262
  22.8 35.1 %collective-permute-start.5 = (bf16[2,64,1024]{2,1,0:T(8,128)(2,1)S(1)}, bf16[2,64,1024]{2,1,0:T(8,128)(2,1)S(1)}, u32[]{:S(2)}, u32[]{:S(2)}) collective-permute-start(bf16[2,64,1024]{2,1,0:T(8,128)(2,1)S(1)} %shard_map.178), channel_id=1, source_target_pairs={{0,4},{1,5},{2,6},{3,7},{4,8},{5,9},{6,10},{7,11},{8,12},{9,13},{1... | collective-permute-start | bytes 786440 | tf_op jit(solution)/shard_map/ppermute | solution.py:272
  25.9 37.2 %collective-permute-start.4 = (bf16[2,64,1024]{2,1,0:T(8,128)(2,1)S(1)}, bf16[2,64,1024]{2,1,0:T(8,128)(2,1)S(1)}, u32[]{:S(2)}, u32[]{:S(2)}) collective-permute-start(bf16[2,64,1024]{2,1,0:T(8,128)(2,1)S(1)} %shard_map.178), channel_id=1, source_target_pairs={{0,8},{1,9},{2,10},{3,11},{4,12},{5,13},{6,14},{7,15},{8,0},{9,1},... | collective-permute-start | bytes 786440 | tf_op jit(solution)/shard_map/ppermute | solution.py:272
  30.3 32.8 %collective-permute-start.3 = (bf16[2,64,1024]{2,1,0:T(8,128)(2,1)S(1)}, bf16[2,64,1024]{2,1,0:T(8,128)(2,1)S(1)}, u32[]{:S(2)}, u32[]{:S(2)}) collective-permute-start(bf16[2,64,1024]{2,1,0:T(8,128)(2,1)S(1)} %shard_map.178), channel_id=1, source_target_pairs={{0,12},{1,13},{2,14},{3,15},{4,0},{5,1},{6,2},{7,3},{8,4},{9,5},{1... | collective-permute-start | bytes 786440 | tf_op jit(solution)/shard_map/ppermute | solution.py:272
  33.3 29.0 %copy-start.14 = (s32[1,1,4096]{2,1,0:T(1,128)S(1)}, s32[1,1,4096]{2,1,0:T(1,128)}, u32[]{:S(2)}) copy-start(s32[1,1,4096]{2,1,0:T(1,128)} %param.20) | copy-start | bytes 49156
  52.0 11.3 %copy-start.2 = (bf16[8,256,128]{2,1,0:T(8,128)(2,1)}, bf16[8,256,128]{2,1,0:T(8,128)(2,1)S(1)}, u32[]{:S(2)}) copy-start(bf16[8,256,128]{2,1,0:T(8,128)(2,1)S(1)} %all-to-all-done.b0) | copy-start | bytes 1572868
  52.0 15.2 %collective-permute-start.2 = (bf16[8,256,128]{2,1,0:T(8,128)(2,1)S(1)}, bf16[8,256,128]{2,1,0:T(8,128)(2,1)S(1)}, u32[]{:S(2)}, u32[]{:S(2)}) collective-permute-start(bf16[8,256,128]{2,1,0:T(8,128)(2,1)S(1)} %all-to-all-done.b0), channel_id=1, source_target_pairs={{0,32},{16,48},{32,64},{48,80},{64,96},{80,112},{96,128},{112,144}... | collective-permute-start | bytes 1572872 | tf_op jit(solution)/shard_map/ppermute | solution.py:274
  54.9 24.4 %collective-permute-start.1 = (bf16[8,256,128]{2,1,0:T(8,128)(2,1)S(1)}, bf16[8,256,128]{2,1,0:T(8,128)(2,1)S(1)}, u32[]{:S(2)}, u32[]{:S(2)}) collective-permute-start(bf16[8,256,128]{2,1,0:T(8,128)(2,1)S(1)} %all-to-all-done.b0), channel_id=1, source_target_pairs={{0,64},{16,80},{32,480},{48,496},{64,128},{80,144},{96,32},{112,48... | collective-permute-start | bytes 1572872 | tf_op jit(solution)/shard_map/ppermute | solution.py:275
  57.9 25.9 %collective-permute-start = (bf16[8,256,128]{2,1,0:T(8,128)(2,1)S(1)}, bf16[8,256,128]{2,1,0:T(8,128)(2,1)S(1)}, u32[]{:S(2)}, u32[]{:S(2)}) collective-permute-start(bf16[8,256,128]{2,1,0:T(8,128)(2,1)S(1)} %all-to-all-done.b0), channel_id=1, source_target_pairs={{0,480},{16,496},{32,0},{48,16},{64,32},{80,48},{96,64},{112,80},{... | collective-permute-start | bytes 1572872 | tf_op jit(solution)/shard_map/ppermute | solution.py:273
  63.1 20.7 %copy-start.18 = (bf16[1,1,16,4096]{3,2,1,0:T(8,128)(2,1)S(1)}, bf16[1,1,16,4096]{3,2,1,0:T(8,128)(2,1)}, u32[]{:S(2)}) copy-start(bf16[1,1,16,4096]{3,2,1,0:T(8,128)(2,1)} %param.23) | copy-start | bytes 393220
  63.1 20.6 %copy-start.19 = (bf16[1024,64]{0,1:T(8,128)(2,1)S(1)}, bf16[1024,64]{0,1:T(8,128)(2,1)}, u32[]{:S(2)}) copy-start(bf16[1024,64]{0,1:T(8,128)(2,1)} %param.26) | copy-start | bytes 393220
  63.1 20.6 %copy-start.20 = (s32[1,1,4096]{2,1,0:T(1,128)S(1)}, s32[1,1,4096]{2,1,0:T(1,128)}, u32[]{:S(2)}) copy-start(s32[1,1,4096]{2,1,0:T(1,128)} %param.21) | copy-start | bytes 49156
  63.3 38.0 %collective-permute-start.6 = (bf16[4,2,64,1024]{3,2,1,0:T(8,128)(2,1)S(1)}, bf16[4,2,64,1024]{3,2,1,0:T(8,128)(2,1)S(1)}, u32[]{:S(2)}, u32[]{:S(2)}) collective-permute-start(bf16[4,2,64,1024]{3,2,1,0:T(8,128)(2,1)S(1)} %pad_maximum_fusion.wa_ref), channel_id=1, source_target_pairs={{0,2},{1,3},{2,0},{3,1},{4,6},{5,7},{6,4},{7,5},{8,10},{9,11},{10,... | collective-permute-start | bytes 3145736 | tf_op jit(solution)/shard_map/ppermute | solution.py:278
  83.8 1.0 copy-start.3
  84.8 42.6 %copy-start.1 = (bf16[1,1,512,1024]{3,2,1,0:T(8,128)(2,1)S(1)}, bf16[1,1,512,1024]{3,2,1,0:T(8,128)(2,1)}, u32[]{:S(2)}) copy-start(bf16[1,1,512,1024]{3,2,1,0:T(8,128)(2,1)} %param.17) | copy-start | bytes 3145732
  91.9 0.7 copy-start.8
  92.6 13.5 %all-to-all-start.1 = ((bf16[32,8,128]{2,1,0:T(8,128)(2,1)}), bf16[32,8,128]{2,1,0:T(8,128)(2,1)S(1)}, u32[]{:S(2)}, u32[]{:S(2)}) async-start(bf16[32,8,128]{2,1,0:T(8,128)(2,1)} %get-tuple-element.11), calls=%async_computation.1 | async-start | bytes 131072 | tf_op jit(solution)/shard_map/all_to_all | solution.py:316
  98.9 28.5 %copy-start.6 = (bf16[64,1024]{1,0:T(8,128)(2,1)S(1)}, bf16[64,1024]{1,0:T(8,128)(2,1)}, u32[]{:S(2)}) copy-start(bf16[64,1024]{1,0:T(8,128)(2,1)} %upf_ref.1) | copy-start | bytes 393220
  98.9 28.5 %copy-start.7 = (bf16[64,1024]{1,0:T(8,128)(2,1)S(1)}, bf16[64,1024]{1,0:T(8,128)(2,1)}, u32[]{:S(2)}) copy-start(bf16[64,1024]{1,0:T(8,128)(2,1)} %upr_ref.1) | copy-start | bytes 393220
  99.0 16.8 %collective-permute-start.7 = (bf16[4,2,64,1024]{3,2,1,0:T(8,128)(2,1)S(1)}, bf16[4,2,64,1024]{3,2,1,0:T(8,128)(2,1)}, u32[]{:S(2)}, u32[]{:S(2)}) collective-permute-start(bf16[4,2,64,1024]{3,2,1,0:T(8,128)(2,1)S(1)} %pad_maximum_fusion.wa_ref), channel_id=1, source_target_pairs={{0,1},{1,0},{2,3},{3,2},{4,5},{5,4},{6,7},{7,6},{8,9},{9,8},{10,11... | collective-permute-start | bytes 3145736 | tf_op jit(solution)/shard_map/ppermute | solution.py:279
  106.1 21.3 %collective-permute-start.8 = (bf16[4,2,64,1024]{3,2,1,0:T(8,128)(2,1)S(1)}, bf16[4,2,64,1024]{3,2,1,0:T(8,128)(2,1)}, u32[]{:S(2)}, u32[]{:S(2)}) collective-permute-start(bf16[4,2,64,1024]{3,2,1,0:T(8,128)(2,1)S(1)} %collective-permute-done.6.wb_ref), channel_id=1, source_target_pairs={{0,1},{1,0},{2,3},{3,2},{4,5},{5,4},{6,7},{7,6},{8,9},{9,8},{10,11... | collective-permute-start | bytes 3145736 | tf_op jit(solution)/shard_map/ppermute | solution.py:320
  109.5 17.9 %all-to-all-start.2 = ((bf16[16,16,128]{2,1,0:T(8,128)(2,1)}), bf16[16,16,128]{2,1,0:T(8,128)(2,1)S(1)}, u32[]{:S(2)}, u32[]{:S(2)}) async-start(bf16[16,16,128]{2,1,0:T(8,128)(2,1)} %shard_map.179), calls=%async_computation.2 | async-start | bytes 131072 | tf_op jit(solution)/shard_map/all_to_all | solution.py:329
  127.4 0.7 copy-start.17
  127.4 0.7 copy-start.15
  128.1 1.0 copy-start.5
  129.1 0.9 copy-start.9
  130.0 19.0 %copy-start.10 = (bf16[256,256]{1,0:T(8,128)(2,1)S(1)}, bf16[256,256]{1,0:T(8,128)(2,1)}, u32[]{:S(2)}) copy-start(bf16[256,256]{1,0:T(8,128)(2,1)} %w_ref.1) | copy-start | bytes 393220
  130.1 19.0 %copy-start.16 = (bf16[1,16,256]{2,1,0:T(8,128)(2,1)S(1)}, bf16[1,16,256]{2,1,0:T(8,128)(2,1)}, u32[]{:S(2)}) copy-start(bf16[1,16,256]{2,1,0:T(8,128)(2,1)} %param.18) | copy-start | bytes 24580
  138.2 20.7 %copy-start.4 = (bf16[256,1024]{1,0:T(8,128)(2,1)S(1)}, bf16[256,1024]{1,0:T(8,128)(2,1)}, u32[]{:S(2)}) copy-start(bf16[256,1024]{1,0:T(8,128)(2,1)} %back_ref.1) | copy-start | bytes 1572868

commit v4 on v3

--- a/solution.py
+++ b/solution.py
@@ -29,7 +29,7 @@
     return lax.dot_general(a, b, (((ca,), (cb,)), ((), ())), preferred_element_type=F32)
 
 
-def params(mb=48):
+def params(mb):
     return pltpu.CompilerParams(vmem_limit_bytes=mb * 1024 * 1024)
 
 
@@ -127,8 +127,13 @@
         o_ref[half + j] = jnp.concatenate([first[:, width:], second[:, width:]], axis=1).astype(BF16)
 
 
+def forward_kernel(x_ref, tm_ref, upf_ref, o_ref):
+    forward_out = silu(dot(tm_ref[...], upf_ref[...])).astype(BF16)
+    o_ref[...] = x_ref[...].astype(F32) + forward_out.astype(F32)
+
+
 def edge_kernel(
-    me_ref, x_ref, tm_ref, got_ref, perm_ref, src_ref, upf_ref, upr_ref, proj_ref,
+    me_ref, x_ref, got_ref, perm_ref, src_ref, upr_ref, proj_ref,
     wa_ref, wb_ref, wc_ref, wd_ref, skip_ref, part_ref, w1, w2, sems,
 ):
     me = me_ref[0, 0]
@@ -146,7 +151,7 @@
     for load in loads[0] + loads[1]:
         load.start()
     edges = x_ref.shape[0]
-    width = tm_ref.shape[1]
+    width = got_ref.shape[1] // 2
     got = got_ref[...]
     got = jnp.concatenate([got[:, :width], got[:, width:]], axis=0)
     perm = perm_ref[...]
@@ -155,11 +160,8 @@
         lax.broadcasted_iota(jnp.int32, (edges, edges), 0) == row, 1.0, 0.0
     ).astype(BF16)
     mirror_msg = dot(hot, got, 0, 0).astype(BF16)
-    forward_out = silu(dot(tm_ref[...], upf_ref[...])).astype(BF16)
     mirrored = silu(dot(mirror_msg, upr_ref[...])).astype(BF16)
-    mixed = (
-        (x_ref[...].astype(F32) + forward_out.astype(F32) + mirrored.astype(F32)) * INV_THREE
-    ).astype(BF16)
+    mixed = ((x_ref[...] + mirrored.astype(F32)) * INV_THREE).astype(BF16)
     for load in loads[0]:
         load.wait()
     inner = silu(dot(mixed, w1[...])).astype(BF16)
@@ -253,7 +255,7 @@
             pltpu.VMEM((width, wide), BF16),
             pltpu.SemaphoreType.DMA((2,)),
         ],
-        compiler_params=params(),
+        compiler_params=params(60),
     )(rows, down_proj.T)
 
     groups = [
@@ -267,7 +269,7 @@
         out_shape=struct((2,) + res_first.shape),
         in_specs=[HB, VM, VM],
         out_specs=VM,
-        compiler_params=params(),
+        compiler_params=params(4),
     )(far, res_first, res_second)
     x_w = [own_w] + [lax.ppermute(own_w, "tgt", along_x(d)) for d in (-1, 2, 1)]
     from_next = lax.ppermute(near, "src", shift(-1))
@@ -276,7 +278,6 @@
 
     x_w = jnp.stack(x_w)
     y_w = lax.ppermute(x_w, "tgt", across(2))
-    cx_w = lax.ppermute(x_w, "tgt", across(1))
 
     my_z = lax.axis_index("src") // YH
     ids = trip_source[0]
@@ -296,7 +297,7 @@
             pltpu.VMEM((edges, 2 * width), F32),
             pltpu.VMEM((2 * width, edges), F32),
         ],
-        compiler_params=params(),
+        compiler_params=params(24),
         cost_estimate=pl.CostEstimate(flops=10**11, bytes_accessed=10**7, transcendentals=0),
     )(
         pos,
@@ -316,41 +317,48 @@
     got = lax.all_to_all(
         send, ("src", "tgt"), split_axis=0, concat_axis=0, tiled=True, axis_index_groups=plane
     )
-    got, y_w = lax.optimization_barrier((got, y_w))
-    cy_w = lax.ppermute(y_w, "tgt", across(1))
     turned = pl.pallas_call(
         turn_kernel,
         out_shape=struct((Z, NEAR // 2, 2 * width)),
         in_specs=[VM],
         out_specs=VM,
         scratch_shapes=[pltpu.VMEM((NEAR * Z // 2, 2 * width), F32)],
-        compiler_params=params(),
+        compiler_params=params(4),
     )(got)
+    turned, x_w, y_w = lax.optimization_barrier((turned, x_w, y_w))
+    cx_w = lax.ppermute(x_w, "tgt", across(1))
+    cy_w = lax.ppermute(y_w, "tgt", across(1))
     arrived = lax.all_to_all(
         turned, "src", split_axis=0, concat_axis=0, tiled=True, axis_index_groups=lines
     )
 
     atoms = atom_state.shape[1] * NT
     da = atom_state.shape[2]
+    base = pl.pallas_call(
+        forward_kernel,
+        out_shape=struct((edges, wide), F32),
+        in_specs=[VM] * 3,
+        out_specs=VM,
+        compiler_params=params(12),
+        cost_estimate=pl.CostEstimate(flops=10**11, bytes_accessed=10**6, transcendentals=0),
+    )(rows, tm, up_forward)
     skipped, part = pl.pallas_call(
         edge_kernel,
         out_shape=(struct((edges, wide)), struct((atoms, da))),
-        in_specs=[SM] + [VM] * 8 + [HB] * 4,
+        in_specs=[SM] + [VM] * 6 + [HB] * 4,
         out_specs=(VM, VM),
         scratch_shapes=[
             pltpu.VMEM((wide, wide), BF16),
             pltpu.VMEM((wide, wide), BF16),
             pltpu.SemaphoreType.DMA((2, NT)),
         ],
-        compiler_params=params(),
+        compiler_params=params(20),
     )(
         lax.axis_index("tgt").astype(jnp.int32).reshape(1, 1),
-        rows,
-        tm,
+        base,
         arrived.reshape(edges // 2, 2 * width),
         reverse_perm[0],
         edge_source[0],
-        up_forward,
         up_reverse,
         atom_proj,
         x_w,
@@ -367,7 +375,7 @@
         out_shape=(struct((atoms // NT, da)), struct((NT, atoms // NT, da))),
         in_specs=[VM] * 3,
         out_specs=(VM, VM),
-        compiler_params=params(),
+        compiler_params=params(4),
     )(parts, atom_state[0], atom_self)
     block = lax.all_to_all(spread, "tgt", split_axis=0, concat_axis=0, tiled=True)
     edge_new = pl.pallas_call(
@@ -375,7 +383,7 @@
         out_shape=struct((edges, wide)),
         in_specs=[VM] * 4,
         out_specs=VM,
-        compiler_params=params(),
+        compiler_params=params(8),
     )(skipped, block.reshape(atoms, da), edge_source[0], atom_back)
     return (edge_new[None, None], atom_new[None])
 

time: 162 us -> 153 us (0.944)
  waiting for transfers between devices: 53.3 us -> 46.6 us
    all_to_all x1, waiting for transfers between devices: 11.6 us -> 3.74 us  [local(): lax.all_to_all(turned, 'src', split_axis=0, concat_axis=0, tiled=True, ax...]
    all_to_all x1, waiting for transfers between devices: 4.82 us -> 7.14 us  [local(): lax.all_to_all(send, ('src', 'tgt'), split_axis=0, concat_axis=0, tiled=T...]
    pallas_call x1, Pallas kernels: 8.16 us -> 6.38 us  [local(): pl.pallas_call(edge_kernel, out_shape=(struct((edges, wide)), struct((ato...]
    unnamed x42 -> x36, local copies, waits for them, and re-layouts: 6.5 us -> 4.92 us
  transfers between devices with their start and end apart: 12 -> 12, of which waited for: 6 -> 6; matrix products, arithmetic and copies ran while one was open for 0% -> 0% of each run, Pallas kernels for 5% -> 6%
where the time goes in v4:
time: 153 us
  starting transfers between devices  59.2 us (39%)
  waiting for transfers between devices  46.6 us (30%)
  Pallas kernels  20.3 us (13%)
  blocking collectives  19.9 us (13%)
  local copies, waits for them, and re-layouts  4.92 us (3%)
  between operations  1.59 us (1%)
    all_to_all x1, starting transfers between devices, local(): lax.all_to_all(far, 'src', split_axis=0, concat_axis=0, tiled=True, axis_...  18.4 us
    all_to_all x1, waiting for transfers between devices, local(): lax.all_to_all(far, 'src', split_axis=0, concat_axis=0, tiled=True, axis_...  17.6 us
    ppermute x1, waiting for transfers between devices, local(): from_two = lax.ppermute(near, 'src', shift_two())  12.1 us
    all_to_all x1, blocking collectives, local(): lax.all_to_all(part.reshape(NT, atoms // NT, da), 'tgt', split_axis=0, co...  10.9 us
    ppermute x3, starting transfers between devices, local(): x_w = [own_w] + [lax.ppermute(own_w, 'tgt', along_x(d)) for d in (-1, 2, 1)]  10.5 us
    all_to_all x1, blocking collectives, local(): lax.all_to_all(spread, 'tgt', split_axis=0, concat_axis=0, tiled=True)  9.06 us
    pallas_call x1, Pallas kernels, local(): pl.pallas_call(contract_kernel, out_shape=(struct((edges, width)), struct...  7.16 us
    all_to_all x1, waiting for transfers between devices, local(): lax.all_to_all(send, ('src', 'tgt'), split_axis=0, concat_axis=0, tiled=T...  7.14 us
  transfers between devices with their start and end apart: 12, of which 6 were waited for; matrix products, arithmetic and copies ran while one was open for 0% of the time, Pallas kernels for 6%

profile of v4, /device:TPU:1, one launch (start us, length us, event | category | flops | bytes accessed | tf_op | source)
XLA Modules:
  0.0 152.7 jit_solution(18078574339455247877)
XLA Ops:
  0.6 0.0 copy-start.7
  0.6 0.0 copy-start.6
  0.7 0.0 copy-start.8
  0.7 2.6 %shard_map.176.after_ref = bf16[8,256,128]{2,1,0:T(8,128)(2,1)} custom-call(bf16[512,1024]{1,0:T(8,128)(2,1)} %bitcast.20, bf16[64,1024]{1,0:T(8,128)(2,1)} %bitcast.38), custom_call_target="tpu_custom_call" | custom-call | tf_op jit(solution)/shard_map/pallas_call | solution.py:248
  3.3 0.0 copy-start.12
  3.3 0.0 copy-start.13
  3.3 0.0 copy-start.15
  3.4 18.4 %all-to-all-start = ((bf16[8,256,128]{2,1,0:T(8,128)(2,1)}), bf16[8,256,128]{2,1,0:T(8,128)(2,1)S(1)}, u32[]{:S(2)}, u32[]{:S(2)}) async-start(bf16[8,256,128]{2,1,0:T(8,128)(2,1)} %shard_map.176.after_ref), calls=%async_computation | async-start | bytes 1048576 | tf_op jit(solution)/shard_map/all_to_all | solution.py:264
  21.8 0.0 copy-done.7
  21.8 0.0 copy-done.6
  21.8 0.0 copy-start
  21.8 1.0 copy-done
  22.9 3.1 %collective-permute-start.5 = (bf16[2,64,1024]{2,1,0:T(8,128)(2,1)S(1)}, bf16[2,64,1024]{2,1,0:T(8,128)(2,1)S(1)}, u32[]{:S(2)}, u32[]{:S(2)}) collective-permute-start(bf16[2,64,1024]{2,1,0:T(8,128)(2,1)S(1)} %shard_map.180), channel_id=1, source_target_pairs={{0,4},{1,5},{2,6},{3,7},{4,8},{5,9},{6,10},{7,11},{8,12},{9,13},{1... | collective-permute-start | bytes 786440 | tf_op jit(solution)/shard_map/ppermute | solution.py:274
  26.0 4.4 %collective-permute-start.4 = (bf16[2,64,1024]{2,1,0:T(8,128)(2,1)S(1)}, bf16[2,64,1024]{2,1,0:T(8,128)(2,1)S(1)}, u32[]{:S(2)}, u32[]{:S(2)}) collective-permute-start(bf16[2,64,1024]{2,1,0:T(8,128)(2,1)S(1)} %shard_map.180), channel_id=1, source_target_pairs={{0,8},{1,9},{2,10},{3,11},{4,12},{5,13},{6,14},{7,15},{8,0},{9,1},... | collective-permute-start | bytes 786440 | tf_op jit(solution)/shard_map/ppermute | solution.py:274
  30.4 3.1 %collective-permute-start.3 = (bf16[2,64,1024]{2,1,0:T(8,128)(2,1)S(1)}, bf16[2,64,1024]{2,1,0:T(8,128)(2,1)S(1)}, u32[]{:S(2)}, u32[]{:S(2)}) collective-permute-start(bf16[2,64,1024]{2,1,0:T(8,128)(2,1)S(1)} %shard_map.180), channel_id=1, source_target_pairs={{0,12},{1,13},{2,14},{3,15},{4,0},{5,1},{6,2},{7,3},{8,4},{9,5},{1... | collective-permute-start | bytes 786440 | tf_op jit(solution)/shard_map/ppermute | solution.py:274
  33.4 17.6 %all-to-all-done.b0 = bf16[8,256,128]{2,1,0:T(8,128)(2,1)S(1)} async-done(((bf16[8,256,128]{2,1,0:T(8,128)(2,1)}), bf16[8,256,128]{2,1,0:T(8,128)(2,1)S(1)}, u32[]{:S(2)}, u32[]{:S(2)}) %all-to-all-start) | async-done | bytes 524320 | tf_op jit(solution)/shard_map/all_to_all | solution.py:264
  51.0 2.9 %collective-permute-start.2 = (bf16[8,256,128]{2,1,0:T(8,128)(2,1)S(1)}, bf16[8,256,128]{2,1,0:T(8,128)(2,1)S(1)}, u32[]{:S(2)}, u32[]{:S(2)}) collective-permute-start(bf16[8,256,128]{2,1,0:T(8,128)(2,1)S(1)} %all-to-all-done.b0), channel_id=1, source_target_pairs={{0,32},{16,48},{32,64},{48,80},{64,96},{80,112},{96,128},{112,144}... | collective-permute-start | bytes 1572872 | tf_op jit(solution)/shard_map/ppermute | solution.py:276
  54.0 2.9 %collective-permute-start.1 = (bf16[8,256,128]{2,1,0:T(8,128)(2,1)S(1)}, bf16[8,256,128]{2,1,0:T(8,128)(2,1)S(1)}, u32[]{:S(2)}, u32[]{:S(2)}) collective-permute-start(bf16[8,256,128]{2,1,0:T(8,128)(2,1)S(1)} %all-to-all-done.b0), channel_id=1, source_target_pairs={{0,64},{16,80},{32,480},{48,496},{64,128},{80,144},{96,32},{112,48... | collective-permute-start | bytes 1572872 | tf_op jit(solution)/shard_map/ppermute | solution.py:277
  56.9 0.0 collective-permute-done.5
  56.9 4.5 %collective-permute-start = (bf16[8,256,128]{2,1,0:T(8,128)(2,1)S(1)}, bf16[8,256,128]{2,1,0:T(8,128)(2,1)S(1)}, u32[]{:S(2)}, u32[]{:S(2)}) collective-permute-start(bf16[8,256,128]{2,1,0:T(8,128)(2,1)S(1)} %all-to-all-done.b0), channel_id=1, source_target_pairs={{0,480},{16,496},{32,0},{48,16},{64,32},{80,48},{96,64},{112,80},{... | collective-permute-start | bytes 1572872 | tf_op jit(solution)/shard_map/ppermute | solution.py:275
  61.4 0.0 copy-done.8
  61.4 0.1 and_add_fusion.pos_ref
  62.1 0.0 collective-permute-done.4
  62.1 0.0 collective-permute-done.3
  62.1 0.1 pad_maximum_fusion.wa_ref
  62.3 2.3 %collective-permute-start.6 = (bf16[4,2,64,1024]{3,2,1,0:T(8,128)(2,1)S(1)}, bf16[4,2,64,1024]{3,2,1,0:T(8,128)(2,1)}, u32[]{:S(2)}, u32[]{:S(2)}) collective-permute-start(bf16[4,2,64,1024]{3,2,1,0:T(8,128)(2,1)S(1)} %pad_maximum_fusion.wa_ref), channel_id=1, source_target_pairs={{0,2},{1,3},{2,0},{3,1},{4,6},{5,7},{6,4},{7,5},{8,10},{9,11},{10,... | collective-permute-start | bytes 3145736 | tf_op jit(solution)/shard_map/ppermute | solution.py:280
  64.6 1.5 collective-permute-done.2.b3
  66.1 12.1 %collective-permute-done.1.b2 = bf16[8,256,128]{2,1,0:T(8,128)(2,1)S(1)} collective-permute-done((bf16[8,256,128]{2,1,0:T(8,128)(2,1)S(1)}, bf16[8,256,128]{2,1,0:T(8,128)(2,1)S(1)}, u32[]{:S(2)}, u32[]{:S(2)}) %collective-permute-start.1) | collective-permute-done | bytes 524320 | tf_op jit(solution)/shard_map/ppermute | solution.py:277
  78.2 4.5 %collective-permute-done.b1 = bf16[8,256,128]{2,1,0:T(8,128)(2,1)S(1)} collective-permute-done((bf16[8,256,128]{2,1,0:T(8,128)(2,1)S(1)}, bf16[8,256,128]{2,1,0:T(8,128)(2,1)S(1)}, u32[]{:S(2)}, u32[]{:S(2)}) %collective-permute-start) | collective-permute-done | bytes 524320 | tf_op jit(solution)/shard_map/ppermute | solution.py:275
  82.7 0.0 copy-done.12
  82.7 0.0 copy-done.13
  82.7 0.0 copy-done.15
  82.7 0.0 copy-start.14
  82.7 7.2 %shard_map.177 = (bf16[512,64]{1,0:T(8,128)(2,1)S(1)}, bf16[32,8,128]{2,1,0:T(8,128)(2,1)}) custom-call(s32[1,4096]{1,0:T(1,128)S(1)} %and_add_fusion.pos_ref, s32[1,1]{1,0:T(1,128)S(6)} %copy.19.cnt_ref, s32[1,4096]{1,0:T(1,128)S(1)} %bitcast.26, s32[1,4096]{1,0:T(1,128)S(1)} %bitcast.33, bf16[16,4096]{1,0:T(8,128)(2,1)S(1)} %bitcast.31, ...), custom_call_target="tpu_custom_call" | custom-call | flops 99999997952 | bytes 10000000 | tf_op jit(solution)/shard_map/pallas_call | solution.py:288
  89.8 0.0 copy-start.16
  89.8 0.7 copy-done.16
  90.5 6.5 %all-to-all-start.1 = ((bf16[32,8,128]{2,1,0:T(8,128)(2,1)}), bf16[32,8,128]{2,1,0:T(8,128)(2,1)S(1)}, u32[]{:S(2)}, u32[]{:S(2)}) async-start(bf16[32,8,128]{2,1,0:T(8,128)(2,1)} %get-tuple-element.12), calls=%async_computation.1 | async-start | bytes 131072 | tf_op jit(solution)/shard_map/all_to_all | solution.py:317
  97.0 7.1 %all-to-all-done.1.x_ref = bf16[32,8,128]{2,1,0:T(8,128)(2,1)S(1)} async-done(((bf16[32,8,128]{2,1,0:T(8,128)(2,1)}), bf16[32,8,128]{2,1,0:T(8,128)(2,1)S(1)}, u32[]{:S(2)}, u32[]{:S(2)}) %all-to-all-start.1) | async-done | bytes 65568 | tf_op jit(solution)/shard_map/all_to_all | solution.py:317
  104.1 0.7 shard_map.179
  104.8 0.0 collective-permute-done.6.wb_ref
  104.8 6.2 %all-to-all-start.2 = ((bf16[16,16,128]{2,1,0:T(8,128)(2,1)}), bf16[16,16,128]{2,1,0:T(8,128)(2,1)S(1)}, u32[]{:S(2)}, u32[]{:S(2)}) async-start(bf16[16,16,128]{2,1,0:T(8,128)(2,1)} %shard_map.179), calls=%async_computation.2 | async-start | bytes 131072 | tf_op jit(solution)/shard_map/all_to_all | solution.py:331
  111.0 3.0 %collective-permute-start.7 = (bf16[4,2,64,1024]{3,2,1,0:T(8,128)(2,1)S(1)}, bf16[4,2,64,1024]{3,2,1,0:T(8,128)(2,1)}, u32[]{:S(2)}, u32[]{:S(2)}) collective-permute-start(bf16[4,2,64,1024]{3,2,1,0:T(8,128)(2,1)S(1)} %pad_maximum_fusion.wa_ref), channel_id=1, source_target_pairs={{0,1},{1,0},{2,3},{3,2},{4,5},{5,4},{6,7},{7,6},{8,9},{9,8},{10,11... | collective-permute-start | bytes 3145736 | tf_op jit(solution)/shard_map/ppermute | solution.py:329
  114.0 1.9 %collective-permute-start.8 = (bf16[4,2,64,1024]{3,2,1,0:T(8,128)(2,1)}, bf16[4,2,64,1024]{3,2,1,0:T(8,128)(2,1)}, u32[]{:S(2)}, u32[]{:S(2)}) collective-permute-start(bf16[4,2,64,1024]{3,2,1,0:T(8,128)(2,1)} %collective-permute-done.6.wb_ref), channel_id=1, source_target_pairs={{0,1},{1,0},{2,3},{3,2},{4,5},{5,4},{6,7},{7,6},{8,9},{9,8},{10,11... | collective-permute-start | bytes 3145736 | tf_op jit(solution)/shard_map/ppermute | solution.py:330
  116.0 0.0 copy-done.14
  116.0 0.0 copy-start.1
  116.0 1.2 copy-done.1
  117.2 0.9 copy-done.17
  118.1 0.8 shard_map.178.x_ref
  118.9 3.7 %all-to-all-done.2 = bf16[16,16,128]{2,1,0:T(8,128)(2,1)S(1)} async-done(((bf16[16,16,128]{2,1,0:T(8,128)(2,1)}), bf16[16,16,128]{2,1,0:T(8,128)(2,1)S(1)}, u32[]{:S(2)}, u32[]{:S(2)}) %all-to-all-start.2) | async-done | bytes 65568 | tf_op jit(solution)/shard_map/all_to_all | solution.py:331
  122.6 0.0 collective-permute-done.7.wc_ref
  122.6 0.0 collective-permute-done.8.wd_ref
  122.6 0.0 copy-done.4
  122.6 0.0 copy-done.9
  122.7 0.0 copy-done.11
  122.7 0.0 copy-start.2
  122.7 1.0 copy-done.2
  123.7 6.4 %shard_map.181 = (bf16[512,1024]{1,0:T(8,128)(2,1)S(1)}, bf16[256,256]{1,0:T(8,128)(2,1)S(1)}) custom-call(s32[1,1]{1,0:T(1,128)} %bitcast.me_ref, f32[512,1024]{1,0:T(8,128)S(1)} %shard_map.178.x_ref, bf16[256,128]{1,0:T(8,128)(2,1)S(1)} %bitcast.24, s32[1,512]{1,0:T(1,128)S(1)} %bitcast.30, s32[1,512]{1,0:T(1,128)S(1)} %bitcast.27, ...), custom_call_target="tpu_custom_call" | custom-call | tf_op jit(solution)/shard_map/pallas_call | solution.py:345
  130.1 10.9 %all_to_all.25.parts_ref = bf16[16,16,256]{2,1,0:T(8,128)(2,1)S(1)} all-to-all(bf16[16,16,256]{2,1,0:T(8,128)(2,1)S(1)} %bitcast.25), channel_id=1, replica_groups=mesh['src'=32,'tgt'=16] {'tgt'}, dimensions={0} | all-to-all | bytes 262144 | tf_op jit(solution)/shard_map/all_to_all | solution.py:370
  141.0 0.0 copy-done.5
  141.0 0.0 copy-done.10
  141.0 0.8 shard_map.182
  141.7 9.1 %all_to_all.26 = bf16[16,16,256]{2,1,0:T(8,128)(2,1)S(1)} all-to-all(bf16[16,16,256]{2,1,0:T(8,128)(2,1)S(1)} %get-tuple-element.18), channel_id=1, replica_groups=mesh['src'=32,'tgt'=16] {'tgt'}, dimensions={0} | all-to-all | bytes 262144 | tf_op jit(solution)/shard_map/all_to_all | solution.py:380
  150.8 0.0 copy-done.3
  150.8 1.8 %shard_map.183 = bf16[512,1024]{1,0:T(8,128)(2,1)} custom-call(bf16[512,1024]{1,0:T(8,128)(2,1)S(1)} %get-tuple-element.16.skip_ref, bf16[256,256]{1,0:T(8,128)(2,1)S(1)} %bitcast.23, s32[1,512]{1,0:T(1,128)S(1)} %bitcast.28, bf16[256,1024]{1,0:T(8,128)(2,1)S(1)} %copy-done.3), custom_call_target="tpu_custom_call" | custom-call | tf_op jit(solution)/shard_map/pallas_call | solution.py:381
  (8 shorter events, 0.0 us)
Async XLA Ops:
  0.6 21.1 %copy-start.7 = (bf16[64,1024]{1,0:T(8,128)(2,1)S(1)}, bf16[64,1024]{1,0:T(8,128)(2,1)}, u32[]{:S(2)}) copy-start(bf16[64,1024]{1,0:T(8,128)(2,1)} %b_ref.1) | copy-start | bytes 393220
  0.6 21.1 %copy-start.6 = (bf16[64,1024]{1,0:T(8,128)(2,1)S(1)}, bf16[64,1024]{1,0:T(8,128)(2,1)}, u32[]{:S(2)}) copy-start(bf16[64,1024]{1,0:T(8,128)(2,1)} %a_ref.1) | copy-start | bytes 393220
  0.7 60.7 %copy-start.8 = (s32[1,1,4096]{2,1,0:T(1,128)S(1)}, s32[1,1,4096]{2,1,0:T(1,128)}, u32[]{:S(2)}) copy-start(s32[1,1,4096]{2,1,0:T(1,128)} %param.20) | copy-start | bytes 49156
  3.3 79.3 %copy-start.12 = (bf16[1,1,16,4096]{3,2,1,0:T(8,128)(2,1)S(1)}, bf16[1,1,16,4096]{3,2,1,0:T(8,128)(2,1)}, u32[]{:S(2)}) copy-start(bf16[1,1,16,4096]{3,2,1,0:T(8,128)(2,1)} %param.23) | copy-start | bytes 393220
  3.3 79.3 %copy-start.13 = (bf16[1024,64]{0,1:T(8,128)(2,1)S(1)}, bf16[1024,64]{0,1:T(8,128)(2,1)}, u32[]{:S(2)}) copy-start(bf16[1024,64]{0,1:T(8,128)(2,1)} %param.26) | copy-start | bytes 393220
  3.3 79.3 %copy-start.15 = (s32[1,1,4096]{2,1,0:T(1,128)S(1)}, s32[1,1,4096]{2,1,0:T(1,128)}, u32[]{:S(2)}) copy-start(s32[1,1,4096]{2,1,0:T(1,128)} %param.21) | copy-start | bytes 49156
  3.4 47.7 %all-to-all-start = ((bf16[8,256,128]{2,1,0:T(8,128)(2,1)}), bf16[8,256,128]{2,1,0:T(8,128)(2,1)S(1)}, u32[]{:S(2)}, u32[]{:S(2)}) async-start(bf16[8,256,128]{2,1,0:T(8,128)(2,1)} %shard_map.176.after_ref), calls=%async_computation | async-start | bytes 1048576 | tf_op jit(solution)/shard_map/all_to_all | solution.py:264
  21.8 1.1 copy-start
  22.9 34.0 %collective-permute-start.5 = (bf16[2,64,1024]{2,1,0:T(8,128)(2,1)S(1)}, bf16[2,64,1024]{2,1,0:T(8,128)(2,1)S(1)}, u32[]{:S(2)}, u32[]{:S(2)}) collective-permute-start(bf16[2,64,1024]{2,1,0:T(8,128)(2,1)S(1)} %shard_map.180), channel_id=1, source_target_pairs={{0,4},{1,5},{2,6},{3,7},{4,8},{5,9},{6,10},{7,11},{8,12},{9,13},{1... | collective-permute-start | bytes 786440 | tf_op jit(solution)/shard_map/ppermute | solution.py:274
  26.0 36.1 %collective-permute-start.4 = (bf16[2,64,1024]{2,1,0:T(8,128)(2,1)S(1)}, bf16[2,64,1024]{2,1,0:T(8,128)(2,1)S(1)}, u32[]{:S(2)}, u32[]{:S(2)}) collective-permute-start(bf16[2,64,1024]{2,1,0:T(8,128)(2,1)S(1)} %shard_map.180), channel_id=1, source_target_pairs={{0,8},{1,9},{2,10},{3,11},{4,12},{5,13},{6,14},{7,15},{8,0},{9,1},... | collective-permute-start | bytes 786440 | tf_op jit(solution)/shard_map/ppermute | solution.py:274
  30.4 31.8 %collective-permute-start.3 = (bf16[2,64,1024]{2,1,0:T(8,128)(2,1)S(1)}, bf16[2,64,1024]{2,1,0:T(8,128)(2,1)S(1)}, u32[]{:S(2)}, u32[]{:S(2)}) collective-permute-start(bf16[2,64,1024]{2,1,0:T(8,128)(2,1)S(1)} %shard_map.180), channel_id=1, source_target_pairs={{0,12},{1,13},{2,14},{3,15},{4,0},{5,1},{6,2},{7,3},{8,4},{9,5},{1... | collective-permute-start | bytes 786440 | tf_op jit(solution)/shard_map/ppermute | solution.py:274
  51.0 15.0 %collective-permute-start.2 = (bf16[8,256,128]{2,1,0:T(8,128)(2,1)S(1)}, bf16[8,256,128]{2,1,0:T(8,128)(2,1)S(1)}, u32[]{:S(2)}, u32[]{:S(2)}) collective-permute-start(bf16[8,256,128]{2,1,0:T(8,128)(2,1)S(1)} %all-to-all-done.b0), channel_id=1, source_target_pairs={{0,32},{16,48},{32,64},{48,80},{64,96},{80,112},{96,128},{112,144}... | collective-permute-start | bytes 1572872 | tf_op jit(solution)/shard_map/ppermute | solution.py:276
  54.0 24.2 %collective-permute-start.1 = (bf16[8,256,128]{2,1,0:T(8,128)(2,1)S(1)}, bf16[8,256,128]{2,1,0:T(8,128)(2,1)S(1)}, u32[]{:S(2)}, u32[]{:S(2)}) collective-permute-start(bf16[8,256,128]{2,1,0:T(8,128)(2,1)S(1)} %all-to-all-done.b0), channel_id=1, source_target_pairs={{0,64},{16,80},{32,480},{48,496},{64,128},{80,144},{96,32},{112,48... | collective-permute-start | bytes 1572872 | tf_op jit(solution)/shard_map/ppermute | solution.py:277
  56.9 25.7 %collective-permute-start = (bf16[8,256,128]{2,1,0:T(8,128)(2,1)S(1)}, bf16[8,256,128]{2,1,0:T(8,128)(2,1)S(1)}, u32[]{:S(2)}, u32[]{:S(2)}) collective-permute-start(bf16[8,256,128]{2,1,0:T(8,128)(2,1)S(1)} %all-to-all-done.b0), channel_id=1, source_target_pairs={{0,480},{16,496},{32,0},{48,16},{64,32},{80,48},{96,64},{112,80},{... | collective-permute-start | bytes 1572872 | tf_op jit(solution)/shard_map/ppermute | solution.py:275
  62.3 42.5 %collective-permute-start.6 = (bf16[4,2,64,1024]{3,2,1,0:T(8,128)(2,1)S(1)}, bf16[4,2,64,1024]{3,2,1,0:T(8,128)(2,1)}, u32[]{:S(2)}, u32[]{:S(2)}) collective-permute-start(bf16[4,2,64,1024]{3,2,1,0:T(8,128)(2,1)S(1)} %pad_maximum_fusion.wa_ref), channel_id=1, source_target_pairs={{0,2},{1,3},{2,0},{3,1},{4,6},{5,7},{6,4},{7,5},{8,10},{9,11},{10,... | collective-permute-start | bytes 3145736 | tf_op jit(solution)/shard_map/ppermute | solution.py:280
  82.7 33.3 %copy-start.14 = (bf16[64,1024]{1,0:T(8,128)(2,1)S(1)}, bf16[64,1024]{1,0:T(8,128)(2,1)}, u32[]{:S(2)}) copy-start(bf16[64,1024]{1,0:T(8,128)(2,1)} %upf_ref.1) | copy-start | bytes 393220
  89.8 0.7 copy-start.16
  90.5 13.6 %all-to-all-start.1 = ((bf16[32,8,128]{2,1,0:T(8,128)(2,1)}), bf16[32,8,128]{2,1,0:T(8,128)(2,1)S(1)}, u32[]{:S(2)}, u32[]{:S(2)}) async-start(bf16[32,8,128]{2,1,0:T(8,128)(2,1)} %get-tuple-element.12), calls=%async_computation.1 | async-start | bytes 131072 | tf_op jit(solution)/shard_map/all_to_all | solution.py:317
  104.8 17.8 %all-to-all-start.2 = ((bf16[16,16,128]{2,1,0:T(8,128)(2,1)}), bf16[16,16,128]{2,1,0:T(8,128)(2,1)S(1)}, u32[]{:S(2)}, u32[]{:S(2)}) async-start(bf16[16,16,128]{2,1,0:T(8,128)(2,1)} %shard_map.179), calls=%async_computation.2 | async-start | bytes 131072 | tf_op jit(solution)/shard_map/all_to_all | solution.py:331
  111.0 11.6 %collective-permute-start.7 = (bf16[4,2,64,1024]{3,2,1,0:T(8,128)(2,1)S(1)}, bf16[4,2,64,1024]{3,2,1,0:T(8,128)(2,1)}, u32[]{:S(2)}, u32[]{:S(2)}) collective-permute-start(bf16[4,2,64,1024]{3,2,1,0:T(8,128)(2,1)S(1)} %pad_maximum_fusion.wa_ref), channel_id=1, source_target_pairs={{0,1},{1,0},{2,3},{3,2},{4,5},{5,4},{6,7},{7,6},{8,9},{9,8},{10,11... | collective-permute-start | bytes 3145736 | tf_op jit(solution)/shard_map/ppermute | solution.py:329
  114.0 8.6 %collective-permute-start.8 = (bf16[4,2,64,1024]{3,2,1,0:T(8,128)(2,1)}, bf16[4,2,64,1024]{3,2,1,0:T(8,128)(2,1)}, u32[]{:S(2)}, u32[]{:S(2)}) collective-permute-start(bf16[4,2,64,1024]{3,2,1,0:T(8,128)(2,1)} %collective-permute-done.6.wb_ref), channel_id=1, source_target_pairs={{0,1},{1,0},{2,3},{3,2},{4,5},{5,4},{6,7},{7,6},{8,9},{9,8},{10,11... | collective-permute-start | bytes 3145736 | tf_op jit(solution)/shard_map/ppermute | solution.py:330
  116.0 1.2 copy-start.1
  117.2 0.9 copy-start.17
  118.1 4.5 %copy-start.4 = (bf16[64,1024]{1,0:T(8,128)(2,1)S(1)}, bf16[64,1024]{1,0:T(8,128)(2,1)}, u32[]{:S(2)}) copy-start(bf16[64,1024]{1,0:T(8,128)(2,1)} %upr_ref.1) | copy-start | bytes 393220
  118.1 4.5 %copy-start.9 = (s32[1,1,512]{2,1,0:T(1,128)S(1)}, s32[1,1,512]{2,1,0:T(1,128)}, u32[]{:S(2)}) copy-start(s32[1,1,512]{2,1,0:T(1,128)} %param.19) | copy-start | bytes 6148
  118.1 4.5 %copy-start.11 = (s32[1,1,512]{2,1,0:T(1,128)S(1)}, s32[1,1,512]{2,1,0:T(1,128)}, u32[]{:S(2)}) copy-start(s32[1,1,512]{2,1,0:T(1,128)} %param.24) | copy-start | bytes 6148
  122.7 1.0 copy-start.2
  123.7 17.3 %copy-start.5 = (bf16[256,256]{1,0:T(8,128)(2,1)S(1)}, bf16[256,256]{1,0:T(8,128)(2,1)}, u32[]{:S(2)}) copy-start(bf16[256,256]{1,0:T(8,128)(2,1)} %w_ref.1) | copy-start | bytes 393220
  123.7 17.3 %copy-start.10 = (bf16[1,16,256]{2,1,0:T(8,128)(2,1)S(1)}, bf16[1,16,256]{2,1,0:T(8,128)(2,1)}, u32[]{:S(2)}) copy-start(bf16[1,16,256]{2,1,0:T(8,128)(2,1)} %param.18) | copy-start | bytes 24580
  123.7 27.1 %copy-start.3 = (bf16[256,1024]{1,0:T(8,128)(2,1)S(1)}, bf16[256,1024]{1,0:T(8,128)(2,1)}, u32[]{:S(2)}) copy-start(bf16[256,1024]{1,0:T(8,128)(2,1)} %back_ref.1) | copy-start | bytes 1572868

commit v5 on v4

--- a/solution.py
+++ b/solution.py
@@ -14,7 +14,7 @@
 
 Z, YH, NT = 16, 2, 16
 NS = Z * YH
-FAR = 8
+FAR = 4
 NEAR = YH * NT
 XS = 4
 PEER = (0, 2, 1, 3)
@@ -58,7 +58,7 @@
 
 
 def contract_kernel(
-    pos_ref, cnt_ref, ids_ref, tgt_ref, basis_ref, bil_ref, b0, b1, b2, b3,
+    pos_ref, cnt_ref, ids_ref, tgt_ref, basis_ref, bil_ref, b0, b1, b2, b3, c0, c1, c2, c3,
     tm_ref, send_ref, col, rows_a, rows_b, acc, total,
 ):
     trips = tgt_ref.shape[1]
@@ -67,7 +67,7 @@
     step = rows_a.shape[0]
 
     def widen(i, c):
-        for n, ref in enumerate((b0, b1, b2, b3)):
+        for n, ref in enumerate((b0, b1, b2, b3, c0, c1, c2, c3)):
             at = pl.multiple_of((n * FAR + i) * 256, 256)
             col[pl.ds(at, 256), :] = ref[i].astype(F32)
         return c
@@ -201,6 +201,10 @@
     return [(z * YH + h, ((z + d) % Z) * YH + h) for z in range(Z) for h in range(YH)]
 
 
+def swap():
+    return [(i, i ^ 1) for i in range(NS)]
+
+
 def shift_two():
     return [
         (z * YH + h, ((z + (2 if z % 2 == 0 else -2)) % Z) * YH + h)
@@ -258,12 +262,11 @@
         compiler_params=params(60),
     )(rows, down_proj.T)
 
-    groups = [
-        [((z0 + 4 * i) % Z) * YH + h for i in range(4) for h in range(YH)] for z0 in range(4)
-    ]
-    near = lax.all_to_all(
+    groups = [[((z0 + 4 * i) % Z) * YH + h for i in range(4)] for z0 in range(4) for h in range(YH)]
+    own = lax.all_to_all(
         far, "src", split_axis=0, concat_axis=0, tiled=True, axis_index_groups=groups
     )
+    other = lax.ppermute(own, "src", swap())
     own_w = pl.pallas_call(
         pack_kernel,
         out_shape=struct((2,) + res_first.shape),
@@ -272,10 +275,9 @@
         compiler_params=params(4),
     )(far, res_first, res_second)
     x_w = [own_w] + [lax.ppermute(own_w, "tgt", along_x(d)) for d in (-1, 2, 1)]
-    from_next = lax.ppermute(near, "src", shift(-1))
-    from_prev = lax.ppermute(near, "src", shift(1))
-    from_two = lax.ppermute(near, "src", shift_two())
-
+    pieces = []
+    for part in (own, other):
+        pieces += [part] + [lax.ppermute(part, "src", p) for p in (shift(-1), shift_two(), shift(1))]
     x_w = jnp.stack(x_w)
     y_w = lax.ppermute(x_w, "tgt", across(2))
 
@@ -283,12 +285,13 @@
     ids = trip_source[0]
     q = ids >> 9
     zq = q >> 1
-    pos = (((zq - my_z) & 3) * FAR + (zq >> 2) * 2 + (q & 1)) * (edges // 2) + (ids & 255)
+    other_y = (q ^ lax.axis_index("src")) & 1
+    pos = ((other_y * 4 + ((zq - my_z) & 3)) * FAR + (zq >> 2)) * (edges // 2) + (ids & 255)
 
     tm, send = pl.pallas_call(
         contract_kernel,
         out_shape=(struct((edges, width)), struct((NEAR, Z // 2, 2 * width))),
-        in_specs=[SM, SM] + [VM] * 8,
+        in_specs=[SM, SM] + [VM] * 12,
         out_specs=(VM, VM),
         scratch_shapes=[
             pltpu.VMEM((NS * edges // 2, 2 * width), F32),
@@ -306,10 +309,7 @@
         trip_target[0],
         trip_basis[0, 0],
         bilinear.T,
-        near,
-        from_next,
-        from_two,
-        from_prev,
+        *pieces,
     )
 
     plane = [[(z * YH + h) * NT + t for h in range(YH) for t in range(NT)] for z in range(Z)]

time: 153 us -> 145 us (0.948)
  waiting for transfers between devices: 46.6 us -> 21.9 us
  starting transfers between devices: 59.2 us -> 74.1 us
  local copies, waits for them, and re-layouts: 4.92 us -> 6.65 us
    ppermute x3 -> x7, starting transfers between devices: 10.3 us -> 27.8 us  [the longest x6 23 us: local(): lax.ppermute(part, 'src', p)]
    all_to_all x1, waiting for transfers between devices: 17.6 us -> 3.48 us  [local(): lax.all_to_all(far, 'src', split_axis=0, concat_axis=0, tiled=True, axis_...]
    ppermute x3 -> x7, waiting for transfers between devices: 18.1 us -> 7.55 us  [the longest x6 7.54 us: local(): lax.ppermute(part, 'src', p)]
    all_to_all x1, starting transfers between devices: 18.4 us -> 15.8 us  [local(): lax.all_to_all(far, 'src', split_axis=0, concat_axis=0, tiled=True, axis_...]
    unnamed x36, local copies, waits for them, and re-layouts: 4.92 us -> 6.65 us
  transfers between devices with their start and end apart: 12 -> 16, of which waited for: 6 -> 6; matrix products, arithmetic and copies ran while one was open for 0% -> 0% of each run, Pallas kernels for 6% -> 6%
where the time goes in v5:
time: 145 us
  starting transfers between devices  74.1 us (51%)
  waiting for transfers between devices  21.9 us (15%)
  Pallas kernels  20.2 us (14%)
  blocking collectives  19.9 us (14%)
  local copies, waits for them, and re-layouts  6.65 us (5%)
  between operations  1.62 us (1%)
    ppermute x6, starting transfers between devices, local(): lax.ppermute(part, 'src', p)  23 us
    all_to_all x1, starting transfers between devices, local(): lax.all_to_all(far, 'src', split_axis=0, concat_axis=0, tiled=True, axis_...  15.8 us
    ppermute x3, starting transfers between devices, local(): x_w = [own_w] + [lax.ppermute(own_w, 'tgt', along_x(d)) for d in (-1, 2, 1)]  11.9 us
    all_to_all x1, blocking collectives, local(): lax.all_to_all(part.reshape(NT, atoms // NT, da), 'tgt', split_axis=0, co...  10.9 us
    all_to_all x1, blocking collectives, local(): lax.all_to_all(spread, 'tgt', split_axis=0, concat_axis=0, tiled=True)  9.06 us
    ppermute x6, waiting for transfers between devices, local(): lax.ppermute(part, 'src', p)  7.54 us
    all_to_all x1, waiting for transfers between devices, local(): lax.all_to_all(send, ('src', 'tgt'), split_axis=0, concat_axis=0, tiled=T...  7.25 us
    pallas_call x1, Pallas kernels, local(): pl.pallas_call(contract_kernel, out_shape=(struct((edges, width)), struct...  7.15 us
  transfers between devices with their start and end apart: 16, of which 6 were waited for; matrix products, arithmetic and copies ran while one was open for 0% of the time, Pallas kernels for 6%

profile of v5, /device:TPU:1, one launch (start us, length us, event | category | flops | bytes accessed | tf_op | source)
XLA Modules:
  0.0 144.5 jit_solution(9343844366338670280)
XLA Ops:
  0.6 0.0 copy-start.8
  0.6 2.5 %shard_map.176.after_ref = bf16[4,256,128]{2,1,0:T(8,128)(2,1)} custom-call(bf16[512,1024]{1,0:T(8,128)(2,1)} %bitcast.20, bf16[64,1024]{1,0:T(8,128)(2,1)} %bitcast.38), custom_call_target="tpu_custom_call" | custom-call | tf_op jit(solution)/shard_map/pallas_call | solution.py:252
  3.2 0.0 copy-start.12
  3.2 0.0 copy-start.13
  3.2 0.0 copy-start.15
  3.2 15.8 %all-to-all-start = ((bf16[4,256,128]{2,1,0:T(8,128)(2,1)}), bf16[4,256,128]{2,1,0:T(8,128)(2,1)S(1)}, u32[]{:S(2)}, u32[]{:S(2)}) async-start(bf16[4,256,128]{2,1,0:T(8,128)(2,1)} %shard_map.176.after_ref), calls=%async_computation | async-start | bytes 524288 | tf_op jit(solution)/shard_map/all_to_all | solution.py:266
  19.0 1.0 copy-done
  20.0 0.9 copy-done.6
  20.9 0.9 copy-done.7
  21.8 3.1 %collective-permute-start.9 = (bf16[2,64,1024]{2,1,0:T(8,128)(2,1)S(1)}, bf16[2,64,1024]{2,1,0:T(8,128)(2,1)S(1)}, u32[]{:S(2)}, u32[]{:S(2)}) collective-permute-start(bf16[2,64,1024]{2,1,0:T(8,128)(2,1)S(1)} %shard_map.180), channel_id=1, source_target_pairs={{0,4},{1,5},{2,6},{3,7},{4,8},{5,9},{6,10},{7,11},{8,12},{9,13},{1... | collective-permute-start | bytes 786440 | tf_op jit(solution)/shard_map/ppermute | solution.py:277
  24.9 4.4 %collective-permute-start.8 = (bf16[2,64,1024]{2,1,0:T(8,128)(2,1)S(1)}, bf16[2,64,1024]{2,1,0:T(8,128)(2,1)S(1)}, u32[]{:S(2)}, u32[]{:S(2)}) collective-permute-start(bf16[2,64,1024]{2,1,0:T(8,128)(2,1)S(1)} %shard_map.180), channel_id=1, source_target_pairs={{0,8},{1,9},{2,10},{3,11},{4,12},{5,13},{6,14},{7,15},{8,0},{9,1},... | collective-permute-start | bytes 786440 | tf_op jit(solution)/shard_map/ppermute | solution.py:277
  29.3 3.5 %all-to-all-done.b0 = bf16[4,256,128]{2,1,0:T(8,128)(2,1)S(1)} async-done(((bf16[4,256,128]{2,1,0:T(8,128)(2,1)}), bf16[4,256,128]{2,1,0:T(8,128)(2,1)S(1)}, u32[]{:S(2)}, u32[]{:S(2)}) %all-to-all-start) | async-done | bytes 262176 | tf_op jit(solution)/shard_map/all_to_all | solution.py:266
  32.8 4.8 %collective-permute-start.3 = (bf16[4,256,128]{2,1,0:T(8,128)(2,1)S(1)}, bf16[4,256,128]{2,1,0:T(8,128)(2,1)S(1)}, u32[]{:S(2)}, u32[]{:S(2)}) collective-permute-start(bf16[4,256,128]{2,1,0:T(8,128)(2,1)S(1)} %all-to-all-done.b0), channel_id=1, source_target_pairs={{0,16},{16,0},{32,48},{48,32},{64,80},{80,64},{96,112},{112,96},{1... | collective-permute-start | bytes 786440 | tf_op jit(solution)/shard_map/ppermute | solution.py:269
  37.6 4.4 %collective-permute-start.7 = (bf16[2,64,1024]{2,1,0:T(8,128)(2,1)S(1)}, bf16[2,64,1024]{2,1,0:T(8,128)(2,1)S(1)}, u32[]{:S(2)}, u32[]{:S(2)}) collective-permute-start(bf16[2,64,1024]{2,1,0:T(8,128)(2,1)S(1)} %shard_map.180), channel_id=1, source_target_pairs={{0,12},{1,13},{2,14},{3,15},{4,0},{5,1},{6,2},{7,3},{8,4},{9,5},{1... | collective-permute-start | bytes 786440 | tf_op jit(solution)/shard_map/ppermute | solution.py:277
  42.0 8.4 %collective-permute-start.2 = (bf16[4,256,128]{2,1,0:T(8,128)(2,1)S(1)}, bf16[4,256,128]{2,1,0:T(8,128)(2,1)S(1)}, u32[]{:S(2)}, u32[]{:S(2)}) collective-permute-start(bf16[4,256,128]{2,1,0:T(8,128)(2,1)S(1)} %all-to-all-done.b0), channel_id=1, source_target_pairs={{0,32},{16,48},{32,64},{48,80},{64,96},{80,112},{96,128},{112,144}... | collective-permute-start | bytes 786440 | tf_op jit(solution)/shard_map/ppermute | solution.py:280
  50.5 0.0 collective-permute-done.9
  50.5 2.3 %collective-permute-start.1 = (bf16[4,256,128]{2,1,0:T(8,128)(2,1)S(1)}, bf16[4,256,128]{2,1,0:T(8,128)(2,1)S(1)}, u32[]{:S(2)}, u32[]{:S(2)}) collective-permute-start(bf16[4,256,128]{2,1,0:T(8,128)(2,1)S(1)} %all-to-all-done.b0), channel_id=1, source_target_pairs={{0,64},{16,80},{32,480},{48,496},{64,128},{80,144},{96,32},{112,48... | collective-permute-start | bytes 786440 | tf_op jit(solution)/shard_map/ppermute | solution.py:280
  52.8 0.0 collective-permute-done.8
  52.8 3.8 %collective-permute-start = (bf16[4,256,128]{2,1,0:T(8,128)(2,1)S(1)}, bf16[4,256,128]{2,1,0:T(8,128)(2,1)S(1)}, u32[]{:S(2)}, u32[]{:S(2)}) collective-permute-start(bf16[4,256,128]{2,1,0:T(8,128)(2,1)S(1)} %all-to-all-done.b0), channel_id=1, source_target_pairs={{0,480},{16,496},{32,0},{48,16},{64,32},{80,48},{96,64},{112,80},{... | collective-permute-start | bytes 786440 | tf_op jit(solution)/shard_map/ppermute | solution.py:280
  56.6 0.0 collective-permute-done.3.c0
  56.6 1.9 %collective-permute-start.6 = (bf16[4,256,128]{2,1,0:T(8,128)(2,1)S(1)}, bf16[4,256,128]{2,1,0:T(8,128)(2,1)S(1)}, u32[]{:S(2)}, u32[]{:S(2)}) collective-permute-start(bf16[4,256,128]{2,1,0:T(8,128)(2,1)S(1)} %collective-permute-done.3.c0), channel_id=1, source_target_pairs={{0,32},{16,48},{32,64},{48,80},{64,96},{80,112},{96,128},{112,144}... | collective-permute-start | bytes 786440 | tf_op jit(solution)/shard_map/ppermute | solution.py:280
  58.5 0.0 collective-permute-done.7
  58.6 3.8 %collective-permute-start.5 = (bf16[4,256,128]{2,1,0:T(8,128)(2,1)S(1)}, bf16[4,256,128]{2,1,0:T(8,128)(2,1)S(1)}, u32[]{:S(2)}, u32[]{:S(2)}) collective-permute-start(bf16[4,256,128]{2,1,0:T(8,128)(2,1)S(1)} %collective-permute-done.3.c0), channel_id=1, source_target_pairs={{0,64},{16,80},{32,480},{48,496},{64,128},{80,144},{96,32},{112,48... | collective-permute-start | bytes 786440 | tf_op jit(solution)/shard_map/ppermute | solution.py:280
  62.4 0.0 collective-permute-done.2.b3
  62.4 2.8 %collective-permute-start.4 = (bf16[4,256,128]{2,1,0:T(8,128)(2,1)S(1)}, bf16[4,256,128]{2,1,0:T(8,128)(2,1)S(1)}, u32[]{:S(2)}, u32[]{:S(2)}) collective-permute-start(bf16[4,256,128]{2,1,0:T(8,128)(2,1)S(1)} %collective-permute-done.3.c0), channel_id=1, source_target_pairs={{0,480},{16,496},{32,0},{48,16},{64,32},{80,48},{96,64},{112,80},{... | collective-permute-start | bytes 786440 | tf_op jit(solution)/shard_map/ppermute | solution.py:280
  65.1 0.0 copy-done.8
  65.2 0.1 and_add_fusion.pos_ref
  65.9 0.1 pad_maximum_fusion.wa_ref
  66.0 0.0 collective-permute-done.1.b2
  66.0 2.3 %collective-permute-start.10 = (bf16[4,2,64,1024]{3,2,1,0:T(8,128)(2,1)S(1)}, bf16[4,2,64,1024]{3,2,1,0:T(8,128)(2,1)}, u32[]{:S(2)}, u32[]{:S(2)}) collective-permute-start(bf16[4,2,64,1024]{3,2,1,0:T(8,128)(2,1)S(1)} %pad_maximum_fusion.wa_ref), channel_id=1, source_target_pairs={{0,2},{1,3},{2,0},{3,1},{4,6},{5,7},{6,4},{7,5},{8,10},{9,11},{10,... | collective-permute-start | bytes 3145736 | tf_op jit(solution)/shard_map/ppermute | solution.py:282
  68.3 0.0 collective-permute-done.b1
  68.4 1.1 collective-permute-done.6.c3
  69.4 3.5 %collective-permute-done.5.c2 = bf16[4,256,128]{2,1,0:T(8,128)(2,1)S(1)} collective-permute-done((bf16[4,256,128]{2,1,0:T(8,128)(2,1)S(1)}, bf16[4,256,128]{2,1,0:T(8,128)(2,1)S(1)}, u32[]{:S(2)}, u32[]{:S(2)}) %collective-permute-start.5) | collective-permute-done | bytes 262176 | tf_op jit(solution)/shard_map/ppermute | solution.py:280
  72.9 3.0 %collective-permute-done.4.c1 = bf16[4,256,128]{2,1,0:T(8,128)(2,1)S(1)} collective-permute-done((bf16[4,256,128]{2,1,0:T(8,128)(2,1)S(1)}, bf16[4,256,128]{2,1,0:T(8,128)(2,1)S(1)}, u32[]{:S(2)}, u32[]{:S(2)}) %collective-permute-start.4) | collective-permute-done | bytes 262176 | tf_op jit(solution)/shard_map/ppermute | solution.py:280
  75.9 0.0 copy-done.12
  75.9 0.0 copy-done.13
  75.9 0.0 copy-done.15
  75.9 7.2 %shard_map.177 = (bf16[512,64]{1,0:T(8,128)(2,1)S(1)}, bf16[32,8,128]{2,1,0:T(8,128)(2,1)}) custom-call(s32[1,4096]{1,0:T(1,128)S(1)} %and_add_fusion.pos_ref, s32[1,1]{1,0:T(1,128)S(6)} %copy.19.cnt_ref, s32[1,4096]{1,0:T(1,128)S(1)} %bitcast.26, s32[1,4096]{1,0:T(1,128)S(1)} %bitcast.33, bf16[16,4096]{1,0:T(8,128)(2,1)S(1)} %bitcast.31, ...), custom_call_target="tpu_custom_call" | custom-call | flops 99999997952 | bytes 10000000 | tf_op jit(solution)/shard_map/pallas_call | solution.py:291
  83.1 0.7 copy-done.16
  83.7 5.1 %all-to-all-start.1 = ((bf16[32,8,128]{2,1,0:T(8,128)(2,1)}), bf16[32,8,128]{2,1,0:T(8,128)(2,1)S(1)}, u32[]{:S(2)}, u32[]{:S(2)}) async-start(bf16[32,8,128]{2,1,0:T(8,128)(2,1)} %get-tuple-element.12), calls=%async_computation.1 | async-start | bytes 131072 | tf_op jit(solution)/shard_map/all_to_all | solution.py:317
  88.8 7.2 %all-to-all-done.1.x_ref = bf16[32,8,128]{2,1,0:T(8,128)(2,1)S(1)} async-done(((bf16[32,8,128]{2,1,0:T(8,128)(2,1)}), bf16[32,8,128]{2,1,0:T(8,128)(2,1)S(1)}, u32[]{:S(2)}, u32[]{:S(2)}) %all-to-all-start.1) | async-done | bytes 65568 | tf_op jit(solution)/shard_map/all_to_all | solution.py:317
  96.0 0.7 shard_map.179
  96.8 0.0 collective-permute-done.10.wb_ref
  96.8 6.1 %all-to-all-start.2 = ((bf16[16,16,128]{2,1,0:T(8,128)(2,1)}), bf16[16,16,128]{2,1,0:T(8,128)(2,1)S(1)}, u32[]{:S(2)}, u32[]{:S(2)}) async-start(bf16[16,16,128]{2,1,0:T(8,128)(2,1)} %shard_map.179), calls=%async_computation.2 | async-start | bytes 131072 | tf_op jit(solution)/shard_map/all_to_all | solution.py:331
  102.9 3.0 %collective-permute-start.11 = (bf16[4,2,64,1024]{3,2,1,0:T(8,128)(2,1)S(1)}, bf16[4,2,64,1024]{3,2,1,0:T(8,128)(2,1)}, u32[]{:S(2)}, u32[]{:S(2)}) collective-permute-start(bf16[4,2,64,1024]{3,2,1,0:T(8,128)(2,1)S(1)} %pad_maximum_fusion.wa_ref), channel_id=1, source_target_pairs={{0,1},{1,0},{2,3},{3,2},{4,5},{5,4},{6,7},{7,6},{8,9},{9,8},{10,11... | collective-permute-start | bytes 3145736 | tf_op jit(solution)/shard_map/ppermute | solution.py:329
  105.9 2.1 %collective-permute-start.12 = (bf16[4,2,64,1024]{3,2,1,0:T(8,128)(2,1)}, bf16[4,2,64,1024]{3,2,1,0:T(8,128)(2,1)}, u32[]{:S(2)}, u32[]{:S(2)}) collective-permute-start(bf16[4,2,64,1024]{3,2,1,0:T(8,128)(2,1)} %collective-permute-done.10.wb_ref), channel_id=1, source_target_pairs={{0,1},{1,0},{2,3},{3,2},{4,5},{5,4},{6,7},{7,6},{8,9},{9,8},{10,11... | collective-permute-start | bytes 3145736 | tf_op jit(solution)/shard_map/ppermute | solution.py:330
  108.0 0.0 copy-done.14
  108.0 0.0 copy-start.1
  108.0 1.2 copy-done.1
  109.3 0.9 copy-done.17
  110.2 0.8 shard_map.178.x_ref
  110.9 3.6 %all-to-all-done.2 = bf16[16,16,128]{2,1,0:T(8,128)(2,1)S(1)} async-done(((bf16[16,16,128]{2,1,0:T(8,128)(2,1)}), bf16[16,16,128]{2,1,0:T(8,128)(2,1)S(1)}, u32[]{:S(2)}, u32[]{:S(2)}) %all-to-all-start.2) | async-done | bytes 65568 | tf_op jit(solution)/shard_map/all_to_all | solution.py:331
  114.5 0.0 collective-permute-done.11.wc_ref
  114.5 0.0 collective-permute-done.12.wd_ref
  114.5 0.0 copy-done.9
  114.5 0.0 copy-done.11
  114.5 0.0 copy-start.2
  114.5 1.0 copy-done.2
  115.6 6.4 %shard_map.181 = (bf16[512,1024]{1,0:T(8,128)(2,1)S(1)}, bf16[256,256]{1,0:T(8,128)(2,1)S(1)}) custom-call(s32[1,1]{1,0:T(1,128)} %bitcast.me_ref, f32[512,1024]{1,0:T(8,128)S(1)} %shard_map.178.x_ref, bf16[256,128]{1,0:T(8,128)(2,1)S(1)} %bitcast.24, s32[1,512]{1,0:T(1,128)S(1)} %bitcast.30, s32[1,512]{1,0:T(1,128)S(1)} %bitcast.27, ...), custom_call_target="tpu_custom_call" | custom-call | tf_op jit(solution)/shard_map/pallas_call | solution.py:345
  122.0 10.9 %all_to_all.25.parts_ref = bf16[16,16,256]{2,1,0:T(8,128)(2,1)S(1)} all-to-all(bf16[16,16,256]{2,1,0:T(8,128)(2,1)S(1)} %bitcast.25), channel_id=1, replica_groups=mesh['src'=32,'tgt'=16] {'tgt'}, dimensions={0} | all-to-all | bytes 262144 | tf_op jit(solution)/shard_map/all_to_all | solution.py:370
  132.8 0.0 copy-done.10
  132.8 0.8 shard_map.182
  133.6 9.1 %all_to_all.26 = bf16[16,16,256]{2,1,0:T(8,128)(2,1)S(1)} all-to-all(bf16[16,16,256]{2,1,0:T(8,128)(2,1)S(1)} %get-tuple-element.18), channel_id=1, replica_groups=mesh['src'=32,'tgt'=16] {'tgt'}, dimensions={0} | all-to-all | bytes 262144 | tf_op jit(solution)/shard_map/all_to_all | solution.py:380
  142.7 1.9 %shard_map.183 = bf16[512,1024]{1,0:T(8,128)(2,1)} custom-call(bf16[512,1024]{1,0:T(8,128)(2,1)S(1)} %get-tuple-element.16.skip_ref, bf16[256,256]{1,0:T(8,128)(2,1)S(1)} %bitcast.23, s32[1,512]{1,0:T(1,128)S(1)} %bitcast.28, bf16[256,1024]{1,0:T(8,128)(2,1)S(1)} %copy-done.3), custom_call_target="tpu_custom_call" | custom-call | tf_op jit(solution)/shard_map/pallas_call | solution.py:381
  (16 shorter events, 0.0 us)
Async XLA Ops:
  0.6 64.5 %copy-start.8 = (s32[1,1,4096]{2,1,0:T(1,128)S(1)}, s32[1,1,4096]{2,1,0:T(1,128)}, u32[]{:S(2)}) copy-start(s32[1,1,4096]{2,1,0:T(1,128)} %param.20) | copy-start | bytes 49156
  3.2 72.7 %copy-start.12 = (bf16[1,1,16,4096]{3,2,1,0:T(8,128)(2,1)S(1)}, bf16[1,1,16,4096]{3,2,1,0:T(8,128)(2,1)}, u32[]{:S(2)}) copy-start(bf16[1,1,16,4096]{3,2,1,0:T(8,128)(2,1)} %param.23) | copy-start | bytes 393220
  3.2 72.7 %copy-start.13 = (bf16[1024,64]{0,1:T(8,128)(2,1)S(1)}, bf16[1024,64]{0,1:T(8,128)(2,1)}, u32[]{:S(2)}) copy-start(bf16[1024,64]{0,1:T(8,128)(2,1)} %param.26) | copy-start | bytes 393220
  3.2 72.7 %copy-start.15 = (s32[1,1,4096]{2,1,0:T(1,128)S(1)}, s32[1,1,4096]{2,1,0:T(1,128)}, u32[]{:S(2)}) copy-start(s32[1,1,4096]{2,1,0:T(1,128)} %param.21) | copy-start | bytes 49156
  3.2 29.6 %all-to-all-start = ((bf16[4,256,128]{2,1,0:T(8,128)(2,1)}), bf16[4,256,128]{2,1,0:T(8,128)(2,1)S(1)}, u32[]{:S(2)}, u32[]{:S(2)}) async-start(bf16[4,256,128]{2,1,0:T(8,128)(2,1)} %shard_map.176.after_ref), calls=%async_computation | async-start | bytes 524288 | tf_op jit(solution)/shard_map/all_to_all | solution.py:266
  19.0 1.0 copy-start
  20.0 0.9 copy-start.6
  20.9 0.9 copy-start.7
  21.8 28.7 %collective-permute-start.9 = (bf16[2,64,1024]{2,1,0:T(8,128)(2,1)S(1)}, bf16[2,64,1024]{2,1,0:T(8,128)(2,1)S(1)}, u32[]{:S(2)}, u32[]{:S(2)}) collective-permute-start(bf16[2,64,1024]{2,1,0:T(8,128)(2,1)S(1)} %shard_map.180), channel_id=1, source_target_pairs={{0,4},{1,5},{2,6},{3,7},{4,8},{5,9},{6,10},{7,11},{8,12},{9,13},{1... | collective-permute-start | bytes 786440 | tf_op jit(solution)/shard_map/ppermute | solution.py:277
  24.9 27.8 %collective-permute-start.8 = (bf16[2,64,1024]{2,1,0:T(8,128)(2,1)S(1)}, bf16[2,64,1024]{2,1,0:T(8,128)(2,1)S(1)}, u32[]{:S(2)}, u32[]{:S(2)}) collective-permute-start(bf16[2,64,1024]{2,1,0:T(8,128)(2,1)S(1)} %shard_map.180), channel_id=1, source_target_pairs={{0,8},{1,9},{2,10},{3,11},{4,12},{5,13},{6,14},{7,15},{8,0},{9,1},... | collective-permute-start | bytes 786440 | tf_op jit(solution)/shard_map/ppermute | solution.py:277
  32.8 23.8 %collective-permute-start.3 = (bf16[4,256,128]{2,1,0:T(8,128)(2,1)S(1)}, bf16[4,256,128]{2,1,0:T(8,128)(2,1)S(1)}, u32[]{:S(2)}, u32[]{:S(2)}) collective-permute-start(bf16[4,256,128]{2,1,0:T(8,128)(2,1)S(1)} %all-to-all-done.b0), channel_id=1, source_target_pairs={{0,16},{16,0},{32,48},{48,32},{64,80},{80,64},{96,112},{112,96},{1... | collective-permute-start | bytes 786440 | tf_op jit(solution)/shard_map/ppermute | solution.py:269
  37.6 21.0 %collective-permute-start.7 = (bf16[2,64,1024]{2,1,0:T(8,128)(2,1)S(1)}, bf16[2,64,1024]{2,1,0:T(8,128)(2,1)S(1)}, u32[]{:S(2)}, u32[]{:S(2)}) collective-permute-start(bf16[2,64,1024]{2,1,0:T(8,128)(2,1)S(1)} %shard_map.180), channel_id=1, source_target_pairs={{0,12},{1,13},{2,14},{3,15},{4,0},{5,1},{6,2},{7,3},{8,4},{9,5},{1... | collective-permute-start | bytes 786440 | tf_op jit(solution)/shard_map/ppermute | solution.py:277
  42.0 20.4 %collective-permute-start.2 = (bf16[4,256,128]{2,1,0:T(8,128)(2,1)S(1)}, bf16[4,256,128]{2,1,0:T(8,128)(2,1)S(1)}, u32[]{:S(2)}, u32[]{:S(2)}) collective-permute-start(bf16[4,256,128]{2,1,0:T(8,128)(2,1)S(1)} %all-to-all-done.b0), channel_id=1, source_target_pairs={{0,32},{16,48},{32,64},{48,80},{64,96},{80,112},{96,128},{112,144}... | collective-permute-start | bytes 786440 | tf_op jit(solution)/shard_map/ppermute | solution.py:280
  50.5 15.6 %collective-permute-start.1 = (bf16[4,256,128]{2,1,0:T(8,128)(2,1)S(1)}, bf16[4,256,128]{2,1,0:T(8,128)(2,1)S(1)}, u32[]{:S(2)}, u32[]{:S(2)}) collective-permute-start(bf16[4,256,128]{2,1,0:T(8,128)(2,1)S(1)} %all-to-all-done.b0), channel_id=1, source_target_pairs={{0,64},{16,80},{32,480},{48,496},{64,128},{80,144},{96,32},{112,48... | collective-permute-start | bytes 786440 | tf_op jit(solution)/shard_map/ppermute | solution.py:280
  52.8 15.6 %collective-permute-start = (bf16[4,256,128]{2,1,0:T(8,128)(2,1)S(1)}, bf16[4,256,128]{2,1,0:T(8,128)(2,1)S(1)}, u32[]{:S(2)}, u32[]{:S(2)}) collective-permute-start(bf16[4,256,128]{2,1,0:T(8,128)(2,1)S(1)} %all-to-all-done.b0), channel_id=1, source_target_pairs={{0,480},{16,496},{32,0},{48,16},{64,32},{80,48},{96,64},{112,80},{... | collective-permute-start | bytes 786440 | tf_op jit(solution)/shard_map/ppermute | solution.py:280
  56.6 12.8 %collective-permute-start.6 = (bf16[4,256,128]{2,1,0:T(8,128)(2,1)S(1)}, bf16[4,256,128]{2,1,0:T(8,128)(2,1)S(1)}, u32[]{:S(2)}, u32[]{:S(2)}) collective-permute-start(bf16[4,256,128]{2,1,0:T(8,128)(2,1)S(1)} %collective-permute-done.3.c0), channel_id=1, source_target_pairs={{0,32},{16,48},{32,64},{48,80},{64,96},{80,112},{96,128},{112,144}... | collective-permute-start | bytes 786440 | tf_op jit(solution)/shard_map/ppermute | solution.py:280
  58.6 14.3 %collective-permute-start.5 = (bf16[4,256,128]{2,1,0:T(8,128)(2,1)S(1)}, bf16[4,256,128]{2,1,0:T(8,128)(2,1)S(1)}, u32[]{:S(2)}, u32[]{:S(2)}) collective-permute-start(bf16[4,256,128]{2,1,0:T(8,128)(2,1)S(1)} %collective-permute-done.3.c0), channel_id=1, source_target_pairs={{0,64},{16,80},{32,480},{48,496},{64,128},{80,144},{96,32},{112,48... | collective-permute-start | bytes 786440 | tf_op jit(solution)/shard_map/ppermute | solution.py:280
  62.4 13.5 %collective-permute-start.4 = (bf16[4,256,128]{2,1,0:T(8,128)(2,1)S(1)}, bf16[4,256,128]{2,1,0:T(8,128)(2,1)S(1)}, u32[]{:S(2)}, u32[]{:S(2)}) collective-permute-start(bf16[4,256,128]{2,1,0:T(8,128)(2,1)S(1)} %collective-permute-done.3.c0), channel_id=1, source_target_pairs={{0,480},{16,496},{32,0},{48,16},{64,32},{80,48},{96,64},{112,80},{... | collective-permute-start | bytes 786440 | tf_op jit(solution)/shard_map/ppermute | solution.py:280
  66.0 30.8 %collective-permute-start.10 = (bf16[4,2,64,1024]{3,2,1,0:T(8,128)(2,1)S(1)}, bf16[4,2,64,1024]{3,2,1,0:T(8,128)(2,1)}, u32[]{:S(2)}, u32[]{:S(2)}) collective-permute-start(bf16[4,2,64,1024]{3,2,1,0:T(8,128)(2,1)S(1)} %pad_maximum_fusion.wa_ref), channel_id=1, source_target_pairs={{0,2},{1,3},{2,0},{3,1},{4,6},{5,7},{6,4},{7,5},{8,10},{9,11},{10,... | collective-permute-start | bytes 3145736 | tf_op jit(solution)/shard_map/ppermute | solution.py:282
  75.9 32.1 %copy-start.14 = (bf16[64,1024]{1,0:T(8,128)(2,1)S(1)}, bf16[64,1024]{1,0:T(8,128)(2,1)}, u32[]{:S(2)}) copy-start(bf16[64,1024]{1,0:T(8,128)(2,1)} %upf_ref.1) | copy-start | bytes 393220
  83.1 0.7 copy-start.16
  83.7 12.3 %all-to-all-start.1 = ((bf16[32,8,128]{2,1,0:T(8,128)(2,1)}), bf16[32,8,128]{2,1,0:T(8,128)(2,1)S(1)}, u32[]{:S(2)}, u32[]{:S(2)}) async-start(bf16[32,8,128]{2,1,0:T(8,128)(2,1)} %get-tuple-element.12), calls=%async_computation.1 | async-start | bytes 131072 | tf_op jit(solution)/shard_map/all_to_all | solution.py:317
  96.8 17.7 %all-to-all-start.2 = ((bf16[16,16,128]{2,1,0:T(8,128)(2,1)}), bf16[16,16,128]{2,1,0:T(8,128)(2,1)S(1)}, u32[]{:S(2)}, u32[]{:S(2)}) async-start(bf16[16,16,128]{2,1,0:T(8,128)(2,1)} %shard_map.179), calls=%async_computation.2 | async-start | bytes 131072 | tf_op jit(solution)/shard_map/all_to_all | solution.py:331
  102.9 11.6 %collective-permute-start.11 = (bf16[4,2,64,1024]{3,2,1,0:T(8,128)(2,1)S(1)}, bf16[4,2,64,1024]{3,2,1,0:T(8,128)(2,1)}, u32[]{:S(2)}, u32[]{:S(2)}) collective-permute-start(bf16[4,2,64,1024]{3,2,1,0:T(8,128)(2,1)S(1)} %pad_maximum_fusion.wa_ref), channel_id=1, source_target_pairs={{0,1},{1,0},{2,3},{3,2},{4,5},{5,4},{6,7},{7,6},{8,9},{9,8},{10,11... | collective-permute-start | bytes 3145736 | tf_op jit(solution)/shard_map/ppermute | solution.py:329
  105.9 8.6 %collective-permute-start.12 = (bf16[4,2,64,1024]{3,2,1,0:T(8,128)(2,1)}, bf16[4,2,64,1024]{3,2,1,0:T(8,128)(2,1)}, u32[]{:S(2)}, u32[]{:S(2)}) collective-permute-start(bf16[4,2,64,1024]{3,2,1,0:T(8,128)(2,1)} %collective-permute-done.10.wb_ref), channel_id=1, source_target_pairs={{0,1},{1,0},{2,3},{3,2},{4,5},{5,4},{6,7},{7,6},{8,9},{9,8},{10,11... | collective-permute-start | bytes 3145736 | tf_op jit(solution)/shard_map/ppermute | solution.py:330
  108.0 1.2 copy-start.1
  109.3 0.9 copy-start.17
  110.2 4.3 %copy-start.4 = (bf16[64,1024]{1,0:T(8,128)(2,1)S(1)}, bf16[64,1024]{1,0:T(8,128)(2,1)}, u32[]{:S(2)}) copy-start(bf16[64,1024]{1,0:T(8,128)(2,1)} %upr_ref.1) | copy-start | bytes 393220
  110.2 4.3 %copy-start.9 = (s32[1,1,512]{2,1,0:T(1,128)S(1)}, s32[1,1,512]{2,1,0:T(1,128)}, u32[]{:S(2)}) copy-start(s32[1,1,512]{2,1,0:T(1,128)} %param.19) | copy-start | bytes 6148
  110.2 4.4 %copy-start.11 = (s32[1,1,512]{2,1,0:T(1,128)S(1)}, s32[1,1,512]{2,1,0:T(1,128)}, u32[]{:S(2)}) copy-start(s32[1,1,512]{2,1,0:T(1,128)} %param.24) | copy-start | bytes 6148
  114.5 1.0 copy-start.2
  115.6 17.3 %copy-start.5 = (bf16[256,256]{1,0:T(8,128)(2,1)S(1)}, bf16[256,256]{1,0:T(8,128)(2,1)}, u32[]{:S(2)}) copy-start(bf16[256,256]{1,0:T(8,128)(2,1)} %w_ref.1) | copy-start | bytes 393220
  115.6 17.3 %copy-start.10 = (bf16[1,16,256]{2,1,0:T(8,128)(2,1)S(1)}, bf16[1,16,256]{2,1,0:T(8,128)(2,1)}, u32[]{:S(2)}) copy-start(bf16[1,16,256]{2,1,0:T(8,128)(2,1)} %param.18) | copy-start | bytes 24580
  115.6 27.1 %copy-start.3 = (bf16[256,1024]{1,0:T(8,128)(2,1)S(1)}, bf16[256,1024]{1,0:T(8,128)(2,1)}, u32[]{:S(2)}) copy-start(bf16[256,1024]{1,0:T(8,128)(2,1)} %back_ref.1) | copy-start | bytes 1572868

commit v6 on v5

--- a/solution.py
+++ b/solution.py
@@ -18,7 +18,7 @@
 NEAR = YH * NT
 XS = 4
 PEER = (0, 2, 1, 3)
-BLOCK = 1024
+BLOCK = 2048
 
 
 def silu(v):
@@ -40,16 +40,25 @@
 
 def down_kernel(x_ref, w_ref, o_ref, x, w, sems):
     load_w = pltpu.make_async_copy(w_ref, w, sems.at[0])
-    load_x = pltpu.make_async_copy(x_ref, x, sems.at[1])
     load_w.start()
-    load_x.start()
+    half = x.shape[0] // 2
+    step = half // 2
+    loads = []
+    for i in range(2):
+        for side in range(2):
+            at = pl.ds(side * half + i * step, step)
+            loads.append(pltpu.make_async_copy(x_ref.at[at], x.at[at], sems.at[1 + len(loads)]))
+            loads[-1].start()
     load_w.wait()
-    load_x.wait()
-    y = silu(dot(x[...], w[...], 1, 1)).astype(BF16)
-    half = y.shape[0] // 2
-    packed = jnp.concatenate([y[:half], y[half:]], axis=1)
-    for i in range(o_ref.shape[0]):
-        o_ref[i] = packed
+    for i in range(2):
+        parts = []
+        for side in range(2):
+            loads[i * 2 + side].wait()
+            rows = x[pl.ds(side * half + i * step, step), :]
+            parts.append(silu(dot(rows, w[...], 1, 1)).astype(BF16))
+        packed = jnp.concatenate(parts, axis=1)
+        for k in range(o_ref.shape[0]):
+            o_ref[k, pl.ds(i * step, step), :] = packed
 
 
 def pack_kernel(after_ref, a_ref, b_ref, ab_ref):
@@ -257,7 +266,7 @@
         scratch_shapes=[
             pltpu.VMEM((edges, wide), BF16),
             pltpu.VMEM((width, wide), BF16),
-            pltpu.SemaphoreType.DMA((2,)),
+            pltpu.SemaphoreType.DMA((5,)),
         ],
         compiler_params=params(60),
     )(rows, down_proj.T)

time: 145 us -> 146 us (level)
  no operation moved by 1% of the time
where the time goes in v6:
time: 146 us
  starting transfers between devices  74.1 us (51%)
  waiting for transfers between devices  21.9 us (15%)
  Pallas kernels  21.1 us (14%)
  blocking collectives  19.9 us (14%)
  local copies, waits for them, and re-layouts  6.65 us (5%)
  between operations  1.62 us (1%)
    ppermute x6, starting transfers between devices, local(): lax.ppermute(part, 'src', p)  23 us
    all_to_all x1, starting transfers between devices, local(): lax.all_to_all(far, 'src', split_axis=0, concat_axis=0, tiled=True, axis_...  15.8 us
    ppermute x3, starting transfers between devices, local(): x_w = [own_w] + [lax.ppermute(own_w, 'tgt', along_x(d)) for d in (-1, 2, 1)]  11.9 us
    all_to_all x1, blocking collectives, local(): lax.all_to_all(part.reshape(NT, atoms // NT, da), 'tgt', split_axis=0, co...  10.9 us
    all_to_all x1, blocking collectives, local(): lax.all_to_all(spread, 'tgt', split_axis=0, concat_axis=0, tiled=True)  9.06 us
    pallas_call x1, Pallas kernels, local(): pl.pallas_call(contract_kernel, out_shape=(struct((edges, width)), struct...  7.62 us
    ppermute x6, waiting for transfers between devices, local(): lax.ppermute(part, 'src', p)  7.56 us
    all_to_all x1, waiting for transfers between devices, local(): lax.all_to_all(send, ('src', 'tgt'), split_axis=0, concat_axis=0, tiled=T...  7.25 us
  transfers between devices with their start and end apart: 16, of which 6 were waited for; matrix products, arithmetic and copies ran while one was open for 0% of the time, Pallas kernels for 6%

profile of v6, /device:TPU:1, one launch (start us, length us, event | category | flops | bytes accessed | tf_op | source)
XLA Modules:
  0.0 145.5 jit_solution(7656518970786165152)
XLA Ops:
  0.6 0.0 copy-start.8
  0.6 3.0 %shard_map.176.after_ref = bf16[4,256,128]{2,1,0:T(8,128)(2,1)} custom-call(bf16[512,1024]{1,0:T(8,128)(2,1)} %bitcast.20, bf16[64,1024]{1,0:T(8,128)(2,1)} %bitcast.38), custom_call_target="tpu_custom_call" | custom-call | tf_op jit(solution)/shard_map/pallas_call | solution.py:261
  3.7 0.0 copy-start.12
  3.7 0.0 copy-start.13
  3.7 0.0 copy-start.15
  3.7 15.8 %all-to-all-start = ((bf16[4,256,128]{2,1,0:T(8,128)(2,1)}), bf16[4,256,128]{2,1,0:T(8,128)(2,1)S(1)}, u32[]{:S(2)}, u32[]{:S(2)}) async-start(bf16[4,256,128]{2,1,0:T(8,128)(2,1)} %shard_map.176.after_ref), calls=%async_computation | async-start | bytes 524288 | tf_op jit(solution)/shard_map/all_to_all | solution.py:275
  19.5 1.0 copy-done
  20.5 0.9 copy-done.6
  21.4 0.9 copy-done.7
  22.3 3.1 %collective-permute-start.9 = (bf16[2,64,1024]{2,1,0:T(8,128)(2,1)S(1)}, bf16[2,64,1024]{2,1,0:T(8,128)(2,1)S(1)}, u32[]{:S(2)}, u32[]{:S(2)}) collective-permute-start(bf16[2,64,1024]{2,1,0:T(8,128)(2,1)S(1)} %shard_map.180), channel_id=1, source_target_pairs={{0,4},{1,5},{2,6},{3,7},{4,8},{5,9},{6,10},{7,11},{8,12},{9,13},{1... | collective-permute-start | bytes 786440 | tf_op jit(solution)/shard_map/ppermute | solution.py:286
  25.4 4.4 %collective-permute-start.8 = (bf16[2,64,1024]{2,1,0:T(8,128)(2,1)S(1)}, bf16[2,64,1024]{2,1,0:T(8,128)(2,1)S(1)}, u32[]{:S(2)}, u32[]{:S(2)}) collective-permute-start(bf16[2,64,1024]{2,1,0:T(8,128)(2,1)S(1)} %shard_map.180), channel_id=1, source_target_pairs={{0,8},{1,9},{2,10},{3,11},{4,12},{5,13},{6,14},{7,15},{8,0},{9,1},... | collective-permute-start | bytes 786440 | tf_op jit(solution)/shard_map/ppermute | solution.py:286
  29.8 3.5 %all-to-all-done.b0 = bf16[4,256,128]{2,1,0:T(8,128)(2,1)S(1)} async-done(((bf16[4,256,128]{2,1,0:T(8,128)(2,1)}), bf16[4,256,128]{2,1,0:T(8,128)(2,1)S(1)}, u32[]{:S(2)}, u32[]{:S(2)}) %all-to-all-start) | async-done | bytes 262176 | tf_op jit(solution)/shard_map/all_to_all | solution.py:275
  33.3 4.8 %collective-permute-start.3 = (bf16[4,256,128]{2,1,0:T(8,128)(2,1)S(1)}, bf16[4,256,128]{2,1,0:T(8,128)(2,1)S(1)}, u32[]{:S(2)}, u32[]{:S(2)}) collective-permute-start(bf16[4,256,128]{2,1,0:T(8,128)(2,1)S(1)} %all-to-all-done.b0), channel_id=1, source_target_pairs={{0,16},{16,0},{32,48},{48,32},{64,80},{80,64},{96,112},{112,96},{1... | collective-permute-start | bytes 786440 | tf_op jit(solution)/shard_map/ppermute | solution.py:278
  38.1 4.4 %collective-permute-start.7 = (bf16[2,64,1024]{2,1,0:T(8,128)(2,1)S(1)}, bf16[2,64,1024]{2,1,0:T(8,128)(2,1)S(1)}, u32[]{:S(2)}, u32[]{:S(2)}) collective-permute-start(bf16[2,64,1024]{2,1,0:T(8,128)(2,1)S(1)} %shard_map.180), channel_id=1, source_target_pairs={{0,12},{1,13},{2,14},{3,15},{4,0},{5,1},{6,2},{7,3},{8,4},{9,5},{1... | collective-permute-start | bytes 786440 | tf_op jit(solution)/shard_map/ppermute | solution.py:286
  42.5 8.4 %collective-permute-start.2 = (bf16[4,256,128]{2,1,0:T(8,128)(2,1)S(1)}, bf16[4,256,128]{2,1,0:T(8,128)(2,1)S(1)}, u32[]{:S(2)}, u32[]{:S(2)}) collective-permute-start(bf16[4,256,128]{2,1,0:T(8,128)(2,1)S(1)} %all-to-all-done.b0), channel_id=1, source_target_pairs={{0,32},{16,48},{32,64},{48,80},{64,96},{80,112},{96,128},{112,144}... | collective-permute-start | bytes 786440 | tf_op jit(solution)/shard_map/ppermute | solution.py:289
  50.9 0.0 collective-permute-done.9
  51.0 2.3 %collective-permute-start.1 = (bf16[4,256,128]{2,1,0:T(8,128)(2,1)S(1)}, bf16[4,256,128]{2,1,0:T(8,128)(2,1)S(1)}, u32[]{:S(2)}, u32[]{:S(2)}) collective-permute-start(bf16[4,256,128]{2,1,0:T(8,128)(2,1)S(1)} %all-to-all-done.b0), channel_id=1, source_target_pairs={{0,64},{16,80},{32,480},{48,496},{64,128},{80,144},{96,32},{112,48... | collective-permute-start | bytes 786440 | tf_op jit(solution)/shard_map/ppermute | solution.py:289
  53.3 0.0 collective-permute-done.8
  53.3 3.8 %collective-permute-start = (bf16[4,256,128]{2,1,0:T(8,128)(2,1)S(1)}, bf16[4,256,128]{2,1,0:T(8,128)(2,1)S(1)}, u32[]{:S(2)}, u32[]{:S(2)}) collective-permute-start(bf16[4,256,128]{2,1,0:T(8,128)(2,1)S(1)} %all-to-all-done.b0), channel_id=1, source_target_pairs={{0,480},{16,496},{32,0},{48,16},{64,32},{80,48},{96,64},{112,80},{... | collective-permute-start | bytes 786440 | tf_op jit(solution)/shard_map/ppermute | solution.py:289
  57.1 0.0 collective-permute-done.3.c0
  57.1 1.9 %collective-permute-start.6 = (bf16[4,256,128]{2,1,0:T(8,128)(2,1)S(1)}, bf16[4,256,128]{2,1,0:T(8,128)(2,1)S(1)}, u32[]{:S(2)}, u32[]{:S(2)}) collective-permute-start(bf16[4,256,128]{2,1,0:T(8,128)(2,1)S(1)} %collective-permute-done.3.c0), channel_id=1, source_target_pairs={{0,32},{16,48},{32,64},{48,80},{64,96},{80,112},{96,128},{112,144}... | collective-permute-start | bytes 786440 | tf_op jit(solution)/shard_map/ppermute | solution.py:289
  59.0 0.0 collective-permute-done.7
  59.1 3.8 %collective-permute-start.5 = (bf16[4,256,128]{2,1,0:T(8,128)(2,1)S(1)}, bf16[4,256,128]{2,1,0:T(8,128)(2,1)S(1)}, u32[]{:S(2)}, u32[]{:S(2)}) collective-permute-start(bf16[4,256,128]{2,1,0:T(8,128)(2,1)S(1)} %collective-permute-done.3.c0), channel_id=1, source_target_pairs={{0,64},{16,80},{32,480},{48,496},{64,128},{80,144},{96,32},{112,48... | collective-permute-start | bytes 786440 | tf_op jit(solution)/shard_map/ppermute | solution.py:289
  62.9 0.0 collective-permute-done.2.b3
  62.9 2.8 %collective-permute-start.4 = (bf16[4,256,128]{2,1,0:T(8,128)(2,1)S(1)}, bf16[4,256,128]{2,1,0:T(8,128)(2,1)S(1)}, u32[]{:S(2)}, u32[]{:S(2)}) collective-permute-start(bf16[4,256,128]{2,1,0:T(8,128)(2,1)S(1)} %collective-permute-done.3.c0), channel_id=1, source_target_pairs={{0,480},{16,496},{32,0},{48,16},{64,32},{80,48},{96,64},{112,80},{... | collective-permute-start | bytes 786440 | tf_op jit(solution)/shard_map/ppermute | solution.py:289
  65.6 0.0 copy-done.8
  65.6 0.1 and_add_fusion.pos_ref
  66.4 0.1 pad_maximum_fusion.wa_ref
  66.5 0.0 collective-permute-done.1.b2
  66.5 2.3 %collective-permute-start.10 = (bf16[4,2,64,1024]{3,2,1,0:T(8,128)(2,1)S(1)}, bf16[4,2,64,1024]{3,2,1,0:T(8,128)(2,1)}, u32[]{:S(2)}, u32[]{:S(2)}) collective-permute-start(bf16[4,2,64,1024]{3,2,1,0:T(8,128)(2,1)S(1)} %pad_maximum_fusion.wa_ref), channel_id=1, source_target_pairs={{0,2},{1,3},{2,0},{3,1},{4,6},{5,7},{6,4},{7,5},{8,10},{9,11},{10,... | collective-permute-start | bytes 3145736 | tf_op jit(solution)/shard_map/ppermute | solution.py:291
  68.8 0.0 collective-permute-done.b1
  68.8 1.1 collective-permute-done.6.c3
  69.9 3.5 %collective-permute-done.5.c2 = bf16[4,256,128]{2,1,0:T(8,128)(2,1)S(1)} collective-permute-done((bf16[4,256,128]{2,1,0:T(8,128)(2,1)S(1)}, bf16[4,256,128]{2,1,0:T(8,128)(2,1)S(1)}, u32[]{:S(2)}, u32[]{:S(2)}) %collective-permute-start.5) | collective-permute-done | bytes 262176 | tf_op jit(solution)/shard_map/ppermute | solution.py:289
  73.4 3.0 %collective-permute-done.4.c1 = bf16[4,256,128]{2,1,0:T(8,128)(2,1)S(1)} collective-permute-done((bf16[4,256,128]{2,1,0:T(8,128)(2,1)S(1)}, bf16[4,256,128]{2,1,0:T(8,128)(2,1)S(1)}, u32[]{:S(2)}, u32[]{:S(2)}) %collective-permute-start.4) | collective-permute-done | bytes 262176 | tf_op jit(solution)/shard_map/ppermute | solution.py:289
  76.4 0.0 copy-done.12
  76.4 0.0 copy-done.13
  76.4 0.0 copy-done.15
  76.4 7.6 %shard_map.177 = (bf16[512,64]{1,0:T(8,128)(2,1)S(1)}, bf16[32,8,128]{2,1,0:T(8,128)(2,1)}) custom-call(s32[1,4096]{1,0:T(1,128)S(1)} %and_add_fusion.pos_ref, s32[1,1]{1,0:T(1,128)S(6)} %copy.19.cnt_ref, s32[1,4096]{1,0:T(1,128)S(1)} %bitcast.26, s32[1,4096]{1,0:T(1,128)S(1)} %bitcast.33, bf16[16,4096]{1,0:T(8,128)(2,1)S(1)} %bitcast.31, ...), custom_call_target="tpu_custom_call" | custom-call | flops 99999997952 | bytes 10000000 | tf_op jit(solution)/shard_map/pallas_call | solution.py:300
  84.0 0.7 copy-done.16
  84.7 5.1 %all-to-all-start.1 = ((bf16[32,8,128]{2,1,0:T(8,128)(2,1)}), bf16[32,8,128]{2,1,0:T(8,128)(2,1)S(1)}, u32[]{:S(2)}, u32[]{:S(2)}) async-start(bf16[32,8,128]{2,1,0:T(8,128)(2,1)} %get-tuple-element.12), calls=%async_computation.1 | async-start | bytes 131072 | tf_op jit(solution)/shard_map/all_to_all | solution.py:326
  89.8 7.2 %all-to-all-done.1.x_ref = bf16[32,8,128]{2,1,0:T(8,128)(2,1)S(1)} async-done(((bf16[32,8,128]{2,1,0:T(8,128)(2,1)}), bf16[32,8,128]{2,1,0:T(8,128)(2,1)S(1)}, u32[]{:S(2)}, u32[]{:S(2)}) %all-to-all-start.1) | async-done | bytes 65568 | tf_op jit(solution)/shard_map/all_to_all | solution.py:326
  97.1 0.7 shard_map.179
  97.8 0.0 collective-permute-done.10.wb_ref
  97.8 6.1 %all-to-all-start.2 = ((bf16[16,16,128]{2,1,0:T(8,128)(2,1)}), bf16[16,16,128]{2,1,0:T(8,128)(2,1)S(1)}, u32[]{:S(2)}, u32[]{:S(2)}) async-start(bf16[16,16,128]{2,1,0:T(8,128)(2,1)} %shard_map.179), calls=%async_computation.2 | async-start | bytes 131072 | tf_op jit(solution)/shard_map/all_to_all | solution.py:340
  103.9 3.0 %collective-permute-start.11 = (bf16[4,2,64,1024]{3,2,1,0:T(8,128)(2,1)S(1)}, bf16[4,2,64,1024]{3,2,1,0:T(8,128)(2,1)}, u32[]{:S(2)}, u32[]{:S(2)}) collective-permute-start(bf16[4,2,64,1024]{3,2,1,0:T(8,128)(2,1)S(1)} %pad_maximum_fusion.wa_ref), channel_id=1, source_target_pairs={{0,1},{1,0},{2,3},{3,2},{4,5},{5,4},{6,7},{7,6},{8,9},{9,8},{10,11... | collective-permute-start | bytes 3145736 | tf_op jit(solution)/shard_map/ppermute | solution.py:338
  106.9 2.1 %collective-permute-start.12 = (bf16[4,2,64,1024]{3,2,1,0:T(8,128)(2,1)}, bf16[4,2,64,1024]{3,2,1,0:T(8,128)(2,1)}, u32[]{:S(2)}, u32[]{:S(2)}) collective-permute-start(bf16[4,2,64,1024]{3,2,1,0:T(8,128)(2,1)} %collective-permute-done.10.wb_ref), channel_id=1, source_target_pairs={{0,1},{1,0},{2,3},{3,2},{4,5},{5,4},{6,7},{7,6},{8,9},{9,8},{10,11... | collective-permute-start | bytes 3145736 | tf_op jit(solution)/shard_map/ppermute | solution.py:339
  109.0 0.0 copy-done.14
  109.0 0.0 copy-start.1
  109.0 1.2 copy-done.1
  110.2 0.9 copy-done.17
  111.1 0.8 shard_map.178.x_ref
  111.9 3.6 %all-to-all-done.2 = bf16[16,16,128]{2,1,0:T(8,128)(2,1)S(1)} async-done(((bf16[16,16,128]{2,1,0:T(8,128)(2,1)}), bf16[16,16,128]{2,1,0:T(8,128)(2,1)S(1)}, u32[]{:S(2)}, u32[]{:S(2)}) %all-to-all-start.2) | async-done | bytes 65568 | tf_op jit(solution)/shard_map/all_to_all | solution.py:340
  115.5 0.0 collective-permute-done.11.wc_ref
  115.5 0.0 collective-permute-done.12.wd_ref
  115.5 0.0 copy-done.4
  115.5 0.0 copy-done.9
  115.5 0.0 copy-start.2
  115.5 1.0 copy-done.2
  116.6 6.4 %shard_map.181 = (bf16[512,1024]{1,0:T(8,128)(2,1)S(1)}, bf16[256,256]{1,0:T(8,128)(2,1)S(1)}) custom-call(s32[1,1]{1,0:T(1,128)} %bitcast.me_ref, f32[512,1024]{1,0:T(8,128)S(1)} %shard_map.178.x_ref, bf16[256,128]{1,0:T(8,128)(2,1)S(1)} %bitcast.24, s32[1,512]{1,0:T(1,128)S(1)} %bitcast.30, s32[1,512]{1,0:T(1,128)S(1)} %bitcast.27, ...), custom_call_target="tpu_custom_call" | custom-call | tf_op jit(solution)/shard_map/pallas_call | solution.py:354
  122.9 10.9 %all_to_all.25.parts_ref = bf16[16,16,256]{2,1,0:T(8,128)(2,1)S(1)} all-to-all(bf16[16,16,256]{2,1,0:T(8,128)(2,1)S(1)} %bitcast.25), channel_id=1, replica_groups=mesh['src'=32,'tgt'=16] {'tgt'}, dimensions={0} | all-to-all | bytes 262144 | tf_op jit(solution)/shard_map/all_to_all | solution.py:379
  133.8 0.0 copy-done.5
  133.8 0.8 shard_map.182
  134.6 9.1 %all_to_all.26 = bf16[16,16,256]{2,1,0:T(8,128)(2,1)S(1)} all-to-all(bf16[16,16,256]{2,1,0:T(8,128)(2,1)S(1)} %get-tuple-element.18), channel_id=1, replica_groups=mesh['src'=32,'tgt'=16] {'tgt'}, dimensions={0} | all-to-all | bytes 262144 | tf_op jit(solution)/shard_map/all_to_all | solution.py:389
  143.7 1.9 %shard_map.183 = bf16[512,1024]{1,0:T(8,128)(2,1)} custom-call(bf16[512,1024]{1,0:T(8,128)(2,1)S(1)} %get-tuple-element.16.skip_ref, bf16[256,256]{1,0:T(8,128)(2,1)S(1)} %bitcast.23, s32[1,512]{1,0:T(1,128)S(1)} %bitcast.28, bf16[256,1024]{1,0:T(8,128)(2,1)S(1)} %copy-done.3), custom_call_target="tpu_custom_call" | custom-call | tf_op jit(solution)/shard_map/pallas_call | solution.py:390
  (16 shorter events, 0.0 us)
Async XLA Ops:
  0.6 65.0 %copy-start.8 = (s32[1,1,4096]{2,1,0:T(1,128)S(1)}, s32[1,1,4096]{2,1,0:T(1,128)}, u32[]{:S(2)}) copy-start(s32[1,1,4096]{2,1,0:T(1,128)} %param.20) | copy-start | bytes 49156
  3.7 72.7 %copy-start.12 = (bf16[1,1,16,4096]{3,2,1,0:T(8,128)(2,1)S(1)}, bf16[1,1,16,4096]{3,2,1,0:T(8,128)(2,1)}, u32[]{:S(2)}) copy-start(bf16[1,1,16,4096]{3,2,1,0:T(8,128)(2,1)} %param.23) | copy-start | bytes 393220
  3.7 72.7 %copy-start.13 = (bf16[1024,64]{0,1:T(8,128)(2,1)S(1)}, bf16[1024,64]{0,1:T(8,128)(2,1)}, u32[]{:S(2)}) copy-start(bf16[1024,64]{0,1:T(8,128)(2,1)} %param.26) | copy-start | bytes 393220
  3.7 72.7 %copy-start.15 = (s32[1,1,4096]{2,1,0:T(1,128)S(1)}, s32[1,1,4096]{2,1,0:T(1,128)}, u32[]{:S(2)}) copy-start(s32[1,1,4096]{2,1,0:T(1,128)} %param.21) | copy-start | bytes 49156
  3.7 29.6 %all-to-all-start = ((bf16[4,256,128]{2,1,0:T(8,128)(2,1)}), bf16[4,256,128]{2,1,0:T(8,128)(2,1)S(1)}, u32[]{:S(2)}, u32[]{:S(2)}) async-start(bf16[4,256,128]{2,1,0:T(8,128)(2,1)} %shard_map.176.after_ref), calls=%async_computation | async-start | bytes 524288 | tf_op jit(solution)/shard_map/all_to_all | solution.py:275
  19.5 1.0 copy-start
  20.5 0.9 copy-start.6
  21.4 0.9 copy-start.7
  22.3 28.6 %collective-permute-start.9 = (bf16[2,64,1024]{2,1,0:T(8,128)(2,1)S(1)}, bf16[2,64,1024]{2,1,0:T(8,128)(2,1)S(1)}, u32[]{:S(2)}, u32[]{:S(2)}) collective-permute-start(bf16[2,64,1024]{2,1,0:T(8,128)(2,1)S(1)} %shard_map.180), channel_id=1, source_target_pairs={{0,4},{1,5},{2,6},{3,7},{4,8},{5,9},{6,10},{7,11},{8,12},{9,13},{1... | collective-permute-start | bytes 786440 | tf_op jit(solution)/shard_map/ppermute | solution.py:286
  25.4 27.9 %collective-permute-start.8 = (bf16[2,64,1024]{2,1,0:T(8,128)(2,1)S(1)}, bf16[2,64,1024]{2,1,0:T(8,128)(2,1)S(1)}, u32[]{:S(2)}, u32[]{:S(2)}) collective-permute-start(bf16[2,64,1024]{2,1,0:T(8,128)(2,1)S(1)} %shard_map.180), channel_id=1, source_target_pairs={{0,8},{1,9},{2,10},{3,11},{4,12},{5,13},{6,14},{7,15},{8,0},{9,1},... | collective-permute-start | bytes 786440 | tf_op jit(solution)/shard_map/ppermute | solution.py:286
  33.3 23.8 %collective-permute-start.3 = (bf16[4,256,128]{2,1,0:T(8,128)(2,1)S(1)}, bf16[4,256,128]{2,1,0:T(8,128)(2,1)S(1)}, u32[]{:S(2)}, u32[]{:S(2)}) collective-permute-start(bf16[4,256,128]{2,1,0:T(8,128)(2,1)S(1)} %all-to-all-done.b0), channel_id=1, source_target_pairs={{0,16},{16,0},{32,48},{48,32},{64,80},{80,64},{96,112},{112,96},{1... | collective-permute-start | bytes 786440 | tf_op jit(solution)/shard_map/ppermute | solution.py:278
  38.1 20.9 %collective-permute-start.7 = (bf16[2,64,1024]{2,1,0:T(8,128)(2,1)S(1)}, bf16[2,64,1024]{2,1,0:T(8,128)(2,1)S(1)}, u32[]{:S(2)}, u32[]{:S(2)}) collective-permute-start(bf16[2,64,1024]{2,1,0:T(8,128)(2,1)S(1)} %shard_map.180), channel_id=1, source_target_pairs={{0,12},{1,13},{2,14},{3,15},{4,0},{5,1},{6,2},{7,3},{8,4},{9,5},{1... | collective-permute-start | bytes 786440 | tf_op jit(solution)/shard_map/ppermute | solution.py:286
  42.5 20.4 %collective-permute-start.2 = (bf16[4,256,128]{2,1,0:T(8,128)(2,1)S(1)}, bf16[4,256,128]{2,1,0:T(8,128)(2,1)S(1)}, u32[]{:S(2)}, u32[]{:S(2)}) collective-permute-start(bf16[4,256,128]{2,1,0:T(8,128)(2,1)S(1)} %all-to-all-done.b0), channel_id=1, source_target_pairs={{0,32},{16,48},{32,64},{48,80},{64,96},{80,112},{96,128},{112,144}... | collective-permute-start | bytes 786440 | tf_op jit(solution)/shard_map/ppermute | solution.py:289
  51.0 15.6 %collective-permute-start.1 = (bf16[4,256,128]{2,1,0:T(8,128)(2,1)S(1)}, bf16[4,256,128]{2,1,0:T(8,128)(2,1)S(1)}, u32[]{:S(2)}, u32[]{:S(2)}) collective-permute-start(bf16[4,256,128]{2,1,0:T(8,128)(2,1)S(1)} %all-to-all-done.b0), channel_id=1, source_target_pairs={{0,64},{16,80},{32,480},{48,496},{64,128},{80,144},{96,32},{112,48... | collective-permute-start | bytes 786440 | tf_op jit(solution)/shard_map/ppermute | solution.py:289
  53.3 15.5 %collective-permute-start = (bf16[4,256,128]{2,1,0:T(8,128)(2,1)S(1)}, bf16[4,256,128]{2,1,0:T(8,128)(2,1)S(1)}, u32[]{:S(2)}, u32[]{:S(2)}) collective-permute-start(bf16[4,256,128]{2,1,0:T(8,128)(2,1)S(1)} %all-to-all-done.b0), channel_id=1, source_target_pairs={{0,480},{16,496},{32,0},{48,16},{64,32},{80,48},{96,64},{112,80},{... | collective-permute-start | bytes 786440 | tf_op jit(solution)/shard_map/ppermute | solution.py:289
  57.1 12.8 %collective-permute-start.6 = (bf16[4,256,128]{2,1,0:T(8,128)(2,1)S(1)}, bf16[4,256,128]{2,1,0:T(8,128)(2,1)S(1)}, u32[]{:S(2)}, u32[]{:S(2)}) collective-permute-start(bf16[4,256,128]{2,1,0:T(8,128)(2,1)S(1)} %collective-permute-done.3.c0), channel_id=1, source_target_pairs={{0,32},{16,48},{32,64},{48,80},{64,96},{80,112},{96,128},{112,144}... | collective-permute-start | bytes 786440 | tf_op jit(solution)/shard_map/ppermute | solution.py:289
  59.1 14.3 %collective-permute-start.5 = (bf16[4,256,128]{2,1,0:T(8,128)(2,1)S(1)}, bf16[4,256,128]{2,1,0:T(8,128)(2,1)S(1)}, u32[]{:S(2)}, u32[]{:S(2)}) collective-permute-start(bf16[4,256,128]{2,1,0:T(8,128)(2,1)S(1)} %collective-permute-done.3.c0), channel_id=1, source_target_pairs={{0,64},{16,80},{32,480},{48,496},{64,128},{80,144},{96,32},{112,48... | collective-permute-start | bytes 786440 | tf_op jit(solution)/shard_map/ppermute | solution.py:289
  62.9 13.5 %collective-permute-start.4 = (bf16[4,256,128]{2,1,0:T(8,128)(2,1)S(1)}, bf16[4,256,128]{2,1,0:T(8,128)(2,1)S(1)}, u32[]{:S(2)}, u32[]{:S(2)}) collective-permute-start(bf16[4,256,128]{2,1,0:T(8,128)(2,1)S(1)} %collective-permute-done.3.c0), channel_id=1, source_target_pairs={{0,480},{16,496},{32,0},{48,16},{64,32},{80,48},{96,64},{112,80},{... | collective-permute-start | bytes 786440 | tf_op jit(solution)/shard_map/ppermute | solution.py:289
  66.5 31.3 %collective-permute-start.10 = (bf16[4,2,64,1024]{3,2,1,0:T(8,128)(2,1)S(1)}, bf16[4,2,64,1024]{3,2,1,0:T(8,128)(2,1)}, u32[]{:S(2)}, u32[]{:S(2)}) collective-permute-start(bf16[4,2,64,1024]{3,2,1,0:T(8,128)(2,1)S(1)} %pad_maximum_fusion.wa_ref), channel_id=1, source_target_pairs={{0,2},{1,3},{2,0},{3,1},{4,6},{5,7},{6,4},{7,5},{8,10},{9,11},{10,... | collective-permute-start | bytes 3145736 | tf_op jit(solution)/shard_map/ppermute | solution.py:291
  76.4 32.6 %copy-start.14 = (bf16[64,1024]{1,0:T(8,128)(2,1)S(1)}, bf16[64,1024]{1,0:T(8,128)(2,1)}, u32[]{:S(2)}) copy-start(bf16[64,1024]{1,0:T(8,128)(2,1)} %upf_ref.1) | copy-start | bytes 393220
  84.0 0.7 copy-start.16
  84.7 12.4 %all-to-all-start.1 = ((bf16[32,8,128]{2,1,0:T(8,128)(2,1)}), bf16[32,8,128]{2,1,0:T(8,128)(2,1)S(1)}, u32[]{:S(2)}, u32[]{:S(2)}) async-start(bf16[32,8,128]{2,1,0:T(8,128)(2,1)} %get-tuple-element.12), calls=%async_computation.1 | async-start | bytes 131072 | tf_op jit(solution)/shard_map/all_to_all | solution.py:326
  97.8 17.7 %all-to-all-start.2 = ((bf16[16,16,128]{2,1,0:T(8,128)(2,1)}), bf16[16,16,128]{2,1,0:T(8,128)(2,1)S(1)}, u32[]{:S(2)}, u32[]{:S(2)}) async-start(bf16[16,16,128]{2,1,0:T(8,128)(2,1)} %shard_map.179), calls=%async_computation.2 | async-start | bytes 131072 | tf_op jit(solution)/shard_map/all_to_all | solution.py:340
  103.9 11.6 %collective-permute-start.11 = (bf16[4,2,64,1024]{3,2,1,0:T(8,128)(2,1)S(1)}, bf16[4,2,64,1024]{3,2,1,0:T(8,128)(2,1)}, u32[]{:S(2)}, u32[]{:S(2)}) collective-permute-start(bf16[4,2,64,1024]{3,2,1,0:T(8,128)(2,1)S(1)} %pad_maximum_fusion.wa_ref), channel_id=1, source_target_pairs={{0,1},{1,0},{2,3},{3,2},{4,5},{5,4},{6,7},{7,6},{8,9},{9,8},{10,11... | collective-permute-start | bytes 3145736 | tf_op jit(solution)/shard_map/ppermute | solution.py:338
  106.9 8.6 %collective-permute-start.12 = (bf16[4,2,64,1024]{3,2,1,0:T(8,128)(2,1)}, bf16[4,2,64,1024]{3,2,1,0:T(8,128)(2,1)}, u32[]{:S(2)}, u32[]{:S(2)}) collective-permute-start(bf16[4,2,64,1024]{3,2,1,0:T(8,128)(2,1)} %collective-permute-done.10.wb_ref), channel_id=1, source_target_pairs={{0,1},{1,0},{2,3},{3,2},{4,5},{5,4},{6,7},{7,6},{8,9},{9,8},{10,11... | collective-permute-start | bytes 3145736 | tf_op jit(solution)/shard_map/ppermute | solution.py:339
  109.0 1.2 copy-start.1
  110.2 0.9 copy-start.17
  111.1 4.3 %copy-start.4 = (bf16[64,1024]{1,0:T(8,128)(2,1)S(1)}, bf16[64,1024]{1,0:T(8,128)(2,1)}, u32[]{:S(2)}) copy-start(bf16[64,1024]{1,0:T(8,128)(2,1)} %upr_ref.1) | copy-start | bytes 393220
  111.1 4.3 %copy-start.9 = (s32[1,1,512]{2,1,0:T(1,128)S(1)}, s32[1,1,512]{2,1,0:T(1,128)}, u32[]{:S(2)}) copy-start(s32[1,1,512]{2,1,0:T(1,128)} %param.19) | copy-start | bytes 6148
  111.1 4.4 %copy-start.11 = (s32[1,1,512]{2,1,0:T(1,128)S(1)}, s32[1,1,512]{2,1,0:T(1,128)}, u32[]{:S(2)}) copy-start(s32[1,1,512]{2,1,0:T(1,128)} %param.24) | copy-start | bytes 6148
  115.5 1.0 copy-start.2
  116.5 17.3 %copy-start.5 = (bf16[256,256]{1,0:T(8,128)(2,1)S(1)}, bf16[256,256]{1,0:T(8,128)(2,1)}, u32[]{:S(2)}) copy-start(bf16[256,256]{1,0:T(8,128)(2,1)} %w_ref.1) | copy-start | bytes 393220
  116.6 17.3 %copy-start.10 = (bf16[1,16,256]{2,1,0:T(8,128)(2,1)S(1)}, bf16[1,16,256]{2,1,0:T(8,128)(2,1)}, u32[]{:S(2)}) copy-start(bf16[1,16,256]{2,1,0:T(8,128)(2,1)} %param.18) | copy-start | bytes 24580
  116.6 27.1 %copy-start.3 = (bf16[256,1024]{1,0:T(8,128)(2,1)S(1)}, bf16[256,1024]{1,0:T(8,128)(2,1)}, u32[]{:S(2)}) copy-start(bf16[256,1024]{1,0:T(8,128)(2,1)} %back_ref.1) | copy-start | bytes 1572868
